TPU v7x, 512 devices: a whole 4x4x16 slice. The times are simulated.
512 devices in a mesh: in: 8 (over y, core), out: 8 (over z_hi, x), tok: 8 (over z_lo).
Axes of the slice: x: 4, y: 4, z: 16 (z_hi: 2, z_lo: 8; z = z_hi * 8 + z_lo), core: 2. Of those that a mesh axis runs over, the one named last changes fastest.
Arguments:
- tokens_in: bfloat16 [1024, 8192], P('tok', 'in'), may hold values from -6 to 6
- weight: bfloat16 [8192, 32768], P('in', ('out', 'tok')), may hold values from -0.0625 to 0.0625
- grad_out: bfloat16 [1024, 32768], P('tok', 'out'), may hold values from -6 to 6
Outputs:
- grad_input: bfloat16 [1024, 8192], P('tok', ('in', 'out'))
- grad_weight: bfloat16 [8192, 32768], P('in', ('out', 'tok'))
- act_factor: float32 [8192, 4096], P(('in', 'tok'), 'out')
- grad_factor: float32 [32768, 4096], P(('out', 'tok'), 'in')
All inputs are finite; a program needn't handle non-finite values.
Results may differ from a plain program's by a relative error of at most 0.0049.
Values may be sent and summed in bfloat16 or wider, within the bound.
No kernel may reach another device: no remote copies, remote signals or barrier semaphores. Data moves between devices by JAX's collectives and lax.ppermute only.
A program may use at most 64 MiB of HBM per device.

v0:
```python
import math

import jax
import jax.numpy as jnp
import numpy as np
from jax import lax
from jax.sharding import PartitionSpec as P

BLK = 4096


def swapped(value, axis, stride):
    mask = 2**stride
    pairs = [(source, source ^ mask) for source in range(lax.axis_size(axis))]
    return lax.ppermute(value, axis, pairs)


def gelu_slope(values):
    scale = math.sqrt(2.0 / math.pi)
    cubic = values * values * values
    tanh_val = jnp.tanh(scale * (values + 0.044715 * cubic))
    return 0.5 * (1.0 + tanh_val) + 0.5 * values * (1.0 - tanh_val * tanh_val) * scale * (
        1.0 + 3.0 * 0.044715 * values * values
    )


def on_device(tokens_in, weight, grad_out):
    n_in = lax.axis_size("in")
    n_out = lax.axis_size("out")
    n_tok = lax.axis_size("tok")
    in_index = lax.axis_index("in")
    out_index = lax.axis_index("out")
    tok_index = lax.axis_index("tok")
    tok_count, in_width = tokens_in.shape
    out_width = grad_out.shape[1]
    weight_block, token_block = (
        lax.all_gather(weight, "tok", axis=1, tiled=True),
        lax.all_gather(tokens_in, "tok", axis=0, tiled=True),
    )
    total_tokens = token_block.shape[0]
    partial_sum = jnp.dot(tokens_in, weight_block, preferred_element_type=jnp.float32)
    preact = lax.psum(partial_sum, "in")
    grad_pre = (grad_out.astype(jnp.float32) * gelu_slope(preact)).astype(jnp.bfloat16)
    grad_input = lax.psum_scatter(
        lax.dot_general(
            weight_block, grad_pre, (((1,), (1,)), ((), ())), preferred_element_type=jnp.float32
        ),
        "out",
        scatter_dimension=0,
        tiled=True,
    ).T.astype(jnp.bfloat16)
    sub_width = out_width // n_tok
    factor_cols = BLK // n_in
    own_parts = grad_pre.reshape(tok_count, n_tok, sub_width)
    quarters = grad_pre.reshape(tok_count, out_width // BLK, n_in, factor_cols)
    own_cols = lax.dynamic_index_in_dim(quarters, in_index, axis=2, keepdims=False)
    block_of = np.arange(n_tok) * sub_width // BLK
    cross_cols = own_cols[:, block_of, :]
    grad_rows, grad_cross = (
        lax.all_to_all(own_parts, "tok", split_axis=1, concat_axis=0, tiled=True),
        lax.all_to_all(cross_cols, "tok", split_axis=1, concat_axis=0, tiled=True),
    )
    grad_rows = grad_rows.reshape(total_tokens, sub_width)
    grad_cross = grad_cross.reshape(total_tokens, factor_cols)
    grad_weight = lax.dot_general(
        token_block, grad_rows, (((0,), (0,)), ((), ())), preferred_element_type=jnp.float32
    ).astype(jnp.bfloat16)
    grad_factor = lax.dot_general(
        grad_rows, grad_cross, (((0,), (0,)), ((), ())), preferred_element_type=jnp.float32
    ) / float(total_tokens)
    col_width = BLK // n_out
    per_block = BLK // in_width
    col_start = out_index * col_width % in_width
    act_cols = lax.dynamic_slice_in_dim(token_block, col_start, col_width, 1)
    local_pos = in_index % per_block
    owner_pos = out_index * col_width // in_width
    for bit in range(per_block.bit_length() - 1):
        partner = swapped(act_cols, "in", bit)
        keep_own = local_pos >> bit & 1 == owner_pos >> bit & 1
        act_cols = jnp.where(keep_own, act_cols, partner)
    factor_rows = in_width // n_tok
    rows_tokens = lax.dynamic_slice_in_dim(token_block, tok_index * factor_rows, factor_rows, 1)
    act_factor = lax.dot_general(
        rows_tokens, act_cols, (((0,), (0,)), ((), ())), preferred_element_type=jnp.float32
    ) / float(total_tokens)
    return (grad_input, grad_weight, act_factor, grad_factor)


def solution(mesh):
    return jax.shard_map(
        on_device,
        mesh=mesh,
        in_specs=(P("tok", "in"), P("in", ("out", "tok")), P("tok", "out")),
        out_specs=(
            P("tok", ("in", "out")),
            P("in", ("out", "tok")),
            P(("in", "tok"), "out"),
            P(("out", "tok"), "in"),
        ),
        check_vma=False,
    )
```

profile of v0, /device:TPU:8, one launch (start us, length us, event | category | flops | bytes accessed | tf_op | source)
XLA Modules:
  0.0 565.4 jit_solution(2491996832823272782)
XLA Ops:
  7.2 0.0 all-gather.3.cloned.1.call-start
  7.2 0.7 all-gather.3.cloned.1.call-update
  7.9 0.0 all-reduce.2.cloned.1.call-start
  7.9 188.5 %all-gather.3.cloned.1.call-done = bf16[1024,4096]{1,0:T(8,128)(2,1)} async-done(((bf16[1024,512]{1,0:T(8,128)(2,1)}), bf16[1024,4096]{1,0:T(8,128)(2,1)}) %all-gather.3.cloned.1.call-update) | async-done | bytes 8388624 | tf_op jit(solution)/shard_map/all_gather | solution.py:37
  196.5 6.1 %fusion.17 = f32[128,4096]{1,0:T(8,128)} fusion(bf16[128,1024]{1,0:T(8,128)(2,1)} %param.5, bf16[1024,4096]{1,0:T(8,128)(2,1)} %all-gather.3.cloned.1.call-done), kind=kOutput, calls=%fused_computation.28 | convolution fusion | flops 1073741824 | bytes 10747904 | tf_op jit(solution)/shard_map/dot_general | solution.py:41
  202.5 0.0 copy-start.3
  202.5 0.0 all-reduce.2.cloned.1.call-update
  202.6 74.6 %all-reduce.2.cloned.1.call-done = f32[128,4096]{1,0:T(8,128)} async-done(((f32[128,4096]{1,0:T(8,128)}), f32[128,4096]{1,0:T(8,128)}) %all-reduce.2.cloned.1.call-update) | async-done | bytes 2097168 | tf_op jit(solution)/shard_map/psum | solution.py:42
  277.2 0.0 copy-done.3
  277.2 3.0 fusion.8
  280.2 1.3 copy.15
  281.5 10.0 %all-to-all-start = ((bf16[128,8,512]{0,2,1:T(8,128)(2,1)}), bf16[128,8,512]{0,2,1:T(8,128)(2,1)S(1)}, u32[]{:S(2)}, u32[]{:S(2)}) async-start(bf16[128,8,512]{0,2,1:T(8,128)(2,1)} %bitcast.2), calls=%async_computation.1 | async-start | bytes 2097152 | tf_op jit(solution)/shard_map/all_to_all | solution.py:60
  291.4 0.0 all-gather.5.cloned.1.call-start
  291.5 0.7 all-gather.5.cloned.1.call-update
  292.2 0.4 copy.17
  292.6 0.3 constant_dynamic-slice_fusion.1
  292.9 69.4 %all-to-all-done = bf16[128,8,512]{0,2,1:T(8,128)(2,1)S(1)} async-done(((bf16[128,8,512]{0,2,1:T(8,128)(2,1)}), bf16[128,8,512]{0,2,1:T(8,128)(2,1)S(1)}, u32[]{:S(2)}, u32[]{:S(2)}) %all-to-all-start) | async-done | bytes 1048608 | tf_op jit(solution)/shard_map/all_to_all | solution.py:60
  362.3 0.0 copy-start.1
  362.3 1.2 broadcast.25
  363.5 7.3 %all-to-all-start.1 = ((bf16[128,8,512]{2,0,1:T(8,128)(2,1)}), bf16[128,8,512]{2,0,1:T(8,128)(2,1)}, u32[]{:S(2)}, u32[]{:S(2)}) async-start(bf16[128,8,512]{2,0,1:T(8,128)(2,1)} %broadcast.25), calls=%async_computation.2 | async-start | bytes 2097152 | tf_op jit(solution)/shard_map/all_to_all | solution.py:61
  370.8 0.0 reduce-scatter.2.cloned.1.call-start
  370.8 0.0 copy-done.1
  370.8 13.6 %all-gather.5.cloned.1.call-done = bf16[1024,1024]{1,0:T(8,128)(2,1)} async-done(((bf16[128,1024]{1,0:T(8,128)(2,1)}), bf16[1024,1024]{1,0:T(8,128)(2,1)}) %all-gather.5.cloned.1.call-update) | async-done | bytes 2097168 | tf_op jit(solution)/shard_map/all_gather | solution.py:38
  384.4 0.0 copy-start
  384.4 2.4 constant_dynamic-slice_fusion
  386.8 1.9 collective-permute-start
  388.8 2.9 collective-permute-done
  391.7 0.0 copy-done
  391.7 1.4 broadcast_select_fusion
  393.1 2.5 collective-permute-start.1
  395.6 7.1 %convolution_bitcast_fusion.1 = f32[1024,128]{0,1:T(8,128)} fusion(bf16[128,4096]{1,0:T(8,128)(2,1)S(1)} %fusion.8, bf16[1024,4096]{1,0:T(8,128)(2,1)} %all-gather.3.cloned.1.call-done), kind=kOutput, calls=%fused_computation.15 | convolution fusion | flops 1073741824 | bytes 9961472 | tf_op jit(solution)/shard_map/dot_general | solution.py:45
  402.6 0.0 copy-start.2
  402.6 0.0 reduce-scatter.2.cloned.1.call-update
  402.7 18.4 %collective-permute-done.1 = bf16[1024,512]{1,0:T(8,128)(2,1)} collective-permute-done((bf16[1024,512]{1,0:T(8,128)(2,1)}, bf16[1024,512]{1,0:T(8,128)(2,1)}, u32[]{:S(2)}, u32[]{:S(2)}) %collective-permute-start.1) | collective-permute-done | bytes 1048608 | tf_op jit(solution)/shard_map/ppermute | solution.py:15
  421.0 2.3 convolution_multiply_fusion
  423.3 124.1 %reduce-scatter.2.cloned.1.call-done = f32[128,128]{0,1:T(8,128)} async-done(((f32[1024,128]{0,1:T(8,128)}), f32[128,128]{0,1:T(8,128)}) %reduce-scatter.2.cloned.1.call-update) | async-done | bytes 65552 | tf_op jit(solution)/shard_map/reduce_scatter | solution.py:44
  547.5 1.5 convert_bitcast_fusion
  548.9 0.0 copy-done.2
  548.9 1.3 copy.12
  550.2 3.5 fusion.9
  553.7 2.3 copy.14
  556.0 0.0 all-to-all-done.1
  556.0 2.9 fusion.10
  (1 shorter events, 0.0 us)
Async XLA Ops:
  7.2 189.3 %all-gather.3.cloned.1.call-start = ((), (), s32[]{:S(2)}) async-start(), calls=%async_computation.3 | async-start | bytes 9437184 | tf_op jit(solution)/shard_map/all_gather | solution.py:37
  7.9 269.3 %all-reduce.2.cloned.1.call-start = ((), (), s32[]{:S(2)}) async-start(), calls=%async_computation.4 | async-start | bytes 4194304 | tf_op jit(solution)/shard_map/psum | solution.py:42
  202.5 74.6 %copy-start.3 = (bf16[128,4096]{1,0:T(8,128)(2,1)S(1)}, bf16[128,4096]{1,0:T(8,128)(2,1)}, u32[]{:S(2)}) copy-start(bf16[128,4096]{1,0:T(8,128)(2,1)} %param.7) | copy-start | bytes 3145732
  281.5 80.9 %all-to-all-start = ((bf16[128,8,512]{0,2,1:T(8,128)(2,1)}), bf16[128,8,512]{0,2,1:T(8,128)(2,1)S(1)}, u32[]{:S(2)}, u32[]{:S(2)}) async-start(bf16[128,8,512]{0,2,1:T(8,128)(2,1)} %bitcast.2), calls=%async_computation.1 | async-start | bytes 2097152 | tf_op jit(solution)/shard_map/all_to_all | solution.py:60
  291.4 93.0 %all-gather.5.cloned.1.call-start = ((), (), s32[]{:S(2)}) async-start(), calls=%async_computation.6 | async-start | bytes 2359296 | tf_op jit(solution)/shard_map/all_gather | solution.py:38
  362.3 8.5 %copy-start.1 = (bf16[128,8,512]{0,2,1:T(8,128)(2,1)}, bf16[128,8,512]{0,2,1:T(8,128)(2,1)S(1)}, u32[]{:S(2)}) copy-start(bf16[128,8,512]{0,2,1:T(8,128)(2,1)S(1)} %all-to-all-done) | copy-start | bytes 3145732
  363.5 192.5 %all-to-all-start.1 = ((bf16[128,8,512]{2,0,1:T(8,128)(2,1)}), bf16[128,8,512]{2,0,1:T(8,128)(2,1)}, u32[]{:S(2)}, u32[]{:S(2)}) async-start(bf16[128,8,512]{2,0,1:T(8,128)(2,1)} %broadcast.25), calls=%async_computation.2 | async-start | bytes 2097152 | tf_op jit(solution)/shard_map/all_to_all | solution.py:61
  370.8 176.7 %reduce-scatter.2.cloned.1.call-start = ((), (), s32[]{:S(2)}) async-start(), calls=%async_computation.5 | async-start | bytes 589824 | tf_op jit(solution)/shard_map/reduce_scatter | solution.py:44
  384.4 7.3 %copy-start = (bf16[1024,1024]{1,0:T(8,128)(2,1)S(1)}, bf16[1024,1024]{1,0:T(8,128)(2,1)}, u32[]{:S(2)}) copy-start(bf16[1024,1024]{1,0:T(8,128)(2,1)} %all-gather.5.cloned.1.call-done) | copy-start | bytes 6291460
  386.8 4.9 collective-permute-start
  393.1 27.9 %collective-permute-start.1 = (bf16[1024,512]{1,0:T(8,128)(2,1)}, bf16[1024,512]{1,0:T(8,128)(2,1)}, u32[]{:S(2)}, u32[]{:S(2)}) collective-permute-start(bf16[1024,512]{1,0:T(8,128)(2,1)} %broadcast_select_fusion), channel_id=1, source_target_pairs={{0,128},{64,192},{128,0},{192,64},{256,384},{320,448},{384,256},{4... | collective-permute-start | bytes 3145736 | tf_op jit(solution)/shard_map/ppermute | solution.py:15
  402.6 146.3 %copy-start.2 = (bf16[128,8,512]{0,2,1:T(8,128)(2,1)S(1)}, bf16[128,8,512]{0,2,1:T(8,128)(2,1)}, u32[]{:S(2)}) copy-start(bf16[128,8,512]{0,2,1:T(8,128)(2,1)} %copy-done.1) | copy-start | bytes 3145732
Sparse Core Ops, SparseCore 0:
  10.1 186.3 all-gather.2
  202.7 74.4 all-reduce.1
  294.4 90.0 all-gather.4
  402.8 144.6 reduce-scatter.1
where the time goes:
time: 566 us; the launch traced here: 565 us
  waiting for transfers between devices  493 us (87%)
  starting transfers between devices  21.8 us (4%)
  matrix products  21.8 us (4%)
  between operations  13.9 us (2%)
  local copies, waits for them, and re-layouts  9.17 us (2%)
  other arithmetic  5.79 us (1%)
    all_gather x1, waiting for transfers between devices, on_device(): lax.all_gather(weight, 'tok', axis=1, tiled=True)  189 us
    reduce_scatter x1, waiting for transfers between devices, on_device(): lax.psum_scatter(lax.dot_general(weight_block, grad_pre, (((1,), (1,)), (...  124 us
    psum x1, waiting for transfers between devices, on_device(): preact = lax.psum(partial_sum, 'in')  74.6 us
    all_to_all x1, waiting for transfers between devices, on_device(): lax.all_to_all(own_parts, 'tok', split_axis=1, concat_axis=0, tiled=True)  69.4 us
    ppermute x2, waiting for transfers between devices, swapped(): return lax.ppermute(value, axis, pairs)  21.3 us
    all_gather x1, waiting for transfers between devices, on_device(): lax.all_gather(tokens_in, 'tok', axis=0, tiled=True)  13.6 us
  transfers between devices with their start and end apart: 8, of which 7 were waited for; matrix products, arithmetic and copies ran while one was open for 4% of the time, Pallas kernels for 0%

commit v1 on v0

v1 whole, which is shorter than its diff:
```python
import math

import jax
import jax.numpy as jnp
from jax import lax
from jax.sharding import Mesh, PartitionSpec as P

BF16 = jnp.bfloat16
F16 = jnp.float16
F32 = jnp.float32
IN = ("y", "core")
OUT = ("zh", "x")
TOK = ("th", "tl")


def gelu_slope(values):
    scale = math.sqrt(2.0 / math.pi)
    cubic = values * values * values
    tanh_val = jnp.tanh(scale * (values + 0.044715 * cubic))
    return 0.5 * (1.0 + tanh_val) + 0.5 * values * (1.0 - tanh_val * tanh_val) * scale * (
        1.0 + 3.0 * 0.044715 * values * values
    )


def swap(value, axis):
    return lax.ppermute(value, axis, [(0, 1), (1, 0)])


def exchange(value, axis):
    return lax.all_to_all(value, axis, split_axis=0, concat_axis=0, tiled=True)


def spread(value, axis):
    size = lax.axis_size(axis)
    return exchange(jnp.broadcast_to(value[None], (size,) + value.shape), axis)


def total(parts):
    return jnp.sum(parts.astype(F32), axis=0)


def rows_of(value, start, size):
    return lax.dynamic_slice_in_dim(value, start, size, 0)


def cols_of(value, start, size):
    return lax.dynamic_slice_in_dim(value, start, size, 1)


def tn_dot(left, right):
    return lax.dot_general(left, right, (((0,), (0,)), ((), ())), preferred_element_type=F32)


def on_device(tokens_in, weight, grad_out):
    y, core, zh, x, th, tl = (lax.axis_index(a) for a in ("y", "core", "zh", "x", "th", "tl"))
    tok = th * 4 + tl
    piece = core * 4 + y

    with jax.named_scope("gather_tokens"):
        own = rows_of(tokens_in, x * 32, 32)
        other = swap(own, "th")
        both = jnp.where(th == 0, jnp.stack([own, other]), jnp.stack([other, own]))
        near = spread(both, "tl").reshape(4, 2, 2, 16, 1024).transpose(2, 1, 0, 3, 4)
        tokens = spread(near.reshape(256, 1024), "x").reshape(1024, 1024)

    with jax.named_scope("grad_out_piece"):
        own_rows = rows_of(grad_out, piece * 16, 16).reshape(16, 8, 512).transpose(1, 0, 2)
        grad_out_piece = exchange(own_rows, TOK).reshape(128, 512)

    with jax.named_scope("preact"):
        partial = jnp.dot(tokens, weight, preferred_element_type=F32).astype(F16)
        half = total(exchange(partial.reshape(2, 512, 512), "core")).astype(F16)
        preact = total(exchange(half.reshape(4, 128, 512), "y"))
        grad_piece = (grad_out_piece.astype(F32) * gelu_slope(preact)).astype(BF16)

    with jax.named_scope("gather_grad"):
        grad_half = spread(grad_piece, "y")
        grad_rows = spread(grad_half.reshape(512, 512), "core").reshape(1024, 512)

    with jax.named_scope("grad_input"):
        by_x = weight.reshape(2, 4, 128, 512).transpose(1, 0, 2, 3).reshape(4, 256, 512)
        share = jnp.einsum("rc,kfc->krf", grad_rows, by_x, preferred_element_type=F32).astype(BF16)
        part = total(exchange(share, "x")).astype(BF16)
        part = part.reshape(8, 2, 4, 16, 256).transpose(2, 0, 1, 3, 4)
        part = total(exchange(part, "tl")).astype(BF16)
        part = part.reshape(8, 2, 16, 2, 128).transpose(3, 1, 0, 2, 4).reshape(4, 128, 128)
        grad_input = total(exchange(part, ("zh", "th"))).astype(BF16)

    with jax.named_scope("grad_weight"):
        grad_weight = tn_dot(tokens, grad_rows).astype(BF16)

    with jax.named_scope("grad_factor"):
        pieces = lax.all_gather(grad_piece, TOK, axis=0, tiled=True)
        pieces = pieces.reshape(4, 2, 128, 512).transpose(1, 0, 2, 3).reshape(8, 128, 512)
        cross = exchange(pieces, ("core", "y")).reshape(1024, 512)
        grad_factor = tn_dot(grad_rows, cross) / 1024.0

    with jax.named_scope("act_factor"):
        act_cols = cols_of(tokens, x % 2 * 512, 512)
        act_cols = jnp.where(core == x // 2, act_cols, swap(act_cols, "core"))
        from_y = lax.ppermute(act_cols, "y", [(0, 1), (1, 0), (2, 3), (3, 2)])
        act_cols = jnp.where(y % 2 == zh, act_cols, from_y)
        act_factor = tn_dot(cols_of(tokens, tok * 128, 128), act_cols) / 1024.0
    return (grad_input, grad_weight, act_factor, grad_factor)


def solution(mesh):
    fine = Mesh(mesh.devices.reshape(4, 2, 2, 4, 2, 4), ("y", "core", "zh", "x", "th", "tl"))
    return jax.shard_map(
        on_device,
        mesh=fine,
        in_specs=(P(TOK, IN), P(IN, OUT + TOK), P(TOK, OUT)),
        out_specs=(P(TOK, IN + OUT), P(IN, OUT + TOK), P(IN + TOK, OUT), P(OUT + TOK, IN)),
        check_vma=False,
    )
```

time: 566 us -> 263 us (0.46)
  the two profiles are of different devices: /device:TPU:8 before, /device:TPU:36 now
where the time goes in v1:
time: 263 us; the launch traced here: 262 us
  waiting for transfers between devices  118 us (45%)
  starting transfers between devices  63.6 us (24%)
  blocking collectives  26.8 us (10%)
  local copies, waits for them, and re-layouts  15.5 us (6%)
  between operations  14.2 us (5%)
  matrix products  13.9 us (5%)
  other arithmetic  10.5 us (4%)
    all_to_all x8, waiting for transfers between devices, exchange(): return lax.all_to_all(value, axis, split_axis=0, concat_axis=0, tiled=True)  91.1 us
    all_to_all x8, starting transfers between devices, exchange(): return lax.all_to_all(value, axis, split_axis=0, concat_axis=0, tiled=True)  50.2 us
    all_to_all x3, blocking collectives, exchange(): return lax.all_to_all(value, axis, split_axis=0, concat_axis=0, tiled=True)  26.8 us
    all_gather x1, waiting for transfers between devices, on_device(): pieces = lax.all_gather(grad_piece, TOK, axis=0, tiled=True)  18.6 us
    ppermute x2, starting transfers between devices, swap(): return lax.ppermute(value, axis, [(0, 1), (1, 0)])  11 us
    dot_general x3, matrix products, tn_dot(): lax.dot_general(left, right, (((0,), (0,)), ((), ())), preferred_element_...  8.82 us
    ppermute x2, waiting for transfers between devices, swap(): return lax.ppermute(value, axis, [(0, 1), (1, 0)])  7.13 us
    reduce_sum x5, other arithmetic, total(): return jnp.sum(parts.astype(F32), axis=0)  5.9 us
  transfers between devices with their start and end apart: 12, of which 10 were waited for; matrix products, arithmetic and copies ran while one was open for 10% of the time, Pallas kernels for 0%

profile of v1, /device:TPU:36, one launch (start us, length us, event | category | flops | bytes accessed | tf_op | source)
XLA Modules:
  0.0 262.0 jit_solution(55352189075165316)
XLA Ops:
  7.2 0.9 constant_dynamic-slice_fusion.1
  8.1 9.1 %collective-permute-start = (bf16[32,1024]{1,0:T(8,128)(2,1)S(1)}, bf16[32,1024]{1,0:T(8,128)(2,1)S(1)}, u32[]{:S(2)}, u32[]{:S(2)}) collective-permute-start(bf16[32,1024]{1,0:T(8,128)(2,1)S(1)} %constant_dynamic-slice_fusion.1), channel_id=1, source_target_pairs={{0,4},{4,0},{1,5},{5,1},{2,6},{6,2},{3,7},{7,3},{8,12},{12,8},{9,1... | collective-permute-start | bytes 196616 | tf_op jit(solution)/shard_map/gather_tokens/ppermute | solution.py:26
  17.2 0.9 fusion.21
  18.1 4.2 %collective-permute-done = bf16[32,1024]{1,0:T(8,128)(2,1)S(1)} collective-permute-done((bf16[32,1024]{1,0:T(8,128)(2,1)S(1)}, bf16[32,1024]{1,0:T(8,128)(2,1)S(1)}, u32[]{:S(2)}, u32[]{:S(2)}) %collective-permute-start) | collective-permute-done | bytes 65568 | tf_op jit(solution)/shard_map/gather_tokens/ppermute | solution.py:26
  22.3 17.7 %all_to_all.55 = bf16[4,2,32,1024]{3,2,1,0:T(8,128)(2,1)S(1)} all-to-all(bf16[4,2,32,1024]{3,2,1,0:T(8,128)(2,1)S(1)} %broadcast_in_dim.12), channel_id=1, replica_groups=mesh['y'=4,'core'=2,'zh'=2,'x'=4,'th'=2,'tl'=4] {'tl'}, dimensions={0} | all-to-all | bytes 1048576 | tf_op jit(solution)/shard_map/gather_tokens/all_to_all | solution.py:30
  40.0 1.6 broadcast_in_dim.28
  41.6 4.8 %all-to-all-start.2 = ((bf16[4,256,1024]{2,1,0:T(8,128)(2,1)}), bf16[4,256,1024]{2,1,0:T(8,128)(2,1)S(1)}, u32[]{:S(2)}, u32[]{:S(2)}) async-start(bf16[4,256,1024]{2,1,0:T(8,128)(2,1)} %broadcast_in_dim.28), calls=%async_computation.2 | async-start | bytes 4194304 | tf_op jit(solution)/shard_map/gather_tokens/all_to_all | solution.py:30
  46.4 22.1 %all-to-all-done.2 = bf16[4,256,1024]{2,1,0:T(8,128)(2,1)S(1)} async-done(((bf16[4,256,1024]{2,1,0:T(8,128)(2,1)}), bf16[4,256,1024]{2,1,0:T(8,128)(2,1)S(1)}, u32[]{:S(2)}, u32[]{:S(2)}) %all-to-all-start.2) | async-done | bytes 2097184 | tf_op jit(solution)/shard_map/gather_tokens/all_to_all | solution.py:30
  68.5 2.5 convolution_convert_fusion.1
  71.0 4.6 %all_to_all.56 = f16[2,512,512]{2,1,0:T(8,128)(2,1)S(1)} all-to-all(f16[2,512,512]{2,1,0:T(8,128)(2,1)S(1)} %bitcast.63), channel_id=1, replica_groups=mesh['y'=4,'core'=2,'zh'=2,'x'=4,'th'=2,'tl'=4] {'core'}, dimensions={0} | all-to-all | bytes 2097152 | tf_op jit(solution)/shard_map/preact/all_to_all | solution.py:30
  75.8 0.9 convert_element_type.52
  76.7 4.4 %all-to-all-start.4 = ((f16[4,128,512]{2,1,0:T(8,128)(2,1)}), f16[4,128,512]{2,1,0:T(8,128)(2,1)}, u32[]{:S(2)}, u32[]{:S(2)}) async-start(f16[4,128,512]{2,1,0:T(8,128)(2,1)} %bitcast.53), calls=%async_computation.4 | async-start | bytes 1048576 | tf_op jit(solution)/shard_map/preact/all_to_all | solution.py:30
  81.2 0.7 copy.26
  81.9 9.1 %all-to-all-done.4 = f16[4,128,512]{2,1,0:T(8,128)(2,1)} async-done(((f16[4,128,512]{2,1,0:T(8,128)(2,1)}), f16[4,128,512]{2,1,0:T(8,128)(2,1)}, u32[]{:S(2)}, u32[]{:S(2)}) %all-to-all-start.4) | async-done | bytes 524320 | tf_op jit(solution)/shard_map/preact/all_to_all | solution.py:30
  91.0 11.2 %all-to-all-start = ((bf16[8,16,512]{2,1,0:T(8,128)(2,1)}), bf16[8,16,512]{2,1,0:T(8,128)(2,1)}, u32[]{:S(2)}, u32[]{:S(2)}) async-start(bf16[8,16,512]{2,1,0:T(8,128)(2,1)} %copy.26), calls=%async_computation | async-start | bytes 262144 | tf_op jit(solution)/shard_map/grad_out_piece/all_to_all | solution.py:30
  102.2 1.1 convert_reduce_fusion.1
  103.4 9.4 %all-to-all-done = bf16[8,16,512]{2,1,0:T(8,128)(2,1)} async-done(((bf16[8,16,512]{2,1,0:T(8,128)(2,1)}), bf16[8,16,512]{2,1,0:T(8,128)(2,1)}, u32[]{:S(2)}, u32[]{:S(2)}) %all-to-all-start) | async-done | bytes 131104 | tf_op jit(solution)/shard_map/grad_out_piece/all_to_all | solution.py:30
  112.8 1.1 fusion.10
  113.9 0.8 broadcast_in_dim.29
  114.7 4.1 %all-to-all-start.5 = ((bf16[4,128,512]{2,1,0:T(8,128)(2,1)}), bf16[4,128,512]{2,1,0:T(8,128)(2,1)}, u32[]{:S(2)}, u32[]{:S(2)}) async-start(bf16[4,128,512]{2,1,0:T(8,128)(2,1)} %broadcast_in_dim.29), calls=%async_computation.5 | async-start | bytes 1048576 | tf_op jit(solution)/shard_map/gather_grad/all_to_all | solution.py:30
  118.9 2.3 copy.28
  121.1 5.9 %all-to-all-done.5 = bf16[4,128,512]{2,1,0:T(8,128)(2,1)} async-done(((bf16[4,128,512]{2,1,0:T(8,128)(2,1)}), bf16[4,128,512]{2,1,0:T(8,128)(2,1)}, u32[]{:S(2)}, u32[]{:S(2)}) %all-to-all-start.5) | async-done | bytes 524320 | tf_op jit(solution)/shard_map/gather_grad/all_to_all | solution.py:30
  127.0 1.2 broadcast_in_dim.31
  128.2 4.6 %all_to_all.57 = bf16[2,512,512]{2,1,0:T(8,128)(2,1)S(1)} all-to-all(bf16[2,512,512]{2,1,0:T(8,128)(2,1)S(1)} %broadcast_in_dim.31), channel_id=1, replica_groups=mesh['y'=4,'core'=2,'zh'=2,'x'=4,'th'=2,'tl'=4] {'core'}, dimensions={0} | all-to-all | bytes 2097152 | tf_op jit(solution)/shard_map/gather_grad/all_to_all | solution.py:30
  132.8 1.0 copy-done.2
  133.8 2.6 convert_bitcast_fusion
  136.4 7.4 %all-to-all-start.7 = ((bf16[4,1024,256]{2,1,0:T(8,128)(2,1)}), bf16[4,1024,256]{2,1,0:T(8,128)(2,1)}, u32[]{:S(2)}, u32[]{:S(2)}) async-start(bf16[4,1024,256]{2,1,0:T(8,128)(2,1)} %convert_bitcast_fusion), calls=%async_computation.7 | async-start | bytes 4194304 | tf_op jit(solution)/shard_map/grad_input/all_to_all | solution.py:30
  143.8 0.7 all-gather.2.cloned.1.call-update
  144.5 23.3 %all-to-all-done.7 = bf16[4,1024,256]{2,1,0:T(8,128)(2,1)} async-done(((bf16[4,1024,256]{2,1,0:T(8,128)(2,1)}), bf16[4,1024,256]{2,1,0:T(8,128)(2,1)}, u32[]{:S(2)}, u32[]{:S(2)}) %all-to-all-start.7) | async-done | bytes 2097184 | tf_op jit(solution)/shard_map/grad_input/all_to_all | solution.py:30
  167.8 2.8 %reduce_sum.56 = bf16[1024,256]{1,0:T(8,128)(2,1)} reduce(bf16[4,1024,256]{2,1,0:T(8,128)(2,1)} %all-to-all-done.7, bf16[]{:T(256)} %constant.78.clone.1), dimensions={0}, to_apply=%region_2.3 | reduce | flops 786432 | bytes 2621442 | tf_op jit(solution)/shard_map/grad_input/reduce_sum | solution.py:39
  170.6 1.9 copy.29
  172.6 5.1 %all-to-all-start.8 = ((bf16[4,8,2,16,256]{4,3,2,1,0:T(8,128)(2,1)}), bf16[4,8,2,16,256]{4,3,2,1,0:T(8,128)(2,1)}, u32[]{:S(2)}, u32[]{:S(2)}) async-start(bf16[4,8,2,16,256]{4,3,2,1,0:T(8,128)(2,1)} %copy.29), calls=%async_computation.8 | async-start | bytes 1048576 | tf_op jit(solution)/shard_map/grad_input/all_to_all | solution.py:30
  177.6 1.1 constant_dynamic-slice_fusion
  178.7 1.9 collective-permute-start.1
  180.6 2.9 %collective-permute-done.1 = bf16[1024,512]{1,0:T(8,128)(2,1)} collective-permute-done((bf16[1024,512]{1,0:T(8,128)(2,1)}, bf16[1024,512]{1,0:T(8,128)(2,1)}, u32[]{:S(2)}, u32[]{:S(2)}) %collective-permute-start.1) | collective-permute-done | bytes 1048608 | tf_op jit(solution)/shard_map/act_factor/ppermute | solution.py:26
  183.6 2.6 broadcast_select_fusion
  186.2 2.5 collective-permute-start.2
  188.6 18.6 %all-gather.2.cloned.1.call-done = bf16[1024,512]{1,0:T(8,128)(2,1)} async-done(((bf16[128,512]{1,0:T(8,128)(2,1)}), bf16[1024,512]{1,0:T(8,128)(2,1)}) %all-gather.2.cloned.1.call-update) | async-done | bytes 1048592 | tf_op jit(solution)/shard_map/grad_factor/all_gather | solution.py:93
  207.3 2.3 copy.31
  209.5 4.7 %all-to-all-start.10 = ((bf16[8,128,512]{2,1,0:T(8,128)(2,1)}), bf16[8,128,512]{2,1,0:T(8,128)(2,1)}, u32[]{:S(2)}, u32[]{:S(2)}) async-start(bf16[8,128,512]{2,1,0:T(8,128)(2,1)} %bitcast.52), calls=%async_computation.10 | async-start | bytes 2097152 | tf_op jit(solution)/shard_map/grad_factor/all_to_all | solution.py:30
  214.2 3.5 %convolution_convert_fusion = bf16[1024,512]{1,0:T(8,128)(2,1)} fusion(bf16[1024,1024]{1,0:T(8,128)(2,1)S(1)} %bitcast.50, bf16[1024,512]{1,0:T(8,128)(2,1)} %bitcast.59), kind=kOutput, calls=%fused_computation.2 | convolution fusion | flops 1074266112 | bytes 4194304 | tf_op jit(solution)/shard_map/grad_weight/dot_general | solution.py:51
  217.7 1.1 reduce_sum.57
  218.9 0.7 copy.30
  219.6 10.1 %all-to-all-done.10 = bf16[8,128,512]{2,1,0:T(8,128)(2,1)} async-done(((bf16[8,128,512]{2,1,0:T(8,128)(2,1)}), bf16[8,128,512]{2,1,0:T(8,128)(2,1)}, u32[]{:S(2)}, u32[]{:S(2)}) %all-to-all-start.10) | async-done | bytes 1048608 | tf_op jit(solution)/shard_map/grad_factor/all_to_all | solution.py:30
  229.7 8.4 %all-to-all-start.9 = ((bf16[4,128,128]{2,1,0:T(8,128)(2,1)}), bf16[4,128,128]{2,1,0:T(8,128)(2,1)S(1)}, u32[]{:S(2)}, u32[]{:S(2)}) async-start(bf16[4,128,128]{2,1,0:T(8,128)(2,1)} %bitcast.20), calls=%async_computation.9 | async-start | bytes 262144 | tf_op jit(solution)/shard_map/grad_input/all_to_all | solution.py:30
  238.1 2.4 convolution_multiply_fusion.1
  240.5 2.9 %convolution_multiply_fusion = f32[512,512]{1,0:T(8,128)} fusion(bf16[1024,512]{1,0:T(8,128)(2,1)S(1)} %bitcast.60, bf16[1024,512]{1,0:T(8,128)(2,1)} %bitcast.24), kind=kOutput, calls=%fused_computation.4 | convolution fusion | flops 537133056 | bytes 3145728 | tf_op jit(solution)/shard_map/grad_factor/dot_general | solution.py:51
  243.4 11.2 %all-to-all-done.9 = bf16[4,128,128]{2,1,0:T(8,128)(2,1)S(1)} async-done(((bf16[4,128,128]{2,1,0:T(8,128)(2,1)}), bf16[4,128,128]{2,1,0:T(8,128)(2,1)S(1)}, u32[]{:S(2)}, u32[]{:S(2)}) %all-to-all-start.9) | async-done | bytes 131104 | tf_op jit(solution)/shard_map/grad_input/all_to_all | solution.py:30
  (20 shorter events, 1.0 us)
Async XLA Ops:
  7.2 73.9 %copy-start = (bf16[128,4096]{1,0:T(8,128)(2,1)S(1)}, bf16[128,4096]{1,0:T(8,128)(2,1)}, u32[]{:S(2)}) copy-start(bf16[128,4096]{1,0:T(8,128)(2,1)} %param.5) | copy-start | bytes 3145732
  8.1 14.1 %collective-permute-start = (bf16[32,1024]{1,0:T(8,128)(2,1)S(1)}, bf16[32,1024]{1,0:T(8,128)(2,1)S(1)}, u32[]{:S(2)}, u32[]{:S(2)}) collective-permute-start(bf16[32,1024]{1,0:T(8,128)(2,1)S(1)} %constant_dynamic-slice_fusion.1), channel_id=1, source_target_pairs={{0,4},{4,0},{1,5},{5,1},{2,6},{6,2},{3,7},{7,3},{8,12},{12,8},{9,1... | collective-permute-start | bytes 196616 | tf_op jit(solution)/shard_map/gather_tokens/ppermute | solution.py:26
  41.6 26.9 %all-to-all-start.2 = ((bf16[4,256,1024]{2,1,0:T(8,128)(2,1)}), bf16[4,256,1024]{2,1,0:T(8,128)(2,1)S(1)}, u32[]{:S(2)}, u32[]{:S(2)}) async-start(bf16[4,256,1024]{2,1,0:T(8,128)(2,1)} %broadcast_in_dim.28), calls=%async_computation.2 | async-start | bytes 4194304 | tf_op jit(solution)/shard_map/gather_tokens/all_to_all | solution.py:30
  76.7 14.3 %all-to-all-start.4 = ((f16[4,128,512]{2,1,0:T(8,128)(2,1)}), f16[4,128,512]{2,1,0:T(8,128)(2,1)}, u32[]{:S(2)}, u32[]{:S(2)}) async-start(f16[4,128,512]{2,1,0:T(8,128)(2,1)} %bitcast.53), calls=%async_computation.4 | async-start | bytes 1048576 | tf_op jit(solution)/shard_map/preact/all_to_all | solution.py:30
  91.0 21.8 %all-to-all-start = ((bf16[8,16,512]{2,1,0:T(8,128)(2,1)}), bf16[8,16,512]{2,1,0:T(8,128)(2,1)}, u32[]{:S(2)}, u32[]{:S(2)}) async-start(bf16[8,16,512]{2,1,0:T(8,128)(2,1)} %copy.26), calls=%async_computation | async-start | bytes 262144 | tf_op jit(solution)/shard_map/grad_out_piece/all_to_all | solution.py:30
  113.9 14.4 %copy-start.1 = (bf16[128,512]{1,0:T(8,128)(2,1)}, bf16[128,512]{1,0:T(8,128)(2,1)S(1)}, u32[]{:S(2)}) copy-start(bf16[128,512]{1,0:T(8,128)(2,1)S(1)} %fusion.10) | copy-start | bytes 393220
  114.7 12.3 %all-to-all-start.5 = ((bf16[4,128,512]{2,1,0:T(8,128)(2,1)}), bf16[4,128,512]{2,1,0:T(8,128)(2,1)}, u32[]{:S(2)}, u32[]{:S(2)}) async-start(bf16[4,128,512]{2,1,0:T(8,128)(2,1)} %broadcast_in_dim.29), calls=%async_computation.5 | async-start | bytes 1048576 | tf_op jit(solution)/shard_map/gather_grad/all_to_all | solution.py:30
  127.0 6.8 %copy-start.4 = (bf16[4,2,128,512]{3,2,1,0:T(8,128)(2,1)S(1)}, bf16[4,2,128,512]{3,2,1,0:T(8,128)(2,1)}, u32[]{:S(2)}) copy-start(bf16[4,2,128,512]{3,2,1,0:T(8,128)(2,1)} %copy.28) | copy-start | bytes 3145732
  132.8 1.0 copy-start.2
  136.4 31.5 %all-to-all-start.7 = ((bf16[4,1024,256]{2,1,0:T(8,128)(2,1)}), bf16[4,1024,256]{2,1,0:T(8,128)(2,1)}, u32[]{:S(2)}, u32[]{:S(2)}) async-start(bf16[4,1024,256]{2,1,0:T(8,128)(2,1)} %convert_bitcast_fusion), calls=%async_computation.7 | async-start | bytes 4194304 | tf_op jit(solution)/shard_map/grad_input/all_to_all | solution.py:30
  143.8 63.5 %all-gather.2.cloned.1.call-start = ((), (), s32[]{:S(2)}) async-start(), calls=%async_computation.11 | async-start | bytes 1179648 | tf_op jit(solution)/shard_map/grad_factor/all_gather | solution.py:93
  172.6 37.0 %all-to-all-start.8 = ((bf16[4,8,2,16,256]{4,3,2,1,0:T(8,128)(2,1)}), bf16[4,8,2,16,256]{4,3,2,1,0:T(8,128)(2,1)}, u32[]{:S(2)}, u32[]{:S(2)}) async-start(bf16[4,8,2,16,256]{4,3,2,1,0:T(8,128)(2,1)} %copy.29), calls=%async_computation.8 | async-start | bytes 1048576 | tf_op jit(solution)/shard_map/grad_input/all_to_all | solution.py:30
  178.7 4.9 %collective-permute-start.1 = (bf16[1024,512]{1,0:T(8,128)(2,1)}, bf16[1024,512]{1,0:T(8,128)(2,1)}, u32[]{:S(2)}, u32[]{:S(2)}) collective-permute-start(bf16[1024,512]{1,0:T(8,128)(2,1)} %constant_dynamic-slice_fusion), channel_id=1, source_target_pairs={{0,64},{64,0},{1,65},{65,1},{2,66},{66,2},{3,67},{67,3},{4,68},{68... | collective-permute-start | bytes 3145736 | tf_op jit(solution)/shard_map/act_factor/ppermute | solution.py:26
  186.2 51.9 %collective-permute-start.2 = (bf16[1024,512]{1,0:T(8,128)(2,1)}, bf16[1024,512]{1,0:T(8,128)(2,1)}, u32[]{:S(2)}, u32[]{:S(2)}) collective-permute-start(bf16[1024,512]{1,0:T(8,128)(2,1)} %broadcast_select_fusion), channel_id=1, source_target_pairs={{0,128},{128,0},{256,384},{384,256},{1,129},{129,1},{257,385},{385... | collective-permute-start | bytes 3145736 | tf_op jit(solution)/shard_map/act_factor/ppermute | solution.py:101
  209.5 20.2 %all-to-all-start.10 = ((bf16[8,128,512]{2,1,0:T(8,128)(2,1)}), bf16[8,128,512]{2,1,0:T(8,128)(2,1)}, u32[]{:S(2)}, u32[]{:S(2)}) async-start(bf16[8,128,512]{2,1,0:T(8,128)(2,1)} %bitcast.52), calls=%async_computation.10 | async-start | bytes 2097152 | tf_op jit(solution)/shard_map/grad_factor/all_to_all | solution.py:30
  229.7 24.9 %all-to-all-start.9 = ((bf16[4,128,128]{2,1,0:T(8,128)(2,1)}), bf16[4,128,128]{2,1,0:T(8,128)(2,1)S(1)}, u32[]{:S(2)}, u32[]{:S(2)}) async-start(bf16[4,128,128]{2,1,0:T(8,128)(2,1)} %bitcast.20), calls=%async_computation.9 | async-start | bytes 262144 | tf_op jit(solution)/shard_map/grad_input/all_to_all | solution.py:30
  238.1 2.4 copy-start.3
Sparse Core Ops, SparseCore 0:
  147.2 59.9 all-gather.1

commit v2 on v1

v2 whole, which is shorter than its diff:
```python
import math

import jax
import jax.numpy as jnp
from jax import lax
from jax.sharding import Mesh, PartitionSpec as P

BF16 = jnp.bfloat16
F16 = jnp.float16
F32 = jnp.float32
IN = ("y", "core")
OUT = ("zh", "x")
TOK = ("th", "tl")
SCALE = 4096.0


def gelu_slope(values):
    scale = math.sqrt(2.0 / math.pi)
    cubic = values * values * values
    tanh_val = jnp.tanh(scale * (values + 0.044715 * cubic))
    return 0.5 * (1.0 + tanh_val) + 0.5 * values * (1.0 - tanh_val * tanh_val) * scale * (
        1.0 + 3.0 * 0.044715 * values * values
    )


def swap(value, axis):
    return lax.ppermute(value, axis, [(0, 1), (1, 0)])


def ring(step):
    return [(i, (i + step) % 4) for i in range(4)]


def shift(value, step):
    return lax.ppermute(value, "x", ring(step))


def pick(values, at):
    low = jnp.where(at == 0, values[0], values[1])
    high = jnp.where(at == 2, values[2], values[3])
    return jnp.where(at < 2, low, high)


def skew(value, sign):
    pairs = [(k * 4 + i, k * 4 + (i + sign * k) % 4) for k in range(4) for i in range(4)]
    return lax.ppermute(value, ("y", "x"), pairs)


def exchange(value, axis):
    return lax.all_to_all(value, axis, split_axis=0, concat_axis=0, tiled=True)


def spread(value, axis):
    size = lax.axis_size(axis)
    return exchange(jnp.broadcast_to(value[None], (size,) + value.shape), axis)


def total(parts):
    return jnp.sum(parts.astype(F32), axis=0)


def rows_of(value, start, size):
    return lax.dynamic_slice_in_dim(value, start, size, 0)


def cols_of(value, start, size):
    return lax.dynamic_slice_in_dim(value, start, size, 1)


def both_th(own, other, th):
    return jnp.where(th == 0, jnp.stack([own, other]), jnp.stack([other, own]))


def dot(left, right):
    return jnp.dot(left, right, preferred_element_type=F32)


def nt_dot(left, right):
    return lax.dot_general(left, right, (((1,), (1,)), ((), ())), preferred_element_type=F32)


def tn_dot(left, right):
    return lax.dot_general(left, right, (((0,), (0,)), ((), ())), preferred_element_type=F32)


def on_device(tokens_in, weight, grad_out):
    y, core, x, th, tl = (lax.axis_index(a) for a in ("y", "core", "x", "th", "tl"))
    zh = lax.axis_index("zh")
    tok = th * 4 + tl

    with jax.named_scope("gather_weight"):
        after, before = shift(weight, -1), shift(weight, 1)
        far_top, far_low = shift(after[:512], -1), shift(before[512:], 1)
        far = jnp.concatenate([far_top, far_low], axis=0)
        weights = (weight, after, far, before)

    with jax.named_scope("gather_tokens"):
        own = rows_of(tokens_in, x * 32, 32)
        skewed = skew(rows_of(grad_out, (x - y) % 4 * 32 + core * 16, 16), -1)
        keep, send = cols_of(skewed, th * 2048, 2048), cols_of(skewed, (1 - th) * 2048, 2048)
        send = jnp.concatenate([own, send[:, :1024], send[:, 1024:]], axis=0)
        got = swap(send, "th")
        got_grad = jnp.concatenate([got[32:48], got[48:]], axis=1)
        near_grad = both_th(keep.reshape(16, 4, 512), got_grad.reshape(16, 4, 512), th)
        near_grad = near_grad.transpose(2, 1, 0, 3).reshape(4, 16, 1024)
        near = both_th(own, got[:32], th).reshape(64, 1024)
        near = jnp.concatenate([jnp.broadcast_to(near[None], (4, 64, 1024)), near_grad], axis=1)
        near = exchange(near, "tl")
        tokens = near[:, :64].reshape(4, 2, 2, 16, 1024).transpose(2, 1, 0, 3, 4).reshape(256, 1024)
        grad_out_piece = near[:, 64:].reshape(4, 16, 2, 512).transpose(2, 0, 1, 3).reshape(128, 512)

    with jax.named_scope("preact"):
        partial = [
            dot(tokens, weight),
            dot(tokens, after),
            dot(tokens[:, :512], far_top) + dot(tokens[:, 512:], far_low),
            dot(tokens, before),
        ]
        partial = jnp.stack([part.astype(F16) for part in partial])
        partial, late_tokens = lax.optimization_barrier((partial, tokens))
        preact = total(exchange(partial.reshape(8, 128, 512), IN))
        grad_piece = (grad_out_piece.astype(F32) * gelu_slope(preact)).astype(BF16)
        factor_piece = skew(grad_piece, 1)
        grad_piece, factor_piece = lax.optimization_barrier((grad_piece, factor_piece))

    with jax.named_scope("all_tokens"):
        all_tokens = [late_tokens] + [shift(late_tokens, k) for k in range(1, 4)]
        all_tokens = jnp.concatenate(all_tokens, axis=0)

    with jax.named_scope("gather_grad"):
        scaled = (grad_piece.astype(F32) * SCALE).astype(F16)
        grads = lax.all_gather(scaled, IN, axis=0, tiled=True).reshape(4, 256, 512)
        grads = (grads.astype(F32) * (1.0 / SCALE)).astype(BF16)

    with jax.named_scope("grad_input"):
        share = sum(nt_dot(grads[k], weights[k]) for k in range(4)).astype(BF16)
        share = share.reshape(2, 2, 4, 16, 1024).transpose(2, 0, 1, 3, 4)
        part = total(exchange(share, "tl")).astype(BF16)
        part = part.reshape(2, 2, 16, 2, 512).transpose(3, 1, 0, 2, 4).reshape(4, 32, 512)
        part = total(exchange(part, ("zh", "th"))).astype(BF16)
        part = part.reshape(32, 4, 128).transpose(1, 0, 2)
        grad_input = exchange(part, "x").reshape(128, 128)

    with jax.named_scope("grad_columns"):
        grad_cols = jnp.stack([grads[0]] + [shift(grads[k], k) for k in range(1, 4)])

        grad_cols = grad_cols.reshape(1024, 512)

    with jax.named_scope("grad_weight"):
        grad_weight = tn_dot(all_tokens, grad_cols).astype(BF16)

    with jax.named_scope("grad_factor"):
        pieces = both_th(factor_piece, swap(factor_piece, "th"), th)
        pieces = [pieces] + [lax.ppermute(pieces, "tl", ring(k)) for k in range(1, 4)]
        pieces = jnp.stack([pick(pieces, (tl - a) % 4) for a in range(4)], axis=1)
        cross = exchange(pieces.reshape(8, 128, 512), IN).reshape(1024, 512)
        grad_factor = tn_dot(grad_cols, cross) / 1024.0

    with jax.named_scope("act_factor"):
        act_cols = cols_of(all_tokens, x % 2 * 512, 512)
        act_cols = jnp.where(core == x // 2, act_cols, swap(act_cols, "core"))
        from_y = lax.ppermute(act_cols, "y", [(0, 1), (1, 0), (2, 3), (3, 2)])
        act_cols = jnp.where(y % 2 == zh, act_cols, from_y)
        act_factor = tn_dot(cols_of(all_tokens, tok * 128, 128), act_cols) / 1024.0
    return (grad_input, grad_weight, act_factor, grad_factor)


def solution(mesh):
    fine = Mesh(mesh.devices.reshape(4, 2, 2, 4, 2, 4), ("y", "core", "zh", "x", "th", "tl"))
    return jax.shard_map(
        on_device,
        mesh=fine,
        in_specs=(P(TOK, IN), P(IN, OUT + TOK), P(TOK, OUT)),
        out_specs=(P(TOK, IN + OUT), P(IN, OUT + TOK), P(IN + TOK, OUT), P(OUT + TOK, IN)),
        check_vma=False,
    )
```

time: 263 us -> 263 us (level)
  the two profiles are of different devices: /device:TPU:36 before, /device:TPU:40 now
where the time goes in v2:
time: 263 us; the launch traced here: 261 us
  starting transfers between devices  115 us (44%)
  waiting for transfers between devices  83.7 us (32%)
  local copies, waits for them, and re-layouts  23.1 us (9%)
  matrix products  16.7 us (6%)
  blocking collectives  12.8 us (5%)
  other arithmetic  8.98 us (3%)
    all_to_all x6, starting transfers between devices, exchange(): return lax.all_to_all(value, axis, split_axis=0, concat_axis=0, tiled=True)  38.9 us
    ppermute x10, starting transfers between devices, shift(): return lax.ppermute(value, 'x', ring(step))  36.7 us
    ppermute x10, waiting for transfers between devices, shift(): return lax.ppermute(value, 'x', ring(step))  31.5 us
    all_to_all x6, waiting for transfers between devices, exchange(): return lax.all_to_all(value, axis, split_axis=0, concat_axis=0, tiled=True)  21.6 us
    ppermute x3, starting transfers between devices, swap(): return lax.ppermute(value, axis, [(0, 1), (1, 0)])  19.6 us
    ppermute x3, waiting for transfers between devices, swap(): return lax.ppermute(value, axis, [(0, 1), (1, 0)])  15.1 us
    ppermute x3, waiting for transfers between devices, on_device(): lax.ppermute(pieces, 'tl', ring(k))  14.4 us
    all_gather x1, blocking collectives, on_device(): grads = lax.all_gather(scaled, IN, axis=0, tiled=True).reshape(4, 256, 512)  12.8 us
  transfers between devices with their start and end apart: 25, of which 14 were waited for; matrix products, arithmetic and copies ran while one was open for 16% of the time, Pallas kernels for 0%

profile of v2, /device:TPU:40, one launch (start us, length us, event | category | flops | bytes accessed | tf_op | source)
XLA Modules:
  0.0 261.4 jit_solution(5999060037828342006)
XLA Ops:
  1.9 4.7 %collective-permute-start = (bf16[16,4096]{1,0:T(8,128)(2,1)S(1)}, bf16[16,4096]{1,0:T(8,128)(2,1)S(1)}, u32[]{:S(2)}, u32[]{:S(2)}) collective-permute-start(bf16[16,4096]{1,0:T(8,128)(2,1)S(1)} %constant_dynamic-slice_fusion.4), channel_id=1, source_target_pairs={{0,0},{8,8},{16,16},{24,24},{128,152},{136,128},{144,136},{152,144... | collective-permute-start | bytes 393224 | tf_op jit(solution)/shard_map/gather_tokens/ppermute | solution.py:46
  9.3 9.1 %collective-permute-start.1 = (bf16[64,1024]{1,0:T(8,128)(2,1)S(1)}, bf16[64,1024]{1,0:T(8,128)(2,1)S(1)}, u32[]{:S(2)}, u32[]{:S(2)}) collective-permute-start(bf16[64,1024]{1,0:T(8,128)(2,1)S(1)} %pad_maximum_fusion.4), channel_id=1, source_target_pairs={{0,4},{4,0},{1,5},{5,1},{2,6},{6,2},{3,7},{7,3},{8,12},{12,8},{9,1... | collective-permute-start | bytes 393224 | tf_op jit(solution)/shard_map/gather_tokens/ppermute | solution.py:27
  18.5 8.3 %collective-permute-done.1 = bf16[64,1024]{1,0:T(8,128)(2,1)S(1)} collective-permute-done((bf16[64,1024]{1,0:T(8,128)(2,1)S(1)}, bf16[64,1024]{1,0:T(8,128)(2,1)S(1)}, u32[]{:S(2)}, u32[]{:S(2)}) %collective-permute-start.1) | collective-permute-done | bytes 131104 | tf_op jit(solution)/shard_map/gather_tokens/ppermute | solution.py:27
  28.1 6.9 %all-to-all-start = ((bf16[4,80,1024]{2,1,0:T(8,128)(2,1)}), bf16[4,80,1024]{2,1,0:T(8,128)(2,1)}, u32[]{:S(2)}, u32[]{:S(2)}) async-start(bf16[4,80,1024]{2,1,0:T(8,128)(2,1)} %pad_maximum_fusion.3), calls=%async_computation | async-start | bytes 1310720 | tf_op jit(solution)/shard_map/gather_tokens/all_to_all | solution.py:50
  35.1 3.1 %collective-permute-start.4 = (bf16[1024,512]{1,0:T(8,128)(2,1)S(1)}, bf16[1024,512]{1,0:T(8,128)(2,1)S(1)}, u32[]{:S(2)}, u32[]{:S(2)}) collective-permute-start(bf16[1024,512]{1,0:T(8,128)(2,1)S(1)} %copy-done.6), channel_id=1, source_target_pairs={{0,8},{8,16},{16,24},{24,0},{1,9},{9,17},{17,25},{25,1},{2,10},{10... | collective-permute-start | bytes 3145736 | tf_op jit(solution)/shard_map/gather_weight/ppermute | solution.py:35
  38.2 4.4 %collective-permute-start.2 = (bf16[1024,512]{1,0:T(8,128)(2,1)S(1)}, bf16[1024,512]{1,0:T(8,128)(2,1)S(1)}, u32[]{:S(2)}, u32[]{:S(2)}) collective-permute-start(bf16[1024,512]{1,0:T(8,128)(2,1)S(1)} %copy-done.6), channel_id=1, source_target_pairs={{0,24},{8,0},{16,8},{24,16},{1,25},{9,1},{17,9},{25,17},{2,26},{10... | collective-permute-start | bytes 3145736 | tf_op jit(solution)/shard_map/gather_weight/ppermute | solution.py:35
  42.6 20.5 %collective-permute-done.4 = bf16[1024,512]{1,0:T(8,128)(2,1)S(1)} collective-permute-done((bf16[1024,512]{1,0:T(8,128)(2,1)S(1)}, bf16[1024,512]{1,0:T(8,128)(2,1)S(1)}, u32[]{:S(2)}, u32[]{:S(2)}) %collective-permute-start.4) | collective-permute-done | bytes 1048608 | tf_op jit(solution)/shard_map/gather_weight/ppermute | solution.py:35
  64.0 1.9 collective-permute-start.5
  67.7 5.1 %collective-permute-start.3 = (bf16[512,512]{1,0:T(8,128)(2,1)}, bf16[512,512]{1,0:T(8,128)(2,1)S(1)}, u32[]{:S(2)}, u32[]{:S(2)}) collective-permute-start(bf16[512,512]{1,0:T(8,128)(2,1)} %slice.77), channel_id=1, source_target_pairs={{0,24},{8,0},{16,8},{24,16},{1,25},{9,1},{17,9},{25,17},{2,26},{10... | collective-permute-start | bytes 1572872 | tf_op jit(solution)/shard_map/gather_weight/ppermute | solution.py:35
  74.0 1.7 fusion.3
  76.7 3.0 %collective-permute-done.5 = bf16[512,512]{1,0:T(8,128)(2,1)} collective-permute-done((bf16[512,512]{1,0:T(8,128)(2,1)}, bf16[512,512]{1,0:T(8,128)(2,1)}, u32[]{:S(2)}, u32[]{:S(2)}) %collective-permute-start.5) | collective-permute-done | bytes 524320 | tf_op jit(solution)/shard_map/gather_weight/ppermute | solution.py:35
  81.0 1.7 collective-permute-done.3
  84.3 5.1 %all-to-all-start.1 = ((f16[8,128,512]{2,1,0:T(8,128)(2,1)}), f16[8,128,512]{2,1,0:T(8,128)(2,1)S(1)}, u32[]{:S(2)}, u32[]{:S(2)}) async-start(f16[8,128,512]{2,1,0:T(8,128)(2,1)} %bitcast.75), calls=%async_computation.1 | async-start | bytes 2097152 | tf_op jit(solution)/shard_map/preact/all_to_all | solution.py:50
  92.3 11.7 %all-to-all-done.1 = f16[8,128,512]{2,1,0:T(8,128)(2,1)S(1)} async-done(((f16[8,128,512]{2,1,0:T(8,128)(2,1)}), f16[8,128,512]{2,1,0:T(8,128)(2,1)S(1)}, u32[]{:S(2)}, u32[]{:S(2)}) %all-to-all-start.1) | async-done | bytes 1048608 | tf_op jit(solution)/shard_map/preact/all_to_all | solution.py:50
  104.3 3.0 %collective-permute-start.6 = (bf16[128,512]{1,0:T(8,128)(2,1)S(1)}, bf16[128,512]{1,0:T(8,128)(2,1)S(1)}, u32[]{:S(2)}, u32[]{:S(2)}) collective-permute-start(bf16[128,512]{1,0:T(8,128)(2,1)S(1)} %fusion.20), channel_id=1, source_target_pairs={{0,0},{8,8},{16,16},{24,24},{128,136},{136,144},{144,152},{152,128... | collective-permute-start | bytes 393224 | tf_op jit(solution)/shard_map/preact/ppermute | solution.py:46
  107.2 3.1 %collective-permute-start.7 = (bf16[256,1024]{1,0:T(8,128)(2,1)S(1)}, bf16[256,1024]{1,0:T(8,128)(2,1)}, u32[]{:S(2)}, u32[]{:S(2)}) collective-permute-start(bf16[256,1024]{1,0:T(8,128)(2,1)S(1)} %bitcast.71), channel_id=1, source_target_pairs={{0,8},{8,16},{16,24},{24,0},{1,9},{9,17},{17,25},{25,1},{2,10},{10... | collective-permute-start | bytes 1572872 | tf_op jit(solution)/shard_map/all_tokens/ppermute | solution.py:35
  110.3 4.9 %collective-permute-start.8 = (bf16[256,1024]{1,0:T(8,128)(2,1)S(1)}, bf16[256,1024]{1,0:T(8,128)(2,1)}, u32[]{:S(2)}, u32[]{:S(2)}) collective-permute-start(bf16[256,1024]{1,0:T(8,128)(2,1)S(1)} %bitcast.72), channel_id=1, source_target_pairs={{0,16},{8,24},{16,0},{24,8},{1,17},{9,25},{17,1},{25,9},{2,18},{10... | collective-permute-start | bytes 1572872 | tf_op jit(solution)/shard_map/all_tokens/ppermute | solution.py:35
  115.2 4.5 %collective-permute-start.9 = (bf16[256,1024]{1,0:T(8,128)(2,1)S(1)}, bf16[256,1024]{1,0:T(8,128)(2,1)}, u32[]{:S(2)}, u32[]{:S(2)}) collective-permute-start(bf16[256,1024]{1,0:T(8,128)(2,1)S(1)} %bitcast.73), channel_id=1, source_target_pairs={{0,24},{8,0},{16,8},{24,16},{1,25},{9,1},{17,9},{25,17},{2,26},{10... | collective-permute-start | bytes 1572872 | tf_op jit(solution)/shard_map/all_tokens/ppermute | solution.py:35
  119.8 12.8 %all-gather.1 = f16[1024,512]{1,0:T(8,128)(2,1)S(1)} all-gather(f16[128,512]{1,0:T(8,128)(2,1)S(1)} %multiply_convert_fusion.1), channel_id=1, replica_groups=mesh['y'=4,'core'=2,'zh'=2,'x'=4,'th'=2,'tl'=4] {'y','core'}, dimensions={0}, use_global_device_ids=true | all-gather | bytes 1179648 | tf_op jit(solution)/shard_map/gather_grad/all_gather | solution.py:132
  137.1 5.1 %all-to-all-start.2 = ((bf16[4,2,2,16,1024]{4,3,2,1,0:T(8,128)(2,1)}), bf16[4,2,2,16,1024]{4,3,2,1,0:T(8,128)(2,1)S(1)}, u32[]{:S(2)}, u32[]{:S(2)}) async-start(bf16[4,2,2,16,1024]{4,3,2,1,0:T(8,128)(2,1)} %bitcast.77), calls=%async_computation.2 | async-start | bytes 1048576 | tf_op jit(solution)/shard_map/grad_input/all_to_all | solution.py:50
  143.0 1.9 constant_dynamic-update-slice_fusion.2
  144.9 1.9 constant_dynamic-update-slice_fusion.1
  146.8 1.9 constant_dynamic-update-slice_fusion
  148.6 8.6 %collective-permute-start.15 = (bf16[128,512]{1,0:T(8,128)(2,1)S(1)}, bf16[128,512]{1,0:T(8,128)(2,1)S(1)}, u32[]{:S(2)}, u32[]{:S(2)}) collective-permute-start(bf16[128,512]{1,0:T(8,128)(2,1)S(1)} %collective-permute-done.6), channel_id=1, source_target_pairs={{0,4},{4,0},{1,5},{5,1},{2,6},{6,2},{3,7},{7,3},{8,12},{12,8},{9,1... | collective-permute-start | bytes 393224 | tf_op jit(solution)/shard_map/grad_factor/ppermute | solution.py:27
  157.3 2.3 constant_dynamic-slice_fusion.1
  159.6 1.9 collective-permute-start.13
  161.5 6.8 %collective-permute-done.15 = bf16[128,512]{1,0:T(8,128)(2,1)S(1)} collective-permute-done((bf16[128,512]{1,0:T(8,128)(2,1)S(1)}, bf16[128,512]{1,0:T(8,128)(2,1)S(1)}, u32[]{:S(2)}, u32[]{:S(2)}) %collective-permute-start.15) | collective-permute-done | bytes 131104 | tf_op jit(solution)/shard_map/grad_factor/ppermute | solution.py:27
  168.3 4.1 %collective-permute-start.17 = (bf16[2,128,512]{2,1,0:T(8,128)(2,1)S(1)}, bf16[2,128,512]{2,1,0:T(8,128)(2,1)S(1)}, u32[]{:S(2)}, u32[]{:S(2)}) collective-permute-start(bf16[2,128,512]{2,1,0:T(8,128)(2,1)S(1)} %maximum_select_fusion), channel_id=1, source_target_pairs={{0,2},{1,3},{2,0},{3,1},{4,6},{5,7},{6,4},{7,5},{8,10},{9,11},{10,... | collective-permute-start | bytes 786440 | tf_op jit(solution)/shard_map/grad_factor/ppermute | solution.py:154
  172.4 1.9 collective-permute-start.18
  174.4 3.9 %collective-permute-start.16 = (bf16[2,128,512]{2,1,0:T(8,128)(2,1)S(1)}, bf16[2,128,512]{2,1,0:T(8,128)(2,1)}, u32[]{:S(2)}, u32[]{:S(2)}) collective-permute-start(bf16[2,128,512]{2,1,0:T(8,128)(2,1)S(1)} %maximum_select_fusion), channel_id=1, source_target_pairs={{0,1},{1,2},{2,3},{3,0},{4,5},{5,6},{6,7},{7,4},{8,9},{9,10},{10,1... | collective-permute-start | bytes 786440 | tf_op jit(solution)/shard_map/grad_factor/ppermute | solution.py:154
  178.4 8.9 %collective-permute-done.17 = bf16[2,128,512]{2,1,0:T(8,128)(2,1)S(1)} collective-permute-done((bf16[2,128,512]{2,1,0:T(8,128)(2,1)S(1)}, bf16[2,128,512]{2,1,0:T(8,128)(2,1)S(1)}, u32[]{:S(2)}, u32[]{:S(2)}) %collective-permute-start.17) | collective-permute-done | bytes 262176 | tf_op jit(solution)/shard_map/grad_factor/ppermute | solution.py:154
  187.3 5.4 %collective-permute-done.18 = bf16[2,128,512]{2,1,0:T(8,128)(2,1)} collective-permute-done((bf16[2,128,512]{2,1,0:T(8,128)(2,1)S(1)}, bf16[2,128,512]{2,1,0:T(8,128)(2,1)}, u32[]{:S(2)}, u32[]{:S(2)}) %collective-permute-start.18) | collective-permute-done | bytes 262176 | tf_op jit(solution)/shard_map/grad_factor/ppermute | solution.py:154
  195.3 4.7 %all-to-all-start.5 = ((bf16[8,128,512]{2,1,0:T(8,128)(2,1)}), bf16[8,128,512]{2,1,0:T(8,128)(2,1)}, u32[]{:S(2)}, u32[]{:S(2)}) async-start(bf16[8,128,512]{2,1,0:T(8,128)(2,1)} %bitcast.31), calls=%async_computation.5 | async-start | bytes 2097152 | tf_op jit(solution)/shard_map/grad_factor/all_to_all | solution.py:50
  200.9 2.3 collective-permute-start.12
  203.1 4.1 %collective-permute-start.11 = (bf16[256,512]{1,0:T(8,128)(2,1)}, bf16[256,512]{1,0:T(8,128)(2,1)}, u32[]{:S(2)}, u32[]{:S(2)}) collective-permute-start(bf16[256,512]{1,0:T(8,128)(2,1)} %get-tuple-element.18), channel_id=1, source_target_pairs={{0,16},{8,24},{16,0},{24,8},{1,17},{9,25},{17,1},{25,9},{2,18},{10... | collective-permute-start | bytes 786440 | tf_op jit(solution)/shard_map/grad_columns/ppermute | solution.py:35
  207.3 3.3 %collective-permute-start.10 = (bf16[256,512]{1,0:T(8,128)(2,1)S(1)}, bf16[256,512]{1,0:T(8,128)(2,1)}, u32[]{:S(2)}, u32[]{:S(2)}) collective-permute-start(bf16[256,512]{1,0:T(8,128)(2,1)S(1)} %get-tuple-element.19), channel_id=1, source_target_pairs={{0,8},{8,16},{16,24},{24,0},{1,9},{9,17},{17,25},{25,1},{2,10},{10... | collective-permute-start | bytes 786440 | tf_op jit(solution)/shard_map/grad_columns/ppermute | solution.py:35
  210.6 1.5 broadcast_select_fusion
  212.1 2.1 collective-permute-start.14
  214.2 1.8 collective-permute-done.11
  216.0 4.5 %collective-permute-done.10 = bf16[256,512]{1,0:T(8,128)(2,1)} collective-permute-done((bf16[256,512]{1,0:T(8,128)(2,1)S(1)}, bf16[256,512]{1,0:T(8,128)(2,1)}, u32[]{:S(2)}, u32[]{:S(2)}) %collective-permute-start.10) | collective-permute-done | bytes 262176 | tf_op jit(solution)/shard_map/grad_columns/ppermute | solution.py:35
  220.5 2.1 pad_maximum_fusion.1
  223.5 13.4 %all-to-all-start.3 = ((bf16[4,32,512]{2,1,0:T(8,128)(2,1)}), bf16[4,32,512]{2,1,0:T(8,128)(2,1)S(1)}, u32[]{:S(2)}, u32[]{:S(2)}) async-start(bf16[4,32,512]{2,1,0:T(8,128)(2,1)} %bitcast.17), calls=%async_computation.3 | async-start | bytes 262144 | tf_op jit(solution)/shard_map/grad_input/all_to_all | solution.py:50
  236.9 4.2 %convolution_convert_fusion = bf16[1024,512]{1,0:T(8,128)(2,1)} fusion(bf16[1024,1024]{1,0:T(8,128)(2,1)} %constant_dynamic-update-slice_fusion, bf16[1024,512]{1,0:T(8,128)(2,1)} %bitcast.79), kind=kOutput, calls=%fused_computation.2 | convolution fusion | flops 1074266112 | bytes 4194304 | tf_op jit(solution)/shard_map/grad_weight/dot_general | solution.py:83
  241.1 2.9 %convolution_multiply_fusion = f32[512,512]{1,0:T(8,128)} fusion(bf16[1024,512]{1,0:T(8,128)(2,1)S(1)} %bitcast.80, bf16[1024,512]{1,0:T(8,128)(2,1)} %bitcast.32), kind=kOutput, calls=%fused_computation.3 | convolution fusion | flops 537133056 | bytes 3145728 | tf_op jit(solution)/shard_map/grad_factor/dot_general | solution.py:83
  244.0 6.9 %all-to-all-done.3 = bf16[4,32,512]{2,1,0:T(8,128)(2,1)S(1)} async-done(((bf16[4,32,512]{2,1,0:T(8,128)(2,1)}), bf16[4,32,512]{2,1,0:T(8,128)(2,1)S(1)}, u32[]{:S(2)}, u32[]{:S(2)}) %all-to-all-start.3) | async-done | bytes 131104 | tf_op jit(solution)/shard_map/grad_input/all_to_all | solution.py:50
  251.6 3.8 %all-to-all-start.4 = ((bf16[4,32,128]{2,1,0:T(8,128)(2,1)}), bf16[4,32,128]{2,1,0:T(8,128)(2,1)S(1)}, u32[]{:S(2)}, u32[]{:S(2)}) async-start(bf16[4,32,128]{2,1,0:T(8,128)(2,1)} %copy.21), calls=%async_computation.4 | async-start | bytes 65536 | tf_op jit(solution)/shard_map/grad_input/all_to_all | solution.py:50
  255.3 2.4 convolution_multiply_fusion.1
  257.8 3.0 %all-to-all-done.4 = bf16[4,32,128]{2,1,0:T(8,128)(2,1)S(1)} async-done(((bf16[4,32,128]{2,1,0:T(8,128)(2,1)}), bf16[4,32,128]{2,1,0:T(8,128)(2,1)S(1)}, u32[]{:S(2)}, u32[]{:S(2)}) %all-to-all-start.4) | async-done | bytes 32800 | tf_op jit(solution)/shard_map/grad_input/all_to_all | solution.py:50
  (84 shorter events, 27.1 us)
Async XLA Ops:
  0.6 1.2 copy-start
  1.9 7.4 %collective-permute-start = (bf16[16,4096]{1,0:T(8,128)(2,1)S(1)}, bf16[16,4096]{1,0:T(8,128)(2,1)S(1)}, u32[]{:S(2)}, u32[]{:S(2)}) collective-permute-start(bf16[16,4096]{1,0:T(8,128)(2,1)S(1)} %constant_dynamic-slice_fusion.4), channel_id=1, source_target_pairs={{0,0},{8,8},{16,16},{24,24},{128,152},{136,128},{144,136},{152,144... | collective-permute-start | bytes 393224 | tf_op jit(solution)/shard_map/gather_tokens/ppermute | solution.py:46
  9.3 17.4 %collective-permute-start.1 = (bf16[64,1024]{1,0:T(8,128)(2,1)S(1)}, bf16[64,1024]{1,0:T(8,128)(2,1)S(1)}, u32[]{:S(2)}, u32[]{:S(2)}) collective-permute-start(bf16[64,1024]{1,0:T(8,128)(2,1)S(1)} %pad_maximum_fusion.4), channel_id=1, source_target_pairs={{0,4},{4,0},{1,5},{5,1},{2,6},{6,2},{3,7},{7,3},{8,12},{12,8},{9,1... | collective-permute-start | bytes 393224 | tf_op jit(solution)/shard_map/gather_tokens/ppermute | solution.py:27
  26.9 8.2 %copy-start.6 = (bf16[1024,512]{1,0:T(8,128)(2,1)S(1)}, bf16[1024,512]{1,0:T(8,128)(2,1)}, u32[]{:S(2)}) copy-start(bf16[1024,512]{1,0:T(8,128)(2,1)} %param.4) | copy-start | bytes 3145732
  28.1 44.7 %all-to-all-start = ((bf16[4,80,1024]{2,1,0:T(8,128)(2,1)}), bf16[4,80,1024]{2,1,0:T(8,128)(2,1)}, u32[]{:S(2)}, u32[]{:S(2)}) async-start(bf16[4,80,1024]{2,1,0:T(8,128)(2,1)} %pad_maximum_fusion.3), calls=%async_computation | async-start | bytes 1310720 | tf_op jit(solution)/shard_map/gather_tokens/all_to_all | solution.py:50
  35.1 28.0 %collective-permute-start.4 = (bf16[1024,512]{1,0:T(8,128)(2,1)S(1)}, bf16[1024,512]{1,0:T(8,128)(2,1)S(1)}, u32[]{:S(2)}, u32[]{:S(2)}) collective-permute-start(bf16[1024,512]{1,0:T(8,128)(2,1)S(1)} %copy-done.6), channel_id=1, source_target_pairs={{0,8},{8,16},{16,24},{24,0},{1,9},{9,17},{17,25},{25,1},{2,10},{10... | collective-permute-start | bytes 3145736 | tf_op jit(solution)/shard_map/gather_weight/ppermute | solution.py:35
  38.2 27.7 %collective-permute-start.2 = (bf16[1024,512]{1,0:T(8,128)(2,1)S(1)}, bf16[1024,512]{1,0:T(8,128)(2,1)S(1)}, u32[]{:S(2)}, u32[]{:S(2)}) collective-permute-start(bf16[1024,512]{1,0:T(8,128)(2,1)S(1)} %copy-done.6), channel_id=1, source_target_pairs={{0,24},{8,0},{16,8},{24,16},{1,25},{9,1},{17,9},{25,17},{2,26},{10... | collective-permute-start | bytes 3145736 | tf_op jit(solution)/shard_map/gather_weight/ppermute | solution.py:35
  63.1 12.7 %copy-start.1 = (bf16[1024,512]{1,0:T(8,128)(2,1)}, bf16[1024,512]{1,0:T(8,128)(2,1)S(1)}, u32[]{:S(2)}) copy-start(bf16[1024,512]{1,0:T(8,128)(2,1)S(1)} %collective-permute-done.4) | copy-start | bytes 3145732
  64.0 15.7 %collective-permute-start.5 = (bf16[512,512]{1,0:T(8,128)(2,1)}, bf16[512,512]{1,0:T(8,128)(2,1)}, u32[]{:S(2)}, u32[]{:S(2)}) collective-permute-start(bf16[512,512]{1,0:T(8,128)(2,1)} %slice.79), channel_id=1, source_target_pairs={{0,8},{8,16},{16,24},{24,0},{1,9},{9,17},{17,25},{25,1},{2,10},{10... | collective-permute-start | bytes 1572872 | tf_op jit(solution)/shard_map/gather_weight/ppermute | solution.py:35
  65.9 1.0 copy-start.3
  67.7 15.0 %collective-permute-start.3 = (bf16[512,512]{1,0:T(8,128)(2,1)}, bf16[512,512]{1,0:T(8,128)(2,1)S(1)}, u32[]{:S(2)}, u32[]{:S(2)}) collective-permute-start(bf16[512,512]{1,0:T(8,128)(2,1)} %slice.77), channel_id=1, source_target_pairs={{0,24},{8,0},{16,8},{24,16},{1,25},{9,1},{17,9},{25,17},{2,26},{10... | collective-permute-start | bytes 1572872 | tf_op jit(solution)/shard_map/gather_weight/ppermute | solution.py:35
  74.0 2.2 copy-start.4
  84.3 19.6 %all-to-all-start.1 = ((f16[8,128,512]{2,1,0:T(8,128)(2,1)}), f16[8,128,512]{2,1,0:T(8,128)(2,1)S(1)}, u32[]{:S(2)}, u32[]{:S(2)}) async-start(f16[8,128,512]{2,1,0:T(8,128)(2,1)} %bitcast.75), calls=%async_computation.1 | async-start | bytes 2097152 | tf_op jit(solution)/shard_map/preact/all_to_all | solution.py:50
  104.1 28.7 %copy-start.7 = (bf16[1024,512]{1,0:T(8,128)(2,1)S(1)}, bf16[1024,512]{1,0:T(8,128)(2,1)}, u32[]{:S(2)}) copy-start(bf16[1024,512]{1,0:T(8,128)(2,1)} %param.4) | copy-start | bytes 3145732
  104.3 15.5 %collective-permute-start.6 = (bf16[128,512]{1,0:T(8,128)(2,1)S(1)}, bf16[128,512]{1,0:T(8,128)(2,1)S(1)}, u32[]{:S(2)}, u32[]{:S(2)}) collective-permute-start(bf16[128,512]{1,0:T(8,128)(2,1)S(1)} %fusion.20), channel_id=1, source_target_pairs={{0,0},{8,8},{16,16},{24,24},{128,136},{136,144},{144,152},{152,128... | collective-permute-start | bytes 393224 | tf_op jit(solution)/shard_map/preact/ppermute | solution.py:46
  107.2 35.8 %collective-permute-start.7 = (bf16[256,1024]{1,0:T(8,128)(2,1)S(1)}, bf16[256,1024]{1,0:T(8,128)(2,1)}, u32[]{:S(2)}, u32[]{:S(2)}) collective-permute-start(bf16[256,1024]{1,0:T(8,128)(2,1)S(1)} %bitcast.71), channel_id=1, source_target_pairs={{0,8},{8,16},{16,24},{24,0},{1,9},{9,17},{17,25},{25,1},{2,10},{10... | collective-permute-start | bytes 1572872 | tf_op jit(solution)/shard_map/all_tokens/ppermute | solution.py:35
  110.3 34.6 %collective-permute-start.8 = (bf16[256,1024]{1,0:T(8,128)(2,1)S(1)}, bf16[256,1024]{1,0:T(8,128)(2,1)}, u32[]{:S(2)}, u32[]{:S(2)}) collective-permute-start(bf16[256,1024]{1,0:T(8,128)(2,1)S(1)} %bitcast.72), channel_id=1, source_target_pairs={{0,16},{8,24},{16,0},{24,8},{1,17},{9,25},{17,1},{25,9},{2,18},{10... | collective-permute-start | bytes 1572872 | tf_op jit(solution)/shard_map/all_tokens/ppermute | solution.py:35
  115.2 31.6 %collective-permute-start.9 = (bf16[256,1024]{1,0:T(8,128)(2,1)S(1)}, bf16[256,1024]{1,0:T(8,128)(2,1)}, u32[]{:S(2)}, u32[]{:S(2)}) collective-permute-start(bf16[256,1024]{1,0:T(8,128)(2,1)S(1)} %bitcast.73), channel_id=1, source_target_pairs={{0,24},{8,0},{16,8},{24,16},{1,25},{9,1},{17,9},{25,17},{2,26},{10... | collective-permute-start | bytes 1572872 | tf_op jit(solution)/shard_map/all_tokens/ppermute | solution.py:35
  132.6 1.2 copy-start.2
  132.8 1.5 copy-start.5
  137.1 58.2 %all-to-all-start.2 = ((bf16[4,2,2,16,1024]{4,3,2,1,0:T(8,128)(2,1)}), bf16[4,2,2,16,1024]{4,3,2,1,0:T(8,128)(2,1)S(1)}, u32[]{:S(2)}, u32[]{:S(2)}) async-start(bf16[4,2,2,16,1024]{4,3,2,1,0:T(8,128)(2,1)} %bitcast.77), calls=%async_computation.2 | async-start | bytes 1048576 | tf_op jit(solution)/shard_map/grad_input/all_to_all | solution.py:50
  148.6 19.6 %collective-permute-start.15 = (bf16[128,512]{1,0:T(8,128)(2,1)S(1)}, bf16[128,512]{1,0:T(8,128)(2,1)S(1)}, u32[]{:S(2)}, u32[]{:S(2)}) collective-permute-start(bf16[128,512]{1,0:T(8,128)(2,1)S(1)} %collective-permute-done.6), channel_id=1, source_target_pairs={{0,4},{4,0},{1,5},{5,1},{2,6},{6,2},{3,7},{7,3},{8,12},{12,8},{9,1... | collective-permute-start | bytes 393224 | tf_op jit(solution)/shard_map/grad_factor/ppermute | solution.py:27
  159.6 51.0 %collective-permute-start.13 = (bf16[1024,512]{1,0:T(8,128)(2,1)}, bf16[1024,512]{1,0:T(8,128)(2,1)}, u32[]{:S(2)}, u32[]{:S(2)}) collective-permute-start(bf16[1024,512]{1,0:T(8,128)(2,1)} %constant_dynamic-slice_fusion.1), channel_id=1, source_target_pairs={{0,64},{64,0},{1,65},{65,1},{2,66},{66,2},{3,67},{67,3},{4,68},{68... | collective-permute-start | bytes 3145736 | tf_op jit(solution)/shard_map/act_factor/ppermute | solution.py:27
  168.3 19.0 %collective-permute-start.17 = (bf16[2,128,512]{2,1,0:T(8,128)(2,1)S(1)}, bf16[2,128,512]{2,1,0:T(8,128)(2,1)S(1)}, u32[]{:S(2)}, u32[]{:S(2)}) collective-permute-start(bf16[2,128,512]{2,1,0:T(8,128)(2,1)S(1)} %maximum_select_fusion), channel_id=1, source_target_pairs={{0,2},{1,3},{2,0},{3,1},{4,6},{5,7},{6,4},{7,5},{8,10},{9,11},{10,... | collective-permute-start | bytes 786440 | tf_op jit(solution)/shard_map/grad_factor/ppermute | solution.py:154
  172.4 20.3 %collective-permute-start.18 = (bf16[2,128,512]{2,1,0:T(8,128)(2,1)S(1)}, bf16[2,128,512]{2,1,0:T(8,128)(2,1)}, u32[]{:S(2)}, u32[]{:S(2)}) collective-permute-start(bf16[2,128,512]{2,1,0:T(8,128)(2,1)S(1)} %maximum_select_fusion), channel_id=1, source_target_pairs={{0,3},{1,0},{2,1},{3,2},{4,7},{5,4},{6,5},{7,6},{8,11},{9,8},{10,9... | collective-permute-start | bytes 786440 | tf_op jit(solution)/shard_map/grad_factor/ppermute | solution.py:154
  174.4 18.5 %collective-permute-start.16 = (bf16[2,128,512]{2,1,0:T(8,128)(2,1)S(1)}, bf16[2,128,512]{2,1,0:T(8,128)(2,1)}, u32[]{:S(2)}, u32[]{:S(2)}) collective-permute-start(bf16[2,128,512]{2,1,0:T(8,128)(2,1)S(1)} %maximum_select_fusion), channel_id=1, source_target_pairs={{0,1},{1,2},{2,3},{3,0},{4,5},{5,6},{6,7},{7,4},{8,9},{9,10},{10,1... | collective-permute-start | bytes 786440 | tf_op jit(solution)/shard_map/grad_factor/ppermute | solution.py:154
  187.3 5.4 %copy-start.9 = (bf16[2,128,512]{2,1,0:T(8,128)(2,1)}, bf16[2,128,512]{2,1,0:T(8,128)(2,1)S(1)}, u32[]{:S(2)}) copy-start(bf16[2,128,512]{2,1,0:T(8,128)(2,1)S(1)} %collective-permute-done.17) | copy-start | bytes 786436
  195.3 28.2 %all-to-all-start.5 = ((bf16[8,128,512]{2,1,0:T(8,128)(2,1)}), bf16[8,128,512]{2,1,0:T(8,128)(2,1)}, u32[]{:S(2)}, u32[]{:S(2)}) async-start(bf16[8,128,512]{2,1,0:T(8,128)(2,1)} %bitcast.31), calls=%async_computation.5 | async-start | bytes 2097152 | tf_op jit(solution)/shard_map/grad_factor/all_to_all | solution.py:50
  200.9 13.4 %collective-permute-start.12 = (bf16[256,512]{1,0:T(8,128)(2,1)}, bf16[256,512]{1,0:T(8,128)(2,1)S(1)}, u32[]{:S(2)}, u32[]{:S(2)}) collective-permute-start(bf16[256,512]{1,0:T(8,128)(2,1)} %get-tuple-element.17), channel_id=1, source_target_pairs={{0,24},{8,0},{16,8},{24,16},{1,25},{9,1},{17,9},{25,17},{2,26},{10... | collective-permute-start | bytes 786440 | tf_op jit(solution)/shard_map/grad_columns/ppermute | solution.py:35
  203.1 12.9 %collective-permute-start.11 = (bf16[256,512]{1,0:T(8,128)(2,1)}, bf16[256,512]{1,0:T(8,128)(2,1)}, u32[]{:S(2)}, u32[]{:S(2)}) collective-permute-start(bf16[256,512]{1,0:T(8,128)(2,1)} %get-tuple-element.18), channel_id=1, source_target_pairs={{0,16},{8,24},{16,0},{24,8},{1,17},{9,25},{17,1},{25,9},{2,18},{10... | collective-permute-start | bytes 786440 | tf_op jit(solution)/shard_map/grad_columns/ppermute | solution.py:35
  207.3 13.3 %collective-permute-start.10 = (bf16[256,512]{1,0:T(8,128)(2,1)S(1)}, bf16[256,512]{1,0:T(8,128)(2,1)}, u32[]{:S(2)}, u32[]{:S(2)}) collective-permute-start(bf16[256,512]{1,0:T(8,128)(2,1)S(1)} %get-tuple-element.19), channel_id=1, source_target_pairs={{0,8},{8,16},{16,24},{24,0},{1,9},{9,17},{17,25},{25,1},{2,10},{10... | collective-permute-start | bytes 786440 | tf_op jit(solution)/shard_map/grad_columns/ppermute | solution.py:35
  212.1 43.2 %collective-permute-start.14 = (bf16[1024,512]{1,0:T(8,128)(2,1)S(1)}, bf16[1024,512]{1,0:T(8,128)(2,1)}, u32[]{:S(2)}, u32[]{:S(2)}) collective-permute-start(bf16[1024,512]{1,0:T(8,128)(2,1)S(1)} %broadcast_select_fusion), channel_id=1, source_target_pairs={{0,128},{128,0},{256,384},{384,256},{1,129},{129,1},{257,385},{385... | collective-permute-start | bytes 3145736 | tf_op jit(solution)/shard_map/act_factor/ppermute | solution.py:162
  223.5 27.4 %all-to-all-start.3 = ((bf16[4,32,512]{2,1,0:T(8,128)(2,1)}), bf16[4,32,512]{2,1,0:T(8,128)(2,1)S(1)}, u32[]{:S(2)}, u32[]{:S(2)}) async-start(bf16[4,32,512]{2,1,0:T(8,128)(2,1)} %bitcast.17), calls=%async_computation.3 | async-start | bytes 262144 | tf_op jit(solution)/shard_map/grad_input/all_to_all | solution.py:50
  236.9 4.2 %copy-start.8 = (bf16[4,256,512]{2,1,0:T(8,128)(2,1)S(1)}, bf16[4,256,512]{2,1,0:T(8,128)(2,1)}, u32[]{:S(2)}) copy-start(bf16[4,256,512]{2,1,0:T(8,128)(2,1)} %pad_maximum_fusion.1) | copy-start | bytes 3145732
  251.6 9.2 %all-to-all-start.4 = ((bf16[4,32,128]{2,1,0:T(8,128)(2,1)}), bf16[4,32,128]{2,1,0:T(8,128)(2,1)S(1)}, u32[]{:S(2)}, u32[]{:S(2)}) async-start(bf16[4,32,128]{2,1,0:T(8,128)(2,1)} %copy.21), calls=%async_computation.4 | async-start | bytes 65536 | tf_op jit(solution)/shard_map/grad_input/all_to_all | solution.py:50

commit v3 on v1

v3 whole, which is shorter than its diff:
```python
import math

import jax
import jax.numpy as jnp
from jax import lax
from jax.sharding import Mesh, PartitionSpec as P

BF16 = jnp.bfloat16
F16 = jnp.float16
F32 = jnp.float32
IN = ("y", "core")
OUT = ("zh", "x")
TOK = ("th", "tl")
TOKEN_SCALE = 8192.0
GRAD_SCALE = 4096.0


def gelu_slope(values):
    scale = math.sqrt(2.0 / math.pi)
    cubic = values * values * values
    tanh_val = jnp.tanh(scale * (values + 0.044715 * cubic))
    return 0.5 * (1.0 + tanh_val) + 0.5 * values * (1.0 - tanh_val * tanh_val) * scale * (
        1.0 + 3.0 * 0.044715 * values * values
    )


def swap(value, axis):
    return lax.ppermute(value, axis, [(0, 1), (1, 0)])


def ring(step):
    return [(i, (i + step) % 4) for i in range(4)]


def pick(values, at):
    low = jnp.where(at == 0, values[0], values[1])
    high = jnp.where(at == 2, values[2], values[3])
    return jnp.where(at < 2, low, high)


def exchange(value, axis):
    return lax.all_to_all(value, axis, split_axis=0, concat_axis=0, tiled=True)


def spread(value, axis):
    size = lax.axis_size(axis)
    return exchange(jnp.broadcast_to(value[None], (size,) + value.shape), axis)


def total(parts):
    return jnp.sum(parts.astype(F32), axis=0)


def rows_of(value, start, size):
    return lax.dynamic_slice_in_dim(value, start, size, 0)


def cols_of(value, start, size):
    return lax.dynamic_slice_in_dim(value, start, size, 1)


def both_th(own, other, th):
    return jnp.where(th == 0, jnp.stack([own, other]), jnp.stack([other, own]))


def gather_scaled(value, axis, scale):
    scaled = (value.astype(F32) * scale).astype(F16)
    return lax.all_gather(scaled, axis, axis=0, tiled=True)


def unscaled(value, scale):
    return (value.astype(F32) * (1.0 / scale)).astype(BF16)


def tn_dot(left, right):
    return lax.dot_general(left, right, (((0,), (0,)), ((), ())), preferred_element_type=F32)


def on_device(tokens_in, weight, grad_out):
    y, core, zh, x, th, tl = (lax.axis_index(a) for a in ("y", "core", "zh", "x", "th", "tl"))
    tok = th * 4 + tl
    piece = y * 2 + core

    with jax.named_scope("grad_out_piece"):
        grad_out_rows = lax.all_gather(rows_of(grad_out, piece * 16, 16), TOK, axis=0, tiled=True)

    with jax.named_scope("gather_tokens"):
        own = rows_of(tokens_in, x * 32, 32)
        near = spread(both_th(own, swap(own, "th"), th), "tl")
        near = near.reshape(4, 2, 2, 16, 1024).transpose(2, 1, 0, 3, 4).reshape(256, 1024)
        tokens = unscaled(gather_scaled(near, "x", TOKEN_SCALE), TOKEN_SCALE)

    with jax.named_scope("preact"):
        partial = jnp.dot(tokens, weight, preferred_element_type=F32).astype(F16)
        preact = total(exchange(partial.reshape(8, 128, 512), IN))
        grad_out_piece = cols_of(grad_out_rows, tok * 512, 512)
        grad_piece = (grad_out_piece.astype(F32) * gelu_slope(preact)).astype(BF16)

    with jax.named_scope("gather_grad"):
        grad_rows = gather_scaled(grad_piece, IN, GRAD_SCALE)
        grad_rows, other_piece = lax.optimization_barrier((grad_rows, swap(grad_piece, "th")))
        grad_rows = unscaled(grad_rows, GRAD_SCALE)

    with jax.named_scope("gather_factor"):
        pieces = both_th(grad_piece, other_piece, th)
        pieces = [pieces] + [lax.ppermute(pieces, "tl", ring(k)) for k in range(1, 4)]

    with jax.named_scope("act_columns"):
        act_cols = cols_of(tokens, x % 2 * 512, 512)
        act_cols = jnp.where(core == x // 2, act_cols, swap(act_cols, "core"))
        from_y = lax.ppermute(act_cols, "y", [(0, 1), (1, 0), (2, 3), (3, 2)])

    with jax.named_scope("grad_input"):
        by_x = weight.reshape(2, 4, 128, 512).transpose(1, 0, 2, 3).reshape(4, 256, 512)
        share = jnp.einsum("rc,kfc->krf", grad_rows, by_x, preferred_element_type=F32).astype(BF16)
        part, pieces = lax.optimization_barrier((exchange(share, "x"), pieces))
        part = total(part).astype(BF16).reshape(8, 2, 4, 16, 256).transpose(2, 0, 1, 3, 4)
        part, from_y = lax.optimization_barrier((exchange(part, "tl"), from_y))
        part = total(part).astype(BF16)
        part = part.reshape(8, 2, 16, 2, 128).transpose(3, 1, 0, 2, 4).reshape(4, 128, 128)
        grad_input = total(exchange(part, ("zh", "th"))).astype(BF16)

    with jax.named_scope("grad_weight"):
        grad_weight = tn_dot(tokens, grad_rows).astype(BF16)

    with jax.named_scope("grad_factor"):
        pieces = jnp.stack([pick(pieces, (tl - a) % 4) for a in range(4)], axis=1)
        cross = exchange(pieces.reshape(8, 128, 512), IN).reshape(1024, 512)
        grad_factor = tn_dot(grad_rows, cross) / 1024.0

    with jax.named_scope("act_factor"):
        act_cols = jnp.where(y % 2 == zh, act_cols, from_y)
        act_factor = tn_dot(cols_of(tokens, tok * 128, 128), act_cols) / 1024.0
    return (grad_input, grad_weight, act_factor, grad_factor)


def solution(mesh):
    fine = Mesh(mesh.devices.reshape(4, 2, 2, 4, 2, 4), ("y", "core", "zh", "x", "th", "tl"))
    return jax.shard_map(
        on_device,
        mesh=fine,
        in_specs=(P(TOK, IN), P(IN, OUT + TOK), P(TOK, OUT)),
        out_specs=(P(TOK, IN + OUT), P(IN, OUT + TOK), P(IN + TOK, OUT), P(OUT + TOK, IN)),
        check_vma=False,
    )
```

time: 263 us -> 244 us (0.928)
  the two profiles are of different devices: /device:TPU:36 before, /device:TPU:2 now
where the time goes in v3:
time: 244 us; the launch traced here: 243 us
  waiting for transfers between devices  97.2 us (40%)
  starting transfers between devices  59.8 us (25%)
  blocking collectives  34.8 us (14%)
  matrix products  16.2 us (7%)
  between operations  14.2 us (6%)
  other arithmetic  11.8 us (5%)
  local copies, waits for them, and re-layouts  8.9 us (4%)
    all_to_all x6, waiting for transfers between devices, exchange(): return lax.all_to_all(value, axis, split_axis=0, concat_axis=0, tiled=True)  58.6 us
    all_gather x2, blocking collectives, gather_scaled(): return lax.all_gather(scaled, axis, axis=0, tiled=True)  34.8 us
    all_to_all x6, starting transfers between devices, exchange(): return lax.all_to_all(value, axis, split_axis=0, concat_axis=0, tiled=True)  33.6 us
    all_gather x1, waiting for transfers between devices, on_device(): lax.all_gather(rows_of(grad_out, piece * 16, 16), TOK, axis=0, tiled=True)  15.9 us
    ppermute x3, starting transfers between devices, swap(): return lax.ppermute(value, axis, [(0, 1), (1, 0)])  12.9 us
    ppermute x3, waiting for transfers between devices, on_device(): lax.ppermute(pieces, 'tl', ring(k))  10.3 us
    ppermute x3, starting transfers between devices, on_device(): lax.ppermute(pieces, 'tl', ring(k))  9.95 us
    dot_general x3, matrix products, tn_dot(): lax.dot_general(left, right, (((0,), (0,)), ((), ())), preferred_element_...  9.7 us
  transfers between devices with their start and end apart: 14, of which 9 were waited for; matrix products, arithmetic and copies ran while one was open for 12% of the time, Pallas kernels for 0%

profile of v3, /device:TPU:2, one launch (start us, length us, event | category | flops | bytes accessed | tf_op | source)
XLA Modules:
  0.0 243.0 jit_solution(10082662687141321121)
XLA Ops:
  7.2 0.9 constant_dynamic-slice_fusion.1
  8.1 9.1 %collective-permute-start = (bf16[32,1024]{1,0:T(8,128)(2,1)S(1)}, bf16[32,1024]{1,0:T(8,128)(2,1)S(1)}, u32[]{:S(2)}, u32[]{:S(2)}) collective-permute-start(bf16[32,1024]{1,0:T(8,128)(2,1)S(1)} %constant_dynamic-slice_fusion.1), channel_id=1, source_target_pairs={{0,4},{4,0},{1,5},{5,1},{2,6},{6,2},{3,7},{7,3},{8,12},{12,8},{9,1... | collective-permute-start | bytes 196616 | tf_op jit(solution)/shard_map/gather_tokens/ppermute | solution.py:28
  17.2 0.9 fusion.21
  18.1 5.6 %collective-permute-done = bf16[32,1024]{1,0:T(8,128)(2,1)S(1)} collective-permute-done((bf16[32,1024]{1,0:T(8,128)(2,1)S(1)}, bf16[32,1024]{1,0:T(8,128)(2,1)S(1)}, u32[]{:S(2)}, u32[]{:S(2)}) %collective-permute-start) | collective-permute-done | bytes 65568 | tf_op jit(solution)/shard_map/gather_tokens/ppermute | solution.py:28
  23.7 0.9 broadcast_in_dim.2
  24.5 3.6 %all-to-all-start = ((bf16[4,2,32,1024]{3,2,1,0:T(8,128)(2,1)}), bf16[4,2,32,1024]{3,2,1,0:T(8,128)(2,1)S(1)}, u32[]{:S(2)}, u32[]{:S(2)}) async-start(bf16[4,2,32,1024]{3,2,1,0:T(8,128)(2,1)} %broadcast_in_dim.2), calls=%async_computation | async-start | bytes 1048576 | tf_op jit(solution)/shard_map/gather_tokens/all_to_all | solution.py:42
  28.2 0.7 constant_dynamic-slice_fusion.2
  28.9 13.8 %all-to-all-done = bf16[4,2,32,1024]{3,2,1,0:T(8,128)(2,1)S(1)} async-done(((bf16[4,2,32,1024]{3,2,1,0:T(8,128)(2,1)}), bf16[4,2,32,1024]{3,2,1,0:T(8,128)(2,1)S(1)}, u32[]{:S(2)}, u32[]{:S(2)}) %all-to-all-start) | async-done | bytes 524320 | tf_op jit(solution)/shard_map/gather_tokens/all_to_all | solution.py:42
  42.7 0.1 multiply_convert_fusion.2
  42.9 20.6 %all-gather.5 = f16[1024,1024]{1,0:T(8,128)(2,1)S(1)} all-gather(f16[256,1024]{1,0:T(8,128)(2,1)S(1)} %bitcast.46), channel_id=1, replica_groups=mesh['y'=4,'core'=2,'zh'=2,'x'=4,'th'=2,'tl'=4] {'x'}, dimensions={0}, use_global_device_ids=true | all-gather | bytes 2621440 | tf_op jit(solution)/shard_map/gather_tokens/all_gather | solution.py:68
  63.5 2.2 convolution_convert_fusion.1
  65.7 4.6 %all-to-all-start.1 = ((f16[8,128,512]{2,1,0:T(8,128)(2,1)}), f16[8,128,512]{2,1,0:T(8,128)(2,1)S(1)}, u32[]{:S(2)}, u32[]{:S(2)}) async-start(f16[8,128,512]{2,1,0:T(8,128)(2,1)} %bitcast.51), calls=%async_computation.1 | async-start | bytes 2097152 | tf_op jit(solution)/shard_map/preact/all_to_all | solution.py:42
  70.3 1.0 copy.25
  71.4 14.9 %all-to-all-done.1 = f16[8,128,512]{2,1,0:T(8,128)(2,1)S(1)} async-done(((f16[8,128,512]{2,1,0:T(8,128)(2,1)}), f16[8,128,512]{2,1,0:T(8,128)(2,1)S(1)}, u32[]{:S(2)}, u32[]{:S(2)}) %all-to-all-start.1) | async-done | bytes 1048608 | tf_op jit(solution)/shard_map/preact/all_to_all | solution.py:42
  86.3 0.1 convert_reduce_fusion
  86.4 15.9 %all-gather.4.cloned.1.call-done = bf16[128,4096]{1,0:T(8,128)(2,1)} async-done(((bf16[16,4096]{1,0:T(8,128)(2,1)}), bf16[128,4096]{1,0:T(8,128)(2,1)}) %all-gather.4.cloned.1.call-update) | async-done | bytes 1048592 | tf_op jit(solution)/shard_map/grad_out_piece/all_gather | solution.py:85
  102.3 1.1 multiply_convert_fusion.6
  103.4 1.9 collective-permute-start.1
  105.3 14.2 %all-gather.6 = f16[1024,512]{1,0:T(8,128)(2,1)S(1)} all-gather(f16[128,512]{1,0:T(8,128)(2,1)S(1)} %get-tuple-element.22), channel_id=1, replica_groups=mesh['y'=4,'core'=2,'zh'=2,'x'=4,'th'=2,'tl'=4] {'y','core'}, dimensions={0}, use_global_device_ids=true | all-gather | bytes 1179648 | tf_op jit(solution)/shard_map/gather_grad/all_gather | solution.py:68
  119.6 4.3 %convert_bitcast_fusion = bf16[4,1024,256]{2,1,0:T(8,128)(2,1)} fusion(bf16[4,256,512]{2,1,0:T(8,128)(2,1)} %bitcast.50, f16[1024,512]{1,0:T(8,128)(2,1)S(1)} %all-gather.6), kind=kOutput, calls=%fused_computation.1 | convolution fusion | flops 1076363264 | bytes 4194304 | tf_op jit(solution)/shard_map/grad_input/rc,kfc->krf/dot_general | solution.py:115
  123.9 4.8 %all-to-all-start.2 = ((bf16[4,1024,256]{2,1,0:T(8,128)(2,1)}), bf16[4,1024,256]{2,1,0:T(8,128)(2,1)}, u32[]{:S(2)}, u32[]{:S(2)}) async-start(bf16[4,1024,256]{2,1,0:T(8,128)(2,1)} %convert_bitcast_fusion), calls=%async_computation.2 | async-start | bytes 4194304 | tf_op jit(solution)/shard_map/grad_input/all_to_all | solution.py:42
  128.6 2.2 multiply_convert_fusion
  130.9 1.9 collective-permute-start.2
  132.8 3.8 %collective-permute-start.3 = (bf16[2,128,512]{2,1,0:T(8,128)(2,1)S(1)}, bf16[2,128,512]{2,1,0:T(8,128)(2,1)S(1)}, u32[]{:S(2)}, u32[]{:S(2)}) collective-permute-start(bf16[2,128,512]{2,1,0:T(8,128)(2,1)S(1)} %maximum_select_fusion), channel_id=1, source_target_pairs={{0,2},{1,3},{2,0},{3,1},{4,6},{5,7},{6,4},{7,5},{8,10},{9,11},{10,... | collective-permute-start | bytes 786440 | tf_op jit(solution)/shard_map/gather_factor/ppermute | solution.py:106
  136.6 4.3 %collective-permute-start.4 = (bf16[2,128,512]{2,1,0:T(8,128)(2,1)S(1)}, bf16[2,128,512]{2,1,0:T(8,128)(2,1)}, u32[]{:S(2)}, u32[]{:S(2)}) collective-permute-start(bf16[2,128,512]{2,1,0:T(8,128)(2,1)S(1)} %maximum_select_fusion), channel_id=1, source_target_pairs={{0,3},{1,0},{2,1},{3,2},{4,7},{5,4},{6,5},{7,6},{8,11},{9,8},{10,9... | collective-permute-start | bytes 786440 | tf_op jit(solution)/shard_map/gather_factor/ppermute | solution.py:106
  140.9 1.1 constant_dynamic-slice_fusion
  142.0 1.9 collective-permute-start.5
  143.9 10.3 %collective-permute-done.3 = bf16[2,128,512]{2,1,0:T(8,128)(2,1)S(1)} collective-permute-done((bf16[2,128,512]{2,1,0:T(8,128)(2,1)S(1)}, bf16[2,128,512]{2,1,0:T(8,128)(2,1)S(1)}, u32[]{:S(2)}, u32[]{:S(2)}) %collective-permute-start.3) | collective-permute-done | bytes 262176 | tf_op jit(solution)/shard_map/gather_factor/ppermute | solution.py:106
  154.2 0.7 copy-done.7
  154.9 2.8 %reduce_sum.46 = bf16[1024,256]{1,0:T(8,128)(2,1)} reduce(bf16[4,1024,256]{2,1,0:T(8,128)(2,1)} %all-to-all-done.2, bf16[]{:T(256)} %constant.114.clone.1), dimensions={0}, to_apply=%region_1.2 | reduce | flops 786432 | bytes 2621442 | tf_op jit(solution)/shard_map/grad_input/reduce_sum | solution.py:51
  157.7 1.9 copy.26
  159.6 7.2 %all-to-all-start.3 = ((bf16[4,8,2,16,256]{4,3,2,1,0:T(8,128)(2,1)}), bf16[4,8,2,16,256]{4,3,2,1,0:T(8,128)(2,1)}, u32[]{:S(2)}, u32[]{:S(2)}) async-start(bf16[4,8,2,16,256]{4,3,2,1,0:T(8,128)(2,1)} %copy.26), calls=%async_computation.3 | async-start | bytes 1048576 | tf_op jit(solution)/shard_map/grad_input/all_to_all | solution.py:42
  166.9 1.4 broadcast_select_fusion
  168.3 3.3 %collective-permute-start.6 = (bf16[1024,512]{1,0:T(8,128)(2,1)}, bf16[1024,512]{1,0:T(8,128)(2,1)}, u32[]{:S(2)}, u32[]{:S(2)}) collective-permute-start(bf16[1024,512]{1,0:T(8,128)(2,1)} %broadcast_select_fusion), channel_id=1, source_target_pairs={{0,128},{128,0},{256,384},{384,256},{1,129},{129,1},{257,385},{385... | collective-permute-start | bytes 3145736 | tf_op jit(solution)/shard_map/act_columns/ppermute | solution.py:111
  171.6 1.1 select_bitcast_fusion.3
  172.7 1.1 pad_maximum_fusion
  173.8 7.4 %all-to-all-done.3 = bf16[4,8,2,16,256]{4,3,2,1,0:T(8,128)(2,1)} async-done(((bf16[4,8,2,16,256]{4,3,2,1,0:T(8,128)(2,1)}), bf16[4,8,2,16,256]{4,3,2,1,0:T(8,128)(2,1)}, u32[]{:S(2)}, u32[]{:S(2)}) %all-to-all-start.3) | async-done | bytes 524320 | tf_op jit(solution)/shard_map/grad_input/all_to_all | solution.py:42
  181.2 4.2 %all-to-all-start.5 = ((bf16[8,128,512]{2,1,0:T(8,128)(2,1)}), bf16[8,128,512]{2,1,0:T(8,128)(2,1)}, u32[]{:S(2)}, u32[]{:S(2)}) async-start(bf16[8,128,512]{2,1,0:T(8,128)(2,1)} %bitcast.45), calls=%async_computation.5 | async-start | bytes 2097152 | tf_op jit(solution)/shard_map/grad_factor/all_to_all | solution.py:42
  185.5 4.1 %convolution_convert_fusion = bf16[1024,512]{1,0:T(8,128)(2,1)} fusion(f16[1024,512]{1,0:T(8,128)(2,1)} %copy-done.2, f16[1024,1024]{1,0:T(8,128)(2,1)} %copy-done.1), kind=kOutput, calls=%fused_computation.4 | convolution fusion | flops 1078984704 | bytes 4194304 | tf_op jit(solution)/shard_map/grad_weight/dot_general | solution.py:76
  189.6 6.8 %collective-permute-done.6 = bf16[1024,512]{1,0:T(8,128)(2,1)} collective-permute-done((bf16[1024,512]{1,0:T(8,128)(2,1)}, bf16[1024,512]{1,0:T(8,128)(2,1)}, u32[]{:S(2)}, u32[]{:S(2)}) %collective-permute-start.6) | collective-permute-done | bytes 1048608 | tf_op jit(solution)/shard_map/act_columns/ppermute | solution.py:111
  196.4 1.1 reduce_sum.47
  197.6 0.7 copy.27
  198.3 11.0 %all-to-all-done.5 = bf16[8,128,512]{2,1,0:T(8,128)(2,1)} async-done(((bf16[8,128,512]{2,1,0:T(8,128)(2,1)}), bf16[8,128,512]{2,1,0:T(8,128)(2,1)}, u32[]{:S(2)}, u32[]{:S(2)}) %all-to-all-start.5) | async-done | bytes 1048608 | tf_op jit(solution)/shard_map/grad_factor/all_to_all | solution.py:42
  209.2 9.2 %all-to-all-start.4 = ((bf16[4,128,128]{2,1,0:T(8,128)(2,1)}), bf16[4,128,128]{2,1,0:T(8,128)(2,1)S(1)}, u32[]{:S(2)}, u32[]{:S(2)}) async-start(bf16[4,128,128]{2,1,0:T(8,128)(2,1)} %bitcast.16), calls=%async_computation.4 | async-start | bytes 262144 | tf_op jit(solution)/shard_map/grad_input/all_to_all | solution.py:42
  218.4 3.3 %convolution_multiply_fusion = f32[512,512]{1,0:T(8,128)} fusion(bf16[1024,512]{1,0:T(8,128)(2,1)} %bitcast.25, f16[1024,512]{1,0:T(8,128)(2,1)} %copy-done.2), kind=kOutput, calls=%fused_computation.6 | convolution fusion | flops 538705920 | bytes 3145728 | tf_op jit(solution)/shard_map/grad_factor/dot_general | solution.py:76
  221.7 2.3 convolution_multiply_fusion.1
  224.0 11.5 %all-to-all-done.4 = bf16[4,128,128]{2,1,0:T(8,128)(2,1)S(1)} async-done(((bf16[4,128,128]{2,1,0:T(8,128)(2,1)}), bf16[4,128,128]{2,1,0:T(8,128)(2,1)S(1)}, u32[]{:S(2)}, u32[]{:S(2)}) %all-to-all-start.4) | async-done | bytes 131104 | tf_op jit(solution)/shard_map/grad_input/all_to_all | solution.py:42
  235.5 0.6 reduce_sum.48
  (32 shorter events, 0.3 us)
Async XLA Ops:
  7.2 21.0 %copy-start = (bf16[128,4096]{1,0:T(8,128)(2,1)S(1)}, bf16[128,4096]{1,0:T(8,128)(2,1)}, u32[]{:S(2)}) copy-start(bf16[128,4096]{1,0:T(8,128)(2,1)} %param.5) | copy-start | bytes 3145732
  8.1 15.5 %collective-permute-start = (bf16[32,1024]{1,0:T(8,128)(2,1)S(1)}, bf16[32,1024]{1,0:T(8,128)(2,1)S(1)}, u32[]{:S(2)}, u32[]{:S(2)}) collective-permute-start(bf16[32,1024]{1,0:T(8,128)(2,1)S(1)} %constant_dynamic-slice_fusion.1), channel_id=1, source_target_pairs={{0,4},{4,0},{1,5},{5,1},{2,6},{6,2},{3,7},{7,3},{8,12},{12,8},{9,1... | collective-permute-start | bytes 196616 | tf_op jit(solution)/shard_map/gather_tokens/ppermute | solution.py:28
  24.5 18.2 %all-to-all-start = ((bf16[4,2,32,1024]{3,2,1,0:T(8,128)(2,1)}), bf16[4,2,32,1024]{3,2,1,0:T(8,128)(2,1)S(1)}, u32[]{:S(2)}, u32[]{:S(2)}) async-start(bf16[4,2,32,1024]{3,2,1,0:T(8,128)(2,1)} %broadcast_in_dim.2), calls=%async_computation | async-start | bytes 1048576 | tf_op jit(solution)/shard_map/gather_tokens/all_to_all | solution.py:42
  28.2 74.2 %all-gather.4.cloned.1.call-start = ((), (), s32[]{:S(2)}) async-start(), calls=%async_computation.6 | async-start | bytes 1179648 | tf_op jit(solution)/shard_map/grad_out_piece/all_gather | solution.py:85
  42.8 20.7 %copy-start.3 = (bf16[1024,512]{1,0:T(8,128)(2,1)S(1)}, bf16[1024,512]{1,0:T(8,128)(2,1)}, u32[]{:S(2)}) copy-start(bf16[1024,512]{1,0:T(8,128)(2,1)} %param.4) | copy-start | bytes 3145732
  63.5 2.2 copy-start.1
  65.7 4.6 %copy-start.4 = (bf16[1024,512]{1,0:T(8,128)(2,1)S(1)}, bf16[1024,512]{1,0:T(8,128)(2,1)}, u32[]{:S(2)}) copy-start(bf16[1024,512]{1,0:T(8,128)(2,1)} %param.4) | copy-start | bytes 3145732
  65.7 20.6 %all-to-all-start.1 = ((f16[8,128,512]{2,1,0:T(8,128)(2,1)}), f16[8,128,512]{2,1,0:T(8,128)(2,1)S(1)}, u32[]{:S(2)}, u32[]{:S(2)}) async-start(f16[8,128,512]{2,1,0:T(8,128)(2,1)} %bitcast.51), calls=%async_computation.1 | async-start | bytes 2097152 | tf_op jit(solution)/shard_map/preact/all_to_all | solution.py:42
  103.4 16.2 %collective-permute-start.1 = (bf16[128,512]{1,0:T(8,128)(2,1)S(1)}, bf16[128,512]{1,0:T(8,128)(2,1)S(1)}, u32[]{:S(2)}, u32[]{:S(2)}) collective-permute-start(bf16[128,512]{1,0:T(8,128)(2,1)S(1)} %get-tuple-element.23), channel_id=1, source_target_pairs={{0,4},{4,0},{1,5},{5,1},{2,6},{6,2},{3,7},{7,3},{8,12},{12,8},{9,1... | collective-permute-start | bytes 393224 | tf_op jit(solution)/shard_map/gather_grad/ppermute | solution.py:28
  119.6 4.3 %copy-start.2 = (f16[1024,512]{1,0:T(8,128)(2,1)}, f16[1024,512]{1,0:T(8,128)(2,1)S(1)}, u32[]{:S(2)}) copy-start(f16[1024,512]{1,0:T(8,128)(2,1)S(1)} %all-gather.6) | copy-start | bytes 3145732
  119.6 4.3 %copy-start.9 = (bf16[128,512]{1,0:T(8,128)(2,1)}, bf16[128,512]{1,0:T(8,128)(2,1)S(1)}, u32[]{:S(2)}) copy-start(bf16[128,512]{1,0:T(8,128)(2,1)S(1)} %collective-permute-done.1) | copy-start | bytes 393220
  123.9 31.0 %all-to-all-start.2 = ((bf16[4,1024,256]{2,1,0:T(8,128)(2,1)}), bf16[4,1024,256]{2,1,0:T(8,128)(2,1)}, u32[]{:S(2)}, u32[]{:S(2)}) async-start(bf16[4,1024,256]{2,1,0:T(8,128)(2,1)} %convert_bitcast_fusion), calls=%async_computation.2 | async-start | bytes 4194304 | tf_op jit(solution)/shard_map/grad_input/all_to_all | solution.py:42
  128.6 2.2 copy-start.10
  130.9 13.0 %collective-permute-start.2 = (bf16[2,128,512]{2,1,0:T(8,128)(2,1)S(1)}, bf16[2,128,512]{2,1,0:T(8,128)(2,1)S(1)}, u32[]{:S(2)}, u32[]{:S(2)}) collective-permute-start(bf16[2,128,512]{2,1,0:T(8,128)(2,1)S(1)} %maximum_select_fusion), channel_id=1, source_target_pairs={{0,1},{1,2},{2,3},{3,0},{4,5},{5,6},{6,7},{7,4},{8,9},{9,10},{10,1... | collective-permute-start | bytes 786440 | tf_op jit(solution)/shard_map/gather_factor/ppermute | solution.py:106
  132.8 21.3 %collective-permute-start.3 = (bf16[2,128,512]{2,1,0:T(8,128)(2,1)S(1)}, bf16[2,128,512]{2,1,0:T(8,128)(2,1)S(1)}, u32[]{:S(2)}, u32[]{:S(2)}) collective-permute-start(bf16[2,128,512]{2,1,0:T(8,128)(2,1)S(1)} %maximum_select_fusion), channel_id=1, source_target_pairs={{0,2},{1,3},{2,0},{3,1},{4,6},{5,7},{6,4},{7,5},{8,10},{9,11},{10,... | collective-permute-start | bytes 786440 | tf_op jit(solution)/shard_map/gather_factor/ppermute | solution.py:106
  136.6 18.3 %collective-permute-start.4 = (bf16[2,128,512]{2,1,0:T(8,128)(2,1)S(1)}, bf16[2,128,512]{2,1,0:T(8,128)(2,1)}, u32[]{:S(2)}, u32[]{:S(2)}) collective-permute-start(bf16[2,128,512]{2,1,0:T(8,128)(2,1)S(1)} %maximum_select_fusion), channel_id=1, source_target_pairs={{0,3},{1,0},{2,1},{3,2},{4,7},{5,4},{6,5},{7,6},{8,11},{9,8},{10,9... | collective-permute-start | bytes 786440 | tf_op jit(solution)/shard_map/gather_factor/ppermute | solution.py:106
  142.0 24.9 %collective-permute-start.5 = (bf16[1024,512]{1,0:T(8,128)(2,1)}, bf16[1024,512]{1,0:T(8,128)(2,1)}, u32[]{:S(2)}, u32[]{:S(2)}) collective-permute-start(bf16[1024,512]{1,0:T(8,128)(2,1)} %constant_dynamic-slice_fusion), channel_id=1, source_target_pairs={{0,64},{64,0},{1,65},{65,1},{2,66},{66,2},{3,67},{67,3},{4,68},{68... | collective-permute-start | bytes 3145736 | tf_op jit(solution)/shard_map/act_columns/ppermute | solution.py:28
  143.9 10.3 %copy-start.5 = (bf16[2,128,512]{2,1,0:T(8,128)(2,1)}, bf16[2,128,512]{2,1,0:T(8,128)(2,1)S(1)}, u32[]{:S(2)}) copy-start(bf16[2,128,512]{2,1,0:T(8,128)(2,1)S(1)} %collective-permute-done.2) | copy-start | bytes 786436
  154.2 0.7 copy-start.7
  159.6 21.6 %all-to-all-start.3 = ((bf16[4,8,2,16,256]{4,3,2,1,0:T(8,128)(2,1)}), bf16[4,8,2,16,256]{4,3,2,1,0:T(8,128)(2,1)}, u32[]{:S(2)}, u32[]{:S(2)}) async-start(bf16[4,8,2,16,256]{4,3,2,1,0:T(8,128)(2,1)} %copy.26), calls=%async_computation.3 | async-start | bytes 1048576 | tf_op jit(solution)/shard_map/grad_input/all_to_all | solution.py:42
  166.9 4.8 %copy-start.6 = (bf16[2,128,512]{2,1,0:T(8,128)(2,1)S(1)}, bf16[2,128,512]{2,1,0:T(8,128)(2,1)}, u32[]{:S(2)}) copy-start(bf16[2,128,512]{2,1,0:T(8,128)(2,1)} %copy-done.5) | copy-start | bytes 786436
  166.9 4.8 %copy-start.8 = (bf16[2,128,512]{2,1,0:T(8,128)(2,1)S(1)}, bf16[2,128,512]{2,1,0:T(8,128)(2,1)}, u32[]{:S(2)}) copy-start(bf16[2,128,512]{2,1,0:T(8,128)(2,1)} %copy-done.7) | copy-start | bytes 786436
  168.3 28.1 %collective-permute-start.6 = (bf16[1024,512]{1,0:T(8,128)(2,1)}, bf16[1024,512]{1,0:T(8,128)(2,1)}, u32[]{:S(2)}, u32[]{:S(2)}) collective-permute-start(bf16[1024,512]{1,0:T(8,128)(2,1)} %broadcast_select_fusion), channel_id=1, source_target_pairs={{0,128},{128,0},{256,384},{384,256},{1,129},{129,1},{257,385},{385... | collective-permute-start | bytes 3145736 | tf_op jit(solution)/shard_map/act_columns/ppermute | solution.py:111
  181.2 28.0 %all-to-all-start.5 = ((bf16[8,128,512]{2,1,0:T(8,128)(2,1)}), bf16[8,128,512]{2,1,0:T(8,128)(2,1)}, u32[]{:S(2)}, u32[]{:S(2)}) async-start(bf16[8,128,512]{2,1,0:T(8,128)(2,1)} %bitcast.45), calls=%async_computation.5 | async-start | bytes 2097152 | tf_op jit(solution)/shard_map/grad_factor/all_to_all | solution.py:42
  209.2 26.2 %all-to-all-start.4 = ((bf16[4,128,128]{2,1,0:T(8,128)(2,1)}), bf16[4,128,128]{2,1,0:T(8,128)(2,1)S(1)}, u32[]{:S(2)}, u32[]{:S(2)}) async-start(bf16[4,128,128]{2,1,0:T(8,128)(2,1)} %bitcast.16), calls=%async_computation.4 | async-start | bytes 262144 | tf_op jit(solution)/shard_map/grad_input/all_to_all | solution.py:42
Sparse Core Ops, SparseCore 0:
  31.6 70.6 all-gather.3

commit v4 on v3

--- a/solution.py
+++ b/solution.py
@@ -28,14 +28,9 @@
     return lax.ppermute(value, axis, [(0, 1), (1, 0)])
 
 
-def ring(step):
-    return [(i, (i + step) % 4) for i in range(4)]
-
-
-def pick(values, at):
-    low = jnp.where(at == 0, values[0], values[1])
-    high = jnp.where(at == 2, values[2], values[3])
-    return jnp.where(at < 2, low, high)
+def send_along(value, bit, holders):
+    pairs = [(i * 8 + (i ^ h), i * 8 + (i ^ h ^ bit)) for i in range(8) for h in holders]
+    return lax.ppermute(value, IN + TOK, pairs)
 
 
 def exchange(value, axis):
@@ -59,10 +54,6 @@
     return lax.dynamic_slice_in_dim(value, start, size, 1)
 
 
-def both_th(own, other, th):
-    return jnp.where(th == 0, jnp.stack([own, other]), jnp.stack([other, own]))
-
-
 def gather_scaled(value, axis, scale):
     scaled = (value.astype(F32) * scale).astype(F16)
     return lax.all_gather(scaled, axis, axis=0, tiled=True)
@@ -82,12 +73,14 @@
     piece = y * 2 + core
 
     with jax.named_scope("grad_out_piece"):
-        grad_out_rows = lax.all_gather(rows_of(grad_out, piece * 16, 16), TOK, axis=0, tiled=True)
+        own_grad, own = lax.optimization_barrier(
+            (rows_of(grad_out, piece * 16, 16), rows_of(tokens_in, x * 32, 32))
+        )
+        grad_out_rows = lax.all_gather(own_grad, TOK, axis=0, tiled=True)
 
     with jax.named_scope("gather_tokens"):
-        own = rows_of(tokens_in, x * 32, 32)
-        near = spread(both_th(own, swap(own, "th"), th), "tl")
-        near = near.reshape(4, 2, 2, 16, 1024).transpose(2, 1, 0, 3, 4).reshape(256, 1024)
+        near = spread(own, TOK).reshape(8, 2, 16, 1024)
+        near = near.transpose(1, 0, 2, 3).reshape(256, 1024)
         tokens = unscaled(gather_scaled(near, "x", TOKEN_SCALE), TOKEN_SCALE)
 
     with jax.named_scope("preact"):
@@ -97,13 +90,14 @@
         grad_piece = (grad_out_piece.astype(F32) * gelu_slope(preact)).astype(BF16)
 
     with jax.named_scope("gather_grad"):
-        grad_rows = gather_scaled(grad_piece, IN, GRAD_SCALE)
-        grad_rows, other_piece = lax.optimization_barrier((grad_rows, swap(grad_piece, "th")))
-        grad_rows = unscaled(grad_rows, GRAD_SCALE)
+        grad_rows = unscaled(gather_scaled(grad_piece, IN, GRAD_SCALE), GRAD_SCALE)
 
-    with jax.named_scope("gather_factor"):
-        pieces = both_th(grad_piece, other_piece, th)
-        pieces = [pieces] + [lax.ppermute(pieces, "tl", ring(k)) for k in range(1, 4)]
+    with jax.named_scope("factor_columns"):
+        away = tok ^ piece
+        far = send_along(grad_rows, 4, (0,))
+        cross = jnp.where(away == 0, grad_rows, far)
+        mid = send_along(cross, 2, (0, 4))
+        cross = jnp.where(away & 2 == 0, cross, mid)
 
     with jax.named_scope("act_columns"):
         act_cols = cols_of(tokens, x % 2 * 512, 512)
@@ -113,19 +107,19 @@
     with jax.named_scope("grad_input"):
         by_x = weight.reshape(2, 4, 128, 512).transpose(1, 0, 2, 3).reshape(4, 256, 512)
         share = jnp.einsum("rc,kfc->krf", grad_rows, by_x, preferred_element_type=F32).astype(BF16)
-        part, pieces = lax.optimization_barrier((exchange(share, "x"), pieces))
+        part, far = lax.optimization_barrier((exchange(share, "x"), far))
         part = total(part).astype(BF16).reshape(8, 2, 4, 16, 256).transpose(2, 0, 1, 3, 4)
-        part, from_y = lax.optimization_barrier((exchange(part, "tl"), from_y))
-        part = total(part).astype(BF16)
+        part = total(exchange(part, "tl")).astype(BF16)
         part = part.reshape(8, 2, 16, 2, 128).transpose(3, 1, 0, 2, 4).reshape(4, 128, 128)
+        part, cross, from_y = lax.optimization_barrier((part, cross, from_y))
         grad_input = total(exchange(part, ("zh", "th"))).astype(BF16)
 
     with jax.named_scope("grad_weight"):
         grad_weight = tn_dot(tokens, grad_rows).astype(BF16)
 
     with jax.named_scope("grad_factor"):
-        pieces = jnp.stack([pick(pieces, (tl - a) % 4) for a in range(4)], axis=1)
-        cross = exchange(pieces.reshape(8, 128, 512), IN).reshape(1024, 512)
+        near = send_along(cross, 1, (0, 2, 4, 6))
+        cross = jnp.where(away & 1 == 0, cross, near)
         grad_factor = tn_dot(grad_rows, cross) / 1024.0
 
     with jax.named_scope("act_factor"):

time: 244 us -> 231 us (0.947)
  the two profiles are of different devices: /device:TPU:2 before, /device:TPU:14 now
where the time goes in v4:
time: 231 us; the launch traced here: 230 us
  waiting for transfers between devices  96.4 us (42%)
  starting transfers between devices  52 us (23%)
  blocking collectives  29.9 us (13%)
  other arithmetic  15.5 us (7%)
  matrix products  14.6 us (6%)
  between operations  14.2 us (6%)
  local copies, waits for them, and re-layouts  7.64 us (3%)
    all_to_all x5, waiting for transfers between devices, exchange(): return lax.all_to_all(value, axis, split_axis=0, concat_axis=0, tiled=True)  70 us
    all_to_all x5, starting transfers between devices, exchange(): return lax.all_to_all(value, axis, split_axis=0, concat_axis=0, tiled=True)  36.1 us
    all_gather x2, blocking collectives, gather_scaled(): return lax.all_gather(scaled, axis, axis=0, tiled=True)  29.9 us
    ppermute x3, waiting for transfers between devices, send_along(): return lax.ppermute(value, IN + TOK, pairs)  23.1 us
    dot_general x3, matrix products, tn_dot(): lax.dot_general(left, right, (((0,), (0,)), ((), ())), preferred_element_...  9.71 us
    ppermute x1, starting transfers between devices, on_device(): from_y = lax.ppermute(act_cols, 'y', [(0, 1), (1, 0), (2, 3), (3, 2)])  8.68 us
    ppermute x3, starting transfers between devices, send_along(): return lax.ppermute(value, IN + TOK, pairs)  5.25 us
    reduce_sum x4, other arithmetic, total(): return jnp.sum(parts.astype(F32), axis=0)  4.74 us
  transfers between devices with their start and end apart: 11, of which 6 were waited for; matrix products, arithmetic and copies ran while one was open for 12% of the time, Pallas kernels for 0%

profile of v4, /device:TPU:14, one launch (start us, length us, event | category | flops | bytes accessed | tf_op | source)
XLA Modules:
  0.0 230.2 jit_solution(18253924408560697830)
XLA Ops:
  7.2 0.0 copy-start
  7.2 0.9 constant_dynamic-slice_fusion.1
  8.1 0.3 copy-done
  8.4 0.7 constant_dynamic-slice_fusion.2
  9.1 0.9 broadcast_in_dim.2
  9.9 12.5 %all-to-all-start = ((bf16[8,32,1024]{2,1,0:T(8,128)(2,1)}), bf16[8,32,1024]{2,1,0:T(8,128)(2,1)S(1)}, u32[]{:S(2)}, u32[]{:S(2)}) async-start(bf16[8,32,1024]{2,1,0:T(8,128)(2,1)} %broadcast_in_dim.2), calls=%async_computation | async-start | bytes 1048576 | tf_op jit(solution)/shard_map/gather_tokens/all_to_all | solution.py:37
  22.5 0.0 all-gather.4.cloned.1.call-start
  22.5 0.7 all-gather.4.cloned.1.call-update
  23.2 28.4 %all-to-all-done = bf16[8,32,1024]{2,1,0:T(8,128)(2,1)S(1)} async-done(((bf16[8,32,1024]{2,1,0:T(8,128)(2,1)}), bf16[8,32,1024]{2,1,0:T(8,128)(2,1)S(1)}, u32[]{:S(2)}, u32[]{:S(2)}) %all-to-all-start) | async-done | bytes 524320 | tf_op jit(solution)/shard_map/gather_tokens/all_to_all | solution.py:37
  51.6 0.1 multiply_convert_fusion.2
  51.8 0.0 copy-start.4
  51.8 0.1 copy.15
  51.9 16.1 %all-gather.5 = f16[1024,1024]{1,0:T(8,128)(2,1)S(1)} all-gather(f16[256,1024]{1,0:T(8,128)(2,1)S(1)} %bitcast.23), channel_id=1, replica_groups=mesh['y'=4,'core'=2,'zh'=2,'x'=4,'th'=2,'tl'=4] {'x'}, dimensions={0}, use_global_device_ids=true | all-gather | bytes 2621440 | tf_op jit(solution)/shard_map/gather_tokens/all_gather | solution.py:59
  68.0 2.2 convolution_convert_fusion.1
  70.2 5.0 %all-to-all-start.1 = ((f16[8,128,512]{2,1,0:T(8,128)(2,1)}), f16[8,128,512]{2,1,0:T(8,128)(2,1)S(1)}, u32[]{:S(2)}, u32[]{:S(2)}) async-start(f16[8,128,512]{2,1,0:T(8,128)(2,1)} %bitcast.27), calls=%async_computation.1 | async-start | bytes 2097152 | tf_op jit(solution)/shard_map/preact/all_to_all | solution.py:37
  75.2 1.1 copy.16
  76.3 13.4 %all-to-all-done.1 = f16[8,128,512]{2,1,0:T(8,128)(2,1)S(1)} async-done(((f16[8,128,512]{2,1,0:T(8,128)(2,1)}), f16[8,128,512]{2,1,0:T(8,128)(2,1)S(1)}, u32[]{:S(2)}, u32[]{:S(2)}) %all-to-all-start.1) | async-done | bytes 1048608 | tf_op jit(solution)/shard_map/preact/all_to_all | solution.py:37
  89.7 0.1 convert_reduce_fusion
  89.9 2.7 %all-gather.4.cloned.1.call-done = bf16[128,4096]{1,0:T(8,128)(2,1)} async-done(((bf16[16,4096]{1,0:T(8,128)(2,1)}), bf16[128,4096]{1,0:T(8,128)(2,1)}) %all-gather.4.cloned.1.call-update) | async-done | bytes 1048592 | tf_op jit(solution)/shard_map/grad_out_piece/all_gather | solution.py:79
  92.6 1.1 multiply_convert_fusion.3
  93.7 13.9 %all-gather.6 = f16[1024,512]{1,0:T(8,128)(2,1)S(1)} all-gather(f16[128,512]{1,0:T(8,128)(2,1)S(1)} %multiply_convert_fusion.3), channel_id=1, replica_groups=mesh['y'=4,'core'=2,'zh'=2,'x'=4,'th'=2,'tl'=4] {'y','core'}, dimensions={0}, use_global_device_ids=true | all-gather | bytes 1179648 | tf_op jit(solution)/shard_map/gather_grad/all_gather | solution.py:59
  107.5 2.6 %convert_bitcast_fusion = bf16[4,1024,256]{2,1,0:T(8,128)(2,1)} fusion(bf16[4,256,512]{2,1,0:T(8,128)(2,1)S(1)} %bitcast.28, f16[1024,512]{1,0:T(8,128)(2,1)S(1)} %all-gather.6), kind=kOutput, calls=%fused_computation.1 | convolution fusion | flops 1076363264 | bytes 4194304 | tf_op jit(solution)/shard_map/grad_input/rc,kfc->krf/dot_general | solution.py:109
  110.1 4.9 %all-to-all-start.2 = ((bf16[4,1024,256]{2,1,0:T(8,128)(2,1)}), bf16[4,1024,256]{2,1,0:T(8,128)(2,1)}, u32[]{:S(2)}, u32[]{:S(2)}) async-start(bf16[4,1024,256]{2,1,0:T(8,128)(2,1)} %convert_bitcast_fusion), calls=%async_computation.2 | async-start | bytes 4194304 | tf_op jit(solution)/shard_map/grad_input/all_to_all | solution.py:37
  115.1 1.2 multiply_convert_fusion.1
  116.2 1.7 collective-permute-start
  117.9 0.6 multiply_convert_fusion
  118.5 1.1 constant_dynamic-slice_fusion
  119.6 1.9 collective-permute-start.2
  121.6 0.0 collective-permute-done
  121.6 18.6 %all-to-all-done.2 = bf16[4,1024,256]{2,1,0:T(8,128)(2,1)} async-done(((bf16[4,1024,256]{2,1,0:T(8,128)(2,1)}), bf16[4,1024,256]{2,1,0:T(8,128)(2,1)}, u32[]{:S(2)}, u32[]{:S(2)}) %all-to-all-start.2) | async-done | bytes 2097184 | tf_op jit(solution)/shard_map/grad_input/all_to_all | solution.py:37
  140.1 2.8 %reduce_sum.46 = bf16[1024,256]{1,0:T(8,128)(2,1)} reduce(bf16[4,1024,256]{2,1,0:T(8,128)(2,1)} %all-to-all-done.2, bf16[]{:T(256)} %constant.91.clone.1), dimensions={0}, to_apply=%region_1.2 | reduce | flops 786432 | bytes 2621442 | tf_op jit(solution)/shard_map/grad_input/reduce_sum | solution.py:46
  142.9 1.9 copy.17
  144.9 5.5 %all-to-all-start.3 = ((bf16[4,8,2,16,256]{4,3,2,1,0:T(8,128)(2,1)}), bf16[4,8,2,16,256]{4,3,2,1,0:T(8,128)(2,1)}, u32[]{:S(2)}, u32[]{:S(2)}) async-start(bf16[4,8,2,16,256]{4,3,2,1,0:T(8,128)(2,1)} %copy.17), calls=%async_computation.3 | async-start | bytes 1048576 | tf_op jit(solution)/shard_map/grad_input/all_to_all | solution.py:37
  150.4 2.8 %broadcast_select_fusion.1 = bf16[1024,512]{1,0:T(8,128)(2,1)} fusion(bf16[1024,512]{1,0:T(8,128)(2,1)} %collective-permute-done, pred[]{:T(512)S(6)} %eq.19, f16[1024,512]{1,0:T(8,128)(2,1)} %copy-done.1), kind=kLoop, calls=%fused_computation.15 | loop fusion | flops 2097152 | bytes 3145729 | tf_op jit(solution)/shard_map/factor_columns/jit(_where)/select_n | solution.py:98
  153.2 1.3 collective-permute-start.1
  154.5 2.6 %broadcast_select_fusion = bf16[1024,512]{1,0:T(8,128)(2,1)} fusion(bf16[1024,512]{1,0:T(8,128)(2,1)} %collective-permute-done.2, pred[]{:T(512)S(6)} %eq.20, bf16[1024,1024]{1,0:T(8,128)(2,1)S(1)} %multiply_convert_fusion, s32[]{:T(128)S(6)} %select_n.72), kind=kLoop, calls=%fused_computation.14 | loop fusion | flops 524288 | bytes 3145733 | tf_op jit(solution)/shard_map/act_columns/jit(_where)/select_n | solution.py:104
  157.1 8.7 %collective-permute-start.3 = (bf16[1024,512]{1,0:T(8,128)(2,1)}, bf16[1024,512]{1,0:T(8,128)(2,1)}, u32[]{:S(2)}, u32[]{:S(2)}) collective-permute-start(bf16[1024,512]{1,0:T(8,128)(2,1)} %broadcast_select_fusion), channel_id=1, source_target_pairs={{0,128},{128,0},{256,384},{384,256},{1,129},{129,1},{257,385},{385... | collective-permute-start | bytes 3145736 | tf_op jit(solution)/shard_map/act_columns/ppermute | solution.py:105
  165.8 23.0 %collective-permute-done.1 = bf16[1024,512]{1,0:T(8,128)(2,1)} collective-permute-done((bf16[1024,512]{1,0:T(8,128)(2,1)}, bf16[1024,512]{1,0:T(8,128)(2,1)}, u32[]{:S(2)}, u32[]{:S(2)}) %collective-permute-start.1) | collective-permute-done | bytes 1048608 | tf_op jit(solution)/shard_map/factor_columns/ppermute | solution.py:33
  188.9 2.3 %broadcast_select_fusion.2 = bf16[1024,512]{1,0:T(8,128)(2,1)} fusion(bf16[1024,512]{1,0:T(8,128)(2,1)} %broadcast_select_fusion.1, bf16[1024,512]{1,0:T(8,128)(2,1)} %collective-permute-done.1, pred[]{:T(512)S(6)} %eq.18), kind=kLoop, calls=%fused_computation.16 | loop fusion | flops 524288 | bytes 3145729 | tf_op jit(solution)/shard_map/factor_columns/jit(_where)/select_n | solution.py:100
  191.2 1.1 reduce_sum.47
  192.3 0.7 copy.18
  193.0 2.3 collective-permute-start.4
  195.3 8.2 %all-to-all-start.4 = ((bf16[4,128,128]{2,1,0:T(8,128)(2,1)}), bf16[4,128,128]{2,1,0:T(8,128)(2,1)S(1)}, u32[]{:S(2)}, u32[]{:S(2)}) async-start(bf16[4,128,128]{2,1,0:T(8,128)(2,1)} %bitcast.12), calls=%async_computation.4 | async-start | bytes 262144 | tf_op jit(solution)/shard_map/grad_input/all_to_all | solution.py:37
  203.4 4.1 %convolution_convert_fusion = bf16[1024,512]{1,0:T(8,128)(2,1)} fusion(f16[1024,512]{1,0:T(8,128)(2,1)} %copy-done.1, f16[1024,1024]{1,0:T(8,128)(2,1)} %copy-done.2), kind=kOutput, calls=%fused_computation.4 | convolution fusion | flops 1078984704 | bytes 4194304 | tf_op jit(solution)/shard_map/grad_weight/dot_general | solution.py:67
  207.5 2.3 %convolution_multiply_fusion.1 = f32[128,512]{1,0:T(8,128)} fusion(bf16[1024,512]{1,0:T(8,128)(2,1)} %broadcast_select_fusion, bf16[1024,512]{1,0:T(8,128)(2,1)} %collective-permute-done.3, pred[]{:T(512)S(6)} %eq.21, bf16[1024,1024]{1,0:T(8,128)(2,1)S(1)} %multiply_convert_fusion, s32[]{:T(128)S(6)} %select_n.74), kind=kOutput, calls=%fused_computation.7 | convolution fusion | flops 134807552 | bytes 2621445 | tf_op jit(solution)/shard_map/act_factor/dot_general | solution.py:67
  209.9 9.6 %all-to-all-done.4 = bf16[4,128,128]{2,1,0:T(8,128)(2,1)S(1)} async-done(((bf16[4,128,128]{2,1,0:T(8,128)(2,1)}), bf16[4,128,128]{2,1,0:T(8,128)(2,1)S(1)}, u32[]{:S(2)}, u32[]{:S(2)}) %all-to-all-start.4) | async-done | bytes 131104 | tf_op jit(solution)/shard_map/grad_input/all_to_all | solution.py:37
  219.4 0.6 reduce_sum.48
  220.1 3.3 %convolution_multiply_fusion = f32[512,512]{1,0:T(8,128)} fusion(bf16[1024,512]{1,0:T(8,128)(2,1)} %broadcast_select_fusion.2, bf16[1024,512]{1,0:T(8,128)(2,1)} %collective-permute-done.4, pred[]{:T(512)S(6)} %eq.22, f16[1024,512]{1,0:T(8,128)(2,1)} %copy-done.1), kind=kOutput, calls=%fused_computation.6 | convolution fusion | flops 539230208 | bytes 4194305 | tf_op jit(solution)/shard_map/grad_factor/dot_general | solution.py:67
  (14 shorter events, 0.1 us)
Async XLA Ops:
  7.2 1.3 copy-start
  9.9 41.7 %all-to-all-start = ((bf16[8,32,1024]{2,1,0:T(8,128)(2,1)}), bf16[8,32,1024]{2,1,0:T(8,128)(2,1)S(1)}, u32[]{:S(2)}, u32[]{:S(2)}) async-start(bf16[8,32,1024]{2,1,0:T(8,128)(2,1)} %broadcast_in_dim.2), calls=%async_computation | async-start | bytes 1048576 | tf_op jit(solution)/shard_map/gather_tokens/all_to_all | solution.py:37
  22.5 70.1 %all-gather.4.cloned.1.call-start = ((), (), s32[]{:S(2)}) async-start(), calls=%async_computation.5 | async-start | bytes 1179648 | tf_op jit(solution)/shard_map/grad_out_piece/all_gather | solution.py:79
  51.8 16.2 %copy-start.4 = (bf16[1024,512]{1,0:T(8,128)(2,1)S(1)}, bf16[1024,512]{1,0:T(8,128)(2,1)}, u32[]{:S(2)}) copy-start(bf16[1024,512]{1,0:T(8,128)(2,1)} %param.4) | copy-start | bytes 3145732
  68.0 2.2 copy-start.2
  70.2 19.5 %all-to-all-start.1 = ((f16[8,128,512]{2,1,0:T(8,128)(2,1)}), f16[8,128,512]{2,1,0:T(8,128)(2,1)S(1)}, u32[]{:S(2)}, u32[]{:S(2)}) async-start(f16[8,128,512]{2,1,0:T(8,128)(2,1)} %bitcast.27), calls=%async_computation.1 | async-start | bytes 2097152 | tf_op jit(solution)/shard_map/preact/all_to_all | solution.py:37
  76.3 31.2 %copy-start.5 = (bf16[4,2,128,512]{3,2,1,0:T(8,128)(2,1)S(1)}, bf16[4,2,128,512]{3,2,1,0:T(8,128)(2,1)}, u32[]{:S(2)}) copy-start(bf16[4,2,128,512]{3,2,1,0:T(8,128)(2,1)} %copy.16) | copy-start | bytes 3145732
  107.5 7.5 %copy-start.1 = (f16[1024,512]{1,0:T(8,128)(2,1)}, f16[1024,512]{1,0:T(8,128)(2,1)S(1)}, u32[]{:S(2)}) copy-start(f16[1024,512]{1,0:T(8,128)(2,1)S(1)} %all-gather.6) | copy-start | bytes 3145732
  110.1 30.0 %all-to-all-start.2 = ((bf16[4,1024,256]{2,1,0:T(8,128)(2,1)}), bf16[4,1024,256]{2,1,0:T(8,128)(2,1)}, u32[]{:S(2)}, u32[]{:S(2)}) async-start(bf16[4,1024,256]{2,1,0:T(8,128)(2,1)} %convert_bitcast_fusion), calls=%async_computation.2 | async-start | bytes 4194304 | tf_op jit(solution)/shard_map/grad_input/all_to_all | solution.py:37
  115.1 2.9 %copy-start.3 = (f16[1024,1024]{1,0:T(8,128)(2,1)S(1)}, f16[1024,1024]{1,0:T(8,128)(2,1)}, u32[]{:S(2)}) copy-start(f16[1024,1024]{1,0:T(8,128)(2,1)} %copy-done.2) | copy-start | bytes 6291460
  116.2 5.3 %collective-permute-start = (bf16[1024,512]{1,0:T(8,128)(2,1)}, bf16[1024,512]{1,0:T(8,128)(2,1)}, u32[]{:S(2)}, u32[]{:S(2)}) collective-permute-start(bf16[1024,512]{1,0:T(8,128)(2,1)} %multiply_convert_fusion.1), channel_id=1, source_target_pairs={{0,4},{65,69},{130,134},{195,199},{260,256},{325,321},{390,386},{4... | collective-permute-start | bytes 3145736 | tf_op jit(solution)/shard_map/factor_columns/ppermute | solution.py:33
  119.6 34.9 %collective-permute-start.2 = (bf16[1024,512]{1,0:T(8,128)(2,1)}, bf16[1024,512]{1,0:T(8,128)(2,1)}, u32[]{:S(2)}, u32[]{:S(2)}) collective-permute-start(bf16[1024,512]{1,0:T(8,128)(2,1)} %constant_dynamic-slice_fusion), channel_id=1, source_target_pairs={{0,64},{64,0},{1,65},{65,1},{2,66},{66,2},{3,67},{67,3},{4,68},{68... | collective-permute-start | bytes 3145736 | tf_op jit(solution)/shard_map/act_columns/ppermute | solution.py:28
  144.9 46.3 %all-to-all-start.3 = ((bf16[4,8,2,16,256]{4,3,2,1,0:T(8,128)(2,1)}), bf16[4,8,2,16,256]{4,3,2,1,0:T(8,128)(2,1)}, u32[]{:S(2)}, u32[]{:S(2)}) async-start(bf16[4,8,2,16,256]{4,3,2,1,0:T(8,128)(2,1)} %copy.17), calls=%async_computation.3 | async-start | bytes 1048576 | tf_op jit(solution)/shard_map/grad_input/all_to_all | solution.py:37
  153.2 35.7 %collective-permute-start.1 = (bf16[1024,512]{1,0:T(8,128)(2,1)}, bf16[1024,512]{1,0:T(8,128)(2,1)}, u32[]{:S(2)}, u32[]{:S(2)}) collective-permute-start(bf16[1024,512]{1,0:T(8,128)(2,1)} %broadcast_select_fusion.1), channel_id=1, source_target_pairs={{0,2},{4,6},{65,67},{69,71},{130,128},{134,132},{195,193},{199,197... | collective-permute-start | bytes 3145736 | tf_op jit(solution)/shard_map/factor_columns/ppermute | solution.py:33
  157.1 35.9 %collective-permute-start.3 = (bf16[1024,512]{1,0:T(8,128)(2,1)}, bf16[1024,512]{1,0:T(8,128)(2,1)}, u32[]{:S(2)}, u32[]{:S(2)}) collective-permute-start(bf16[1024,512]{1,0:T(8,128)(2,1)} %broadcast_select_fusion), channel_id=1, source_target_pairs={{0,128},{128,0},{256,384},{384,256},{1,129},{129,1},{257,385},{385... | collective-permute-start | bytes 3145736 | tf_op jit(solution)/shard_map/act_columns/ppermute | solution.py:105
  193.0 27.1 %collective-permute-start.4 = (bf16[1024,512]{1,0:T(8,128)(2,1)}, bf16[1024,512]{1,0:T(8,128)(2,1)}, u32[]{:S(2)}, u32[]{:S(2)}) collective-permute-start(bf16[1024,512]{1,0:T(8,128)(2,1)} %broadcast_select_fusion.2), channel_id=1, source_target_pairs={{0,1},{2,3},{4,5},{6,7},{65,64},{67,66},{69,68},{71,70},{130,131},... | collective-permute-start | bytes 3145736 | tf_op jit(solution)/shard_map/grad_factor/ppermute | solution.py:33
  195.3 24.2 %all-to-all-start.4 = ((bf16[4,128,128]{2,1,0:T(8,128)(2,1)}), bf16[4,128,128]{2,1,0:T(8,128)(2,1)S(1)}, u32[]{:S(2)}, u32[]{:S(2)}) async-start(bf16[4,128,128]{2,1,0:T(8,128)(2,1)} %bitcast.12), calls=%async_computation.4 | async-start | bytes 262144 | tf_op jit(solution)/shard_map/grad_input/all_to_all | solution.py:37
Sparse Core Ops, SparseCore 0:
  26.0 66.5 all-gather.3

commit v5 on v4

--- a/solution.py
+++ b/solution.py
@@ -79,13 +79,20 @@
         grad_out_rows = lax.all_gather(own_grad, TOK, axis=0, tiled=True)
 
     with jax.named_scope("gather_tokens"):
-        near = spread(own, TOK).reshape(8, 2, 16, 1024)
-        near = near.transpose(1, 0, 2, 3).reshape(256, 1024)
+        other = swap(own, "th")
+        near = jnp.where(th == 0, jnp.stack([own, other]), jnp.stack([other, own]))
+        near = spread(near, "tl").reshape(4, 2, 2, 16, 1024).transpose(2, 1, 0, 3, 4)
+        near = near.reshape(256, 1024)
         tokens = unscaled(gather_scaled(near, "x", TOKEN_SCALE), TOKEN_SCALE)
 
     with jax.named_scope("preact"):
         partial = jnp.dot(tokens, weight, preferred_element_type=F32).astype(F16)
-        preact = total(exchange(partial.reshape(8, 128, 512), IN))
+        act_cols = cols_of(tokens, x % 2 * 512, 512)
+        act_other = swap(act_cols, "core")
+        parts, act_other = lax.optimization_barrier(
+            (exchange(partial.reshape(8, 128, 512), IN), act_other)
+        )
+        preact = total(parts)
         grad_out_piece = cols_of(grad_out_rows, tok * 512, 512)
         grad_piece = (grad_out_piece.astype(F32) * gelu_slope(preact)).astype(BF16)
 
@@ -97,27 +104,27 @@
         far = send_along(grad_rows, 4, (0,))
         cross = jnp.where(away == 0, grad_rows, far)
         mid = send_along(cross, 2, (0, 4))
-        cross = jnp.where(away & 2 == 0, cross, mid)
 
     with jax.named_scope("act_columns"):
-        act_cols = cols_of(tokens, x % 2 * 512, 512)
-        act_cols = jnp.where(core == x // 2, act_cols, swap(act_cols, "core"))
+        act_cols = jnp.where(core == x // 2, act_cols, act_other)
         from_y = lax.ppermute(act_cols, "y", [(0, 1), (1, 0), (2, 3), (3, 2)])
 
     with jax.named_scope("grad_input"):
         by_x = weight.reshape(2, 4, 128, 512).transpose(1, 0, 2, 3).reshape(4, 256, 512)
         share = jnp.einsum("rc,kfc->krf", grad_rows, by_x, preferred_element_type=F32).astype(BF16)
-        part, far = lax.optimization_barrier((exchange(share, "x"), far))
-        part = total(part).astype(BF16).reshape(8, 2, 4, 16, 256).transpose(2, 0, 1, 3, 4)
-        part = total(exchange(part, "tl")).astype(BF16)
-        part = part.reshape(8, 2, 16, 2, 128).transpose(3, 1, 0, 2, 4).reshape(4, 128, 128)
-        part, cross, from_y = lax.optimization_barrier((part, cross, from_y))
-        grad_input = total(exchange(part, ("zh", "th"))).astype(BF16)
+        part, far, from_y = lax.optimization_barrier((exchange(share, "x"), far, from_y))
+        part = total(part).astype(BF16).reshape(8, 8, 16, 256).transpose(1, 0, 2, 3)
+        part, mid = lax.optimization_barrier((exchange(part, TOK), mid))
+        part = total(part).reshape(128, 256)
+        keep = jnp.where(zh == 0, part[:, :128], part[:, 128:])
+        send = jnp.where(zh == 0, part[:, 128:], part[:, :128]).astype(BF16)
+        grad_input = (keep + swap(send, "zh").astype(F32)).astype(BF16)
 
     with jax.named_scope("grad_weight"):
         grad_weight = tn_dot(tokens, grad_rows).astype(BF16)
 
     with jax.named_scope("grad_factor"):
+        cross = jnp.where(away & 2 == 0, cross, mid)
         near = send_along(cross, 1, (0, 2, 4, 6))
         cross = jnp.where(away & 1 == 0, cross, near)
         grad_factor = tn_dot(grad_rows, cross) / 1024.0

time: 231 us -> 248 us (1.074)
  the two profiles are of different devices: /device:TPU:14 before, /device:TPU:10 now
where the time goes in v5:
time: 248 us; the launch traced here: 247 us
  waiting for transfers between devices  115 us (46%)
  starting transfers between devices  46.1 us (19%)
  blocking collectives  34.3 us (14%)
  between operations  14.3 us (6%)
  other arithmetic  14 us (6%)
  matrix products  12.5 us (5%)
  local copies, waits for them, and re-layouts  10.9 us (4%)
    ppermute x3, waiting for transfers between devices, send_along(): return lax.ppermute(value, IN + TOK, pairs)  39.3 us
    all_gather x2, blocking collectives, gather_scaled(): return lax.all_gather(scaled, axis, axis=0, tiled=True)  34.3 us
    all_to_all x4, waiting for transfers between devices, exchange(): return lax.all_to_all(value, axis, split_axis=0, concat_axis=0, tiled=True)  26.2 us
    ppermute x1, waiting for transfers between devices, on_device(): from_y = lax.ppermute(act_cols, 'y', [(0, 1), (1, 0), (2, 3), (3, 2)])  24.4 us
    ppermute x3, starting transfers between devices, swap(): return lax.ppermute(value, axis, [(0, 1), (1, 0)])  20.5 us
    all_to_all x4, starting transfers between devices, exchange(): return lax.all_to_all(value, axis, split_axis=0, concat_axis=0, tiled=True)  17.8 us
    ppermute x3, waiting for transfers between devices, swap(): return lax.ppermute(value, axis, [(0, 1), (1, 0)])  12.2 us
    all_gather x1, waiting for transfers between devices, on_device(): grad_out_rows = lax.all_gather(own_grad, TOK, axis=0, tiled=True)  12.1 us
  transfers between devices with their start and end apart: 12, of which 7 were waited for; matrix products, arithmetic and copies ran while one was open for 8% of the time, Pallas kernels for 0%

profile of v5, /device:TPU:10, one launch (start us, length us, event | category | flops | bytes accessed | tf_op | source)
XLA Modules:
  0.0 246.9 jit_solution(7594218027552053776)
XLA Ops:
  7.2 0.0 copy-start
  7.2 1.2 copy-done
  8.4 0.7 constant_dynamic-slice_fusion.2
  9.1 0.8 constant_dynamic-slice_fusion.1
  9.9 9.1 %collective-permute-start = (bf16[32,1024]{1,0:T(8,128)(2,1)S(1)}, bf16[32,1024]{1,0:T(8,128)(2,1)S(1)}, u32[]{:S(2)}, u32[]{:S(2)}) collective-permute-start(bf16[32,1024]{1,0:T(8,128)(2,1)S(1)} %constant_dynamic-slice_fusion.1), channel_id=1, source_target_pairs={{0,4},{4,0},{1,5},{5,1},{2,6},{6,2},{3,7},{7,3},{8,12},{12,8},{9,1... | collective-permute-start | bytes 196616 | tf_op jit(solution)/shard_map/gather_tokens/ppermute | solution.py:28
  19.0 6.4 %collective-permute-done = bf16[32,1024]{1,0:T(8,128)(2,1)S(1)} collective-permute-done((bf16[32,1024]{1,0:T(8,128)(2,1)S(1)}, bf16[32,1024]{1,0:T(8,128)(2,1)S(1)}, u32[]{:S(2)}, u32[]{:S(2)}) %collective-permute-start) | collective-permute-done | bytes 65568 | tf_op jit(solution)/shard_map/gather_tokens/ppermute | solution.py:28
  25.5 0.9 broadcast_in_dim.2
  26.3 3.6 %all-to-all-start = ((bf16[4,2,32,1024]{3,2,1,0:T(8,128)(2,1)}), bf16[4,2,32,1024]{3,2,1,0:T(8,128)(2,1)S(1)}, u32[]{:S(2)}, u32[]{:S(2)}) async-start(bf16[4,2,32,1024]{3,2,1,0:T(8,128)(2,1)} %broadcast_in_dim.2), calls=%async_computation | async-start | bytes 1048576 | tf_op jit(solution)/shard_map/gather_tokens/all_to_all | solution.py:37
  29.9 0.7 all-gather.4.cloned.1.call-update
  30.7 13.8 %all-to-all-done = bf16[4,2,32,1024]{3,2,1,0:T(8,128)(2,1)S(1)} async-done(((bf16[4,2,32,1024]{3,2,1,0:T(8,128)(2,1)}), bf16[4,2,32,1024]{3,2,1,0:T(8,128)(2,1)S(1)}, u32[]{:S(2)}, u32[]{:S(2)}) %all-to-all-start) | async-done | bytes 524320 | tf_op jit(solution)/shard_map/gather_tokens/all_to_all | solution.py:37
  44.5 0.1 multiply_convert_fusion.2
  44.6 0.1 copy.13
  44.7 20.4 %all-gather.5 = f16[1024,1024]{1,0:T(8,128)(2,1)S(1)} all-gather(f16[256,1024]{1,0:T(8,128)(2,1)S(1)} %bitcast.22), channel_id=1, replica_groups=mesh['y'=4,'core'=2,'zh'=2,'x'=4,'th'=2,'tl'=4] {'x'}, dimensions={0}, use_global_device_ids=true | all-gather | bytes 2621440 | tf_op jit(solution)/shard_map/gather_tokens/all_gather | solution.py:59
  65.1 0.6 multiply_convert_fusion
  65.8 1.1 constant_dynamic-slice_fusion
  66.9 1.9 collective-permute-start.1
  68.8 2.2 convolution_convert_fusion.1
  71.0 5.0 %all-to-all-start.1 = ((f16[8,128,512]{2,1,0:T(8,128)(2,1)}), f16[8,128,512]{2,1,0:T(8,128)(2,1)}, u32[]{:S(2)}, u32[]{:S(2)}) async-start(f16[8,128,512]{2,1,0:T(8,128)(2,1)} %bitcast.27), calls=%async_computation.1 | async-start | bytes 2097152 | tf_op jit(solution)/shard_map/preact/all_to_all | solution.py:37
  76.1 2.3 copy.14
  78.3 12.4 %all-to-all-done.1 = f16[8,128,512]{2,1,0:T(8,128)(2,1)} async-done(((f16[8,128,512]{2,1,0:T(8,128)(2,1)}), f16[8,128,512]{2,1,0:T(8,128)(2,1)}, u32[]{:S(2)}, u32[]{:S(2)}) %all-to-all-start.1) | async-done | bytes 1048608 | tf_op jit(solution)/shard_map/preact/all_to_all | solution.py:37
  90.7 1.4 convert_reduce_fusion
  92.1 12.1 %all-gather.4.cloned.1.call-done = bf16[128,4096]{1,0:T(8,128)(2,1)} async-done(((bf16[16,4096]{1,0:T(8,128)(2,1)}), bf16[128,4096]{1,0:T(8,128)(2,1)}) %all-gather.4.cloned.1.call-update) | async-done | bytes 1048592 | tf_op jit(solution)/shard_map/grad_out_piece/all_gather | solution.py:79
  104.2 1.1 multiply_convert_fusion.3
  105.3 13.9 %all-gather.6 = f16[1024,512]{1,0:T(8,128)(2,1)S(1)} all-gather(f16[128,512]{1,0:T(8,128)(2,1)S(1)} %multiply_convert_fusion.3), channel_id=1, replica_groups=mesh['y'=4,'core'=2,'zh'=2,'x'=4,'th'=2,'tl'=4] {'y','core'}, dimensions={0}, use_global_device_ids=true | all-gather | bytes 1179648 | tf_op jit(solution)/shard_map/gather_grad/all_gather | solution.py:59
  119.2 1.0 copy-done.1
  120.1 3.9 %convert_bitcast_fusion = bf16[4,1024,256]{2,1,0:T(8,128)(2,1)} fusion(bf16[4,256,512]{2,1,0:T(8,128)(2,1)} %bitcast.26, f16[1024,512]{1,0:T(8,128)(2,1)S(1)} %all-gather.6), kind=kOutput, calls=%fused_computation.1 | convolution fusion | flops 1076363264 | bytes 4194304 | tf_op jit(solution)/shard_map/grad_input/rc,kfc->krf/dot_general | solution.py:114
  124.0 5.0 %all-to-all-start.2 = ((bf16[4,1024,256]{2,1,0:T(8,128)(2,1)}), bf16[4,1024,256]{2,1,0:T(8,128)(2,1)}, u32[]{:S(2)}, u32[]{:S(2)}) async-start(bf16[4,1024,256]{2,1,0:T(8,128)(2,1)} %convert_bitcast_fusion), calls=%async_computation.2 | async-start | bytes 4194304 | tf_op jit(solution)/shard_map/grad_input/all_to_all | solution.py:37
  129.0 1.4 multiply_convert_fusion.1
  130.4 1.7 collective-permute-start.2
  132.1 0.4 broadcast_select_fusion.2
  132.6 1.0 copy-done.5
  133.5 3.3 %collective-permute-start.3 = (bf16[1024,512]{1,0:T(8,128)(2,1)S(1)}, bf16[1024,512]{1,0:T(8,128)(2,1)}, u32[]{:S(2)}, u32[]{:S(2)}) collective-permute-start(bf16[1024,512]{1,0:T(8,128)(2,1)S(1)} %broadcast_select_fusion.2), channel_id=1, source_target_pairs={{0,128},{128,0},{256,384},{384,256},{1,129},{129,1},{257,385},{385... | collective-permute-start | bytes 3145736 | tf_op jit(solution)/shard_map/act_columns/ppermute | solution.py:110
  136.8 24.4 %collective-permute-done.3 = bf16[1024,512]{1,0:T(8,128)(2,1)} collective-permute-done((bf16[1024,512]{1,0:T(8,128)(2,1)S(1)}, bf16[1024,512]{1,0:T(8,128)(2,1)}, u32[]{:S(2)}, u32[]{:S(2)}) %collective-permute-start.3) | collective-permute-done | bytes 1048608 | tf_op jit(solution)/shard_map/act_columns/ppermute | solution.py:110
  161.2 2.8 %reduce_sum.31 = bf16[1024,256]{1,0:T(8,128)(2,1)} reduce(bf16[4,1024,256]{2,1,0:T(8,128)(2,1)} %all-to-all-done.2, bf16[]{:T(256)} %constant.93.clone.1), dimensions={0}, to_apply=%region_1.2 | reduce | flops 786432 | bytes 2621442 | tf_op jit(solution)/shard_map/grad_input/reduce_sum | solution.py:46
  164.1 1.9 copy.15
  166.0 4.1 %all-to-all-start.3 = ((bf16[8,8,16,256]{3,2,1,0:T(8,128)(2,1)}), bf16[8,8,16,256]{3,2,1,0:T(8,128)(2,1)}, u32[]{:S(2)}, u32[]{:S(2)}) async-start(bf16[8,8,16,256]{3,2,1,0:T(8,128)(2,1)} %copy.15), calls=%async_computation.3 | async-start | bytes 1048576 | tf_op jit(solution)/shard_map/grad_input/all_to_all | solution.py:37
  170.1 2.8 %broadcast_select_fusion.1 = bf16[1024,512]{1,0:T(8,128)(2,1)} fusion(bf16[1024,512]{1,0:T(8,128)(2,1)} %collective-permute-done.2, pred[]{:T(512)S(6)} %eq.28, f16[1024,512]{1,0:T(8,128)(2,1)} %copy-done.1), kind=kLoop, calls=%fused_computation.16 | loop fusion | flops 2097152 | bytes 3145729 | tf_op jit(solution)/shard_map/factor_columns/jit(_where)/select_n | solution.py:105
  172.9 1.3 collective-permute-start.4
  174.3 39.3 %collective-permute-done.4 = bf16[1024,512]{1,0:T(8,128)(2,1)} collective-permute-done((bf16[1024,512]{1,0:T(8,128)(2,1)}, bf16[1024,512]{1,0:T(8,128)(2,1)}, u32[]{:S(2)}, u32[]{:S(2)}) %collective-permute-start.4) | collective-permute-done | bytes 1048608 | tf_op jit(solution)/shard_map/factor_columns/ppermute | solution.py:33
  213.6 1.5 broadcast_select_fusion
  215.1 1.5 collective-permute-start.6
  216.6 2.3 convolution_convert_fusion
  218.9 1.1 convert_reduce_fusion.1
  220.0 9.5 %collective-permute-start.5 = (bf16[128,128]{1,0:T(8,128)(2,1)S(1)}, bf16[128,128]{1,0:T(8,128)(2,1)S(1)}, u32[]{:S(2)}, u32[]{:S(2)}) collective-permute-start(bf16[128,128]{1,0:T(8,128)(2,1)S(1)} %select_convert_fusion), channel_id=1, source_target_pairs={{0,32},{32,0},{1,33},{33,1},{2,34},{34,2},{3,35},{35,3},{4,36},{36... | collective-permute-start | bytes 98312 | tf_op jit(solution)/shard_map/grad_input/ppermute | solution.py:28
  229.6 2.4 convolution_multiply_fusion.1
  231.9 5.8 %collective-permute-done.5 = bf16[128,128]{1,0:T(8,128)(2,1)S(1)} collective-permute-done((bf16[128,128]{1,0:T(8,128)(2,1)S(1)}, bf16[128,128]{1,0:T(8,128)(2,1)S(1)}, u32[]{:S(2)}, u32[]{:S(2)}) %collective-permute-start.5) | collective-permute-done | bytes 32800 | tf_op jit(solution)/shard_map/grad_input/ppermute | solution.py:28
  237.7 0.6 add_convert_fusion
  238.3 1.7 convolution_multiply_fusion
  (20 shorter events, 0.1 us)
Async XLA Ops:
  7.2 1.2 copy-start
  9.9 15.5 %collective-permute-start = (bf16[32,1024]{1,0:T(8,128)(2,1)S(1)}, bf16[32,1024]{1,0:T(8,128)(2,1)S(1)}, u32[]{:S(2)}, u32[]{:S(2)}) collective-permute-start(bf16[32,1024]{1,0:T(8,128)(2,1)S(1)} %constant_dynamic-slice_fusion.1), channel_id=1, source_target_pairs={{0,4},{4,0},{1,5},{5,1},{2,6},{6,2},{3,7},{7,3},{8,12},{12,8},{9,1... | collective-permute-start | bytes 196616 | tf_op jit(solution)/shard_map/gather_tokens/ppermute | solution.py:28
  26.3 18.2 %all-to-all-start = ((bf16[4,2,32,1024]{3,2,1,0:T(8,128)(2,1)}), bf16[4,2,32,1024]{3,2,1,0:T(8,128)(2,1)S(1)}, u32[]{:S(2)}, u32[]{:S(2)}) async-start(bf16[4,2,32,1024]{3,2,1,0:T(8,128)(2,1)} %broadcast_in_dim.2), calls=%async_computation | async-start | bytes 1048576 | tf_op jit(solution)/shard_map/gather_tokens/all_to_all | solution.py:37
  29.9 74.2 %all-gather.4.cloned.1.call-start = ((), (), s32[]{:S(2)}) async-start(), calls=%async_computation.4 | async-start | bytes 1179648 | tf_op jit(solution)/shard_map/grad_out_piece/all_gather | solution.py:79
  65.1 3.7 %copy-start.3 = (f16[1024,1024]{1,0:T(8,128)(2,1)}, f16[1024,1024]{1,0:T(8,128)(2,1)S(1)}, u32[]{:S(2)}) copy-start(f16[1024,1024]{1,0:T(8,128)(2,1)S(1)} %all-gather.5) | copy-start | bytes 6291460
  65.7 3.1 %copy-start.7 = (bf16[1024,512]{1,0:T(8,128)(2,1)S(1)}, bf16[1024,512]{1,0:T(8,128)(2,1)}, u32[]{:S(2)}) copy-start(bf16[1024,512]{1,0:T(8,128)(2,1)} %param.4) | copy-start | bytes 3145732
  66.9 23.8 %collective-permute-start.1 = (bf16[1024,512]{1,0:T(8,128)(2,1)}, bf16[1024,512]{1,0:T(8,128)(2,1)}, u32[]{:S(2)}, u32[]{:S(2)}) collective-permute-start(bf16[1024,512]{1,0:T(8,128)(2,1)} %constant_dynamic-slice_fusion), channel_id=1, source_target_pairs={{0,64},{64,0},{1,65},{65,1},{2,66},{66,2},{3,67},{67,3},{4,68},{68... | collective-permute-start | bytes 3145736 | tf_op jit(solution)/shard_map/preact/ppermute | solution.py:28
  71.0 19.6 %all-to-all-start.1 = ((f16[8,128,512]{2,1,0:T(8,128)(2,1)}), f16[8,128,512]{2,1,0:T(8,128)(2,1)}, u32[]{:S(2)}, u32[]{:S(2)}) async-start(f16[8,128,512]{2,1,0:T(8,128)(2,1)} %bitcast.27), calls=%async_computation.1 | async-start | bytes 2097152 | tf_op jit(solution)/shard_map/preact/all_to_all | solution.py:37
  119.1 1.0 copy-start.1
  124.0 37.3 %all-to-all-start.2 = ((bf16[4,1024,256]{2,1,0:T(8,128)(2,1)}), bf16[4,1024,256]{2,1,0:T(8,128)(2,1)}, u32[]{:S(2)}, u32[]{:S(2)}) async-start(bf16[4,1024,256]{2,1,0:T(8,128)(2,1)} %convert_bitcast_fusion), calls=%async_computation.2 | async-start | bytes 4194304 | tf_op jit(solution)/shard_map/grad_input/all_to_all | solution.py:37
  130.4 6.4 %collective-permute-start.2 = (bf16[1024,512]{1,0:T(8,128)(2,1)S(1)}, bf16[1024,512]{1,0:T(8,128)(2,1)}, u32[]{:S(2)}, u32[]{:S(2)}) collective-permute-start(bf16[1024,512]{1,0:T(8,128)(2,1)S(1)} %multiply_convert_fusion.1), channel_id=1, source_target_pairs={{0,4},{65,69},{130,134},{195,199},{260,256},{325,321},{390,386},{4... | collective-permute-start | bytes 3145736 | tf_op jit(solution)/shard_map/factor_columns/ppermute | solution.py:33
  132.6 1.0 copy-start.5
  133.5 27.7 %collective-permute-start.3 = (bf16[1024,512]{1,0:T(8,128)(2,1)S(1)}, bf16[1024,512]{1,0:T(8,128)(2,1)}, u32[]{:S(2)}, u32[]{:S(2)}) collective-permute-start(bf16[1024,512]{1,0:T(8,128)(2,1)S(1)} %broadcast_select_fusion.2), channel_id=1, source_target_pairs={{0,128},{128,0},{256,384},{384,256},{1,129},{129,1},{257,385},{385... | collective-permute-start | bytes 3145736 | tf_op jit(solution)/shard_map/act_columns/ppermute | solution.py:110
  166.0 47.6 %all-to-all-start.3 = ((bf16[8,8,16,256]{3,2,1,0:T(8,128)(2,1)}), bf16[8,8,16,256]{3,2,1,0:T(8,128)(2,1)}, u32[]{:S(2)}, u32[]{:S(2)}) async-start(bf16[8,8,16,256]{3,2,1,0:T(8,128)(2,1)} %copy.15), calls=%async_computation.3 | async-start | bytes 1048576 | tf_op jit(solution)/shard_map/grad_input/all_to_all | solution.py:37
  172.9 40.6 %collective-permute-start.4 = (bf16[1024,512]{1,0:T(8,128)(2,1)}, bf16[1024,512]{1,0:T(8,128)(2,1)}, u32[]{:S(2)}, u32[]{:S(2)}) collective-permute-start(bf16[1024,512]{1,0:T(8,128)(2,1)} %broadcast_select_fusion.1), channel_id=1, source_target_pairs={{0,2},{4,6},{65,67},{69,71},{130,128},{134,132},{195,193},{199,197... | collective-permute-start | bytes 3145736 | tf_op jit(solution)/shard_map/factor_columns/ppermute | solution.py:33
  213.6 3.0 %copy-start.2 = (f16[1024,512]{1,0:T(8,128)(2,1)S(1)}, f16[1024,512]{1,0:T(8,128)(2,1)}, u32[]{:S(2)}) copy-start(f16[1024,512]{1,0:T(8,128)(2,1)} %copy-done.1) | copy-start | bytes 3145732
  213.6 3.0 %copy-start.4 = (f16[1024,1024]{1,0:T(8,128)(2,1)S(1)}, f16[1024,1024]{1,0:T(8,128)(2,1)}, u32[]{:S(2)}) copy-start(f16[1024,1024]{1,0:T(8,128)(2,1)} %copy-done.3) | copy-start | bytes 6291460
  215.1 14.5 %copy-start.6 = (bf16[1024,512]{1,0:T(8,128)(2,1)S(1)}, bf16[1024,512]{1,0:T(8,128)(2,1)}, u32[]{:S(2)}) copy-start(bf16[1024,512]{1,0:T(8,128)(2,1)} %copy-done.5) | copy-start | bytes 3145732
  215.1 23.2 %collective-permute-start.6 = (bf16[1024,512]{1,0:T(8,128)(2,1)S(1)}, bf16[1024,512]{1,0:T(8,128)(2,1)S(1)}, u32[]{:S(2)}, u32[]{:S(2)}) collective-permute-start(bf16[1024,512]{1,0:T(8,128)(2,1)S(1)} %broadcast_select_fusion), channel_id=1, source_target_pairs={{0,1},{2,3},{4,5},{6,7},{65,64},{67,66},{69,68},{71,70},{130,131},... | collective-permute-start | bytes 3145736 | tf_op jit(solution)/shard_map/grad_factor/ppermute | solution.py:33
  220.0 17.7 %collective-permute-start.5 = (bf16[128,128]{1,0:T(8,128)(2,1)S(1)}, bf16[128,128]{1,0:T(8,128)(2,1)S(1)}, u32[]{:S(2)}, u32[]{:S(2)}) collective-permute-start(bf16[128,128]{1,0:T(8,128)(2,1)S(1)} %select_convert_fusion), channel_id=1, source_target_pairs={{0,32},{32,0},{1,33},{33,1},{2,34},{34,2},{3,35},{35,3},{4,36},{36... | collective-permute-start | bytes 98312 | tf_op jit(solution)/shard_map/grad_input/ppermute | solution.py:28
Sparse Core Ops, SparseCore 0:
  33.4 70.6 all-gather.3

commit v6 on v4

--- a/solution.py
+++ b/solution.py
@@ -85,7 +85,12 @@
 
     with jax.named_scope("preact"):
         partial = jnp.dot(tokens, weight, preferred_element_type=F32).astype(F16)
-        preact = total(exchange(partial.reshape(8, 128, 512), IN))
+        act_cols = cols_of(tokens, x % 2 * 512, 512)
+        act_other = swap(act_cols, "core")
+        parts, act_other = lax.optimization_barrier(
+            (exchange(partial.reshape(8, 128, 512), IN), act_other)
+        )
+        preact = total(parts)
         grad_out_piece = cols_of(grad_out_rows, tok * 512, 512)
         grad_piece = (grad_out_piece.astype(F32) * gelu_slope(preact)).astype(BF16)
 
@@ -96,28 +101,27 @@
         away = tok ^ piece
         far = send_along(grad_rows, 4, (0,))
         cross = jnp.where(away == 0, grad_rows, far)
-        mid = send_along(cross, 2, (0, 4))
-        cross = jnp.where(away & 2 == 0, cross, mid)
 
     with jax.named_scope("act_columns"):
-        act_cols = cols_of(tokens, x % 2 * 512, 512)
-        act_cols = jnp.where(core == x // 2, act_cols, swap(act_cols, "core"))
+        act_cols = jnp.where(core == x // 2, act_cols, act_other)
         from_y = lax.ppermute(act_cols, "y", [(0, 1), (1, 0), (2, 3), (3, 2)])
 
     with jax.named_scope("grad_input"):
         by_x = weight.reshape(2, 4, 128, 512).transpose(1, 0, 2, 3).reshape(4, 256, 512)
         share = jnp.einsum("rc,kfc->krf", grad_rows, by_x, preferred_element_type=F32).astype(BF16)
-        part, far = lax.optimization_barrier((exchange(share, "x"), far))
+        part, cross = lax.optimization_barrier((exchange(share, "x"), cross))
+        mid = send_along(cross, 2, (0, 4))
         part = total(part).astype(BF16).reshape(8, 2, 4, 16, 256).transpose(2, 0, 1, 3, 4)
-        part = total(exchange(part, "tl")).astype(BF16)
+        part, from_y, mid = lax.optimization_barrier((exchange(part, "tl"), from_y, mid))
+        part = total(part).astype(BF16)
         part = part.reshape(8, 2, 16, 2, 128).transpose(3, 1, 0, 2, 4).reshape(4, 128, 128)
-        part, cross, from_y = lax.optimization_barrier((part, cross, from_y))
         grad_input = total(exchange(part, ("zh", "th"))).astype(BF16)
 
     with jax.named_scope("grad_weight"):
         grad_weight = tn_dot(tokens, grad_rows).astype(BF16)
 
     with jax.named_scope("grad_factor"):
+        cross = jnp.where(away & 2 == 0, cross, mid)
         near = send_along(cross, 1, (0, 2, 4, 6))
         cross = jnp.where(away & 1 == 0, cross, near)
         grad_factor = tn_dot(grad_rows, cross) / 1024.0

time: 231 us -> 239 us (1.035)
  the two profiles are of different devices: /device:TPU:14 before, /device:TPU:8 now
where the time goes in v6:
time: 239 us; the launch traced here: 238 us
  waiting for transfers between devices  101 us (42%)
  starting transfers between devices  50.6 us (21%)
  blocking collectives  29.4 us (12%)
  other arithmetic  16.7 us (7%)
  matrix products  15.8 us (7%)
  between operations  14.2 us (6%)
  local copies, waits for them, and re-layouts  9.84 us (4%)
    all_to_all x5, waiting for transfers between devices, exchange(): return lax.all_to_all(value, axis, split_axis=0, concat_axis=0, tiled=True)  68.8 us
    all_to_all x5, starting transfers between devices, exchange(): return lax.all_to_all(value, axis, split_axis=0, concat_axis=0, tiled=True)  39.2 us
    all_gather x2, blocking collectives, gather_scaled(): return lax.all_gather(scaled, axis, axis=0, tiled=True)  29.4 us
    ppermute x1, waiting for transfers between devices, on_device(): from_y = lax.ppermute(act_cols, 'y', [(0, 1), (1, 0), (2, 3), (3, 2)])  17.5 us
    ppermute x3, waiting for transfers between devices, send_along(): return lax.ppermute(value, IN + TOK, pairs)  14.4 us
    dot_general x3, matrix products, tn_dot(): lax.dot_general(left, right, (((0,), (0,)), ((), ())), preferred_element_...  9.71 us
    reduce_sum x4, other arithmetic, total(): return jnp.sum(parts.astype(F32), axis=0)  5.99 us
    ppermute x3, starting transfers between devices, send_along(): return lax.ppermute(value, IN + TOK, pairs)  5.26 us
  transfers between devices with their start and end apart: 11, of which 6 were waited for; matrix products, arithmetic and copies ran while one was open for 10% of the time, Pallas kernels for 0%

profile of v6, /device:TPU:8, one launch (start us, length us, event | category | flops | bytes accessed | tf_op | source)
XLA Modules:
  0.0 238.0 jit_solution(8583061408321583127)
XLA Ops:
  7.2 0.0 copy-start
  7.2 0.9 constant_dynamic-slice_fusion.1
  8.1 0.3 copy-done
  8.4 0.7 constant_dynamic-slice_fusion.2
  9.1 0.9 broadcast_in_dim.2
  9.9 12.5 %all-to-all-start = ((bf16[8,32,1024]{2,1,0:T(8,128)(2,1)}), bf16[8,32,1024]{2,1,0:T(8,128)(2,1)S(1)}, u32[]{:S(2)}, u32[]{:S(2)}) async-start(bf16[8,32,1024]{2,1,0:T(8,128)(2,1)} %broadcast_in_dim.2), calls=%async_computation | async-start | bytes 1048576 | tf_op jit(solution)/shard_map/gather_tokens/all_to_all | solution.py:37
  22.5 0.0 all-gather.4.cloned.1.call-start
  22.5 0.7 all-gather.4.cloned.1.call-update
  23.2 28.4 %all-to-all-done = bf16[8,32,1024]{2,1,0:T(8,128)(2,1)S(1)} async-done(((bf16[8,32,1024]{2,1,0:T(8,128)(2,1)}), bf16[8,32,1024]{2,1,0:T(8,128)(2,1)S(1)}, u32[]{:S(2)}, u32[]{:S(2)}) %all-to-all-start) | async-done | bytes 524320 | tf_op jit(solution)/shard_map/gather_tokens/all_to_all | solution.py:37
  51.6 0.1 multiply_convert_fusion.2
  51.8 0.1 copy.15
  51.9 16.4 %all-gather.5 = f16[1024,1024]{1,0:T(8,128)(2,1)S(1)} all-gather(f16[256,1024]{1,0:T(8,128)(2,1)S(1)} %bitcast.23), channel_id=1, replica_groups=mesh['y'=4,'core'=2,'zh'=2,'x'=4,'th'=2,'tl'=4] {'x'}, dimensions={0}, use_global_device_ids=true | all-gather | bytes 2621440 | tf_op jit(solution)/shard_map/gather_tokens/all_gather | solution.py:59
  68.3 0.6 multiply_convert_fusion
  68.9 1.1 constant_dynamic-slice_fusion
  70.0 1.9 collective-permute-start
  71.9 2.2 convolution_convert_fusion.1
  74.2 5.0 %all-to-all-start.1 = ((f16[8,128,512]{2,1,0:T(8,128)(2,1)}), f16[8,128,512]{2,1,0:T(8,128)(2,1)}, u32[]{:S(2)}, u32[]{:S(2)}) async-start(f16[8,128,512]{2,1,0:T(8,128)(2,1)} %bitcast.27), calls=%async_computation.1 | async-start | bytes 2097152 | tf_op jit(solution)/shard_map/preact/all_to_all | solution.py:37
  79.2 2.3 copy.16
  81.4 12.3 %all-to-all-done.1 = f16[8,128,512]{2,1,0:T(8,128)(2,1)} async-done(((f16[8,128,512]{2,1,0:T(8,128)(2,1)}), f16[8,128,512]{2,1,0:T(8,128)(2,1)}, u32[]{:S(2)}, u32[]{:S(2)}) %all-to-all-start.1) | async-done | bytes 1048608 | tf_op jit(solution)/shard_map/preact/all_to_all | solution.py:37
  93.8 1.4 convert_reduce_fusion
  95.2 0.0 all-gather.4.cloned.1.call-done
  95.2 1.1 multiply_convert_fusion.3
  96.3 13.1 %all-gather.6 = f16[1024,512]{1,0:T(8,128)(2,1)S(1)} all-gather(f16[128,512]{1,0:T(8,128)(2,1)S(1)} %multiply_convert_fusion.3), channel_id=1, replica_groups=mesh['y'=4,'core'=2,'zh'=2,'x'=4,'th'=2,'tl'=4] {'y','core'}, dimensions={0}, use_global_device_ids=true | all-gather | bytes 1179648 | tf_op jit(solution)/shard_map/gather_grad/all_gather | solution.py:59
  109.4 1.0 copy-done.1
  110.4 3.8 %convert_bitcast_fusion = bf16[4,1024,256]{2,1,0:T(8,128)(2,1)} fusion(bf16[4,256,512]{2,1,0:T(8,128)(2,1)} %bitcast.28, f16[1024,512]{1,0:T(8,128)(2,1)S(1)} %all-gather.6), kind=kOutput, calls=%fused_computation.1 | convolution fusion | flops 1076363264 | bytes 4194304 | tf_op jit(solution)/shard_map/grad_input/rc,kfc->krf/dot_general | solution.py:111
  114.2 4.5 %all-to-all-start.2 = ((bf16[4,1024,256]{2,1,0:T(8,128)(2,1)}), bf16[4,1024,256]{2,1,0:T(8,128)(2,1)}, u32[]{:S(2)}, u32[]{:S(2)}) async-start(bf16[4,1024,256]{2,1,0:T(8,128)(2,1)} %convert_bitcast_fusion), calls=%async_computation.2 | async-start | bytes 4194304 | tf_op jit(solution)/shard_map/grad_input/all_to_all | solution.py:37
  118.7 2.4 %multiply_convert_fusion.1 = bf16[1024,512]{1,0:T(8,128)(2,1)} fusion(f16[1024,512]{1,0:T(8,128)(2,1)} %copy-done.1), kind=kLoop, calls=%fused_computation.2 | loop fusion | flops 1572864 | bytes 2097152 | tf_op jit(solution)/shard_map/gather_grad/convert_element_type | solution.py:63
  121.1 1.7 collective-permute-start.1
  122.8 2.8 %broadcast_select_fusion.2 = bf16[1024,512]{1,0:T(8,128)(2,1)} fusion(bf16[1024,512]{1,0:T(8,128)(2,1)} %collective-permute-done.1, pred[]{:T(512)S(6)} %eq.18, f16[1024,512]{1,0:T(8,128)(2,1)} %copy-done.1), kind=kLoop, calls=%fused_computation.16 | loop fusion | flops 2097152 | bytes 3145729 | tf_op jit(solution)/shard_map/factor_columns/jit(_where)/select_n | solution.py:103
  125.6 20.2 %all-to-all-done.2 = bf16[4,1024,256]{2,1,0:T(8,128)(2,1)} async-done(((bf16[4,1024,256]{2,1,0:T(8,128)(2,1)}), bf16[4,1024,256]{2,1,0:T(8,128)(2,1)}, u32[]{:S(2)}, u32[]{:S(2)}) %all-to-all-start.2) | async-done | bytes 2097184 | tf_op jit(solution)/shard_map/grad_input/all_to_all | solution.py:37
  145.9 2.8 %reduce_sum.46 = bf16[1024,256]{1,0:T(8,128)(2,1)} reduce(bf16[4,1024,256]{2,1,0:T(8,128)(2,1)} %all-to-all-done.2, bf16[]{:T(256)} %constant.93.clone.1), dimensions={0}, to_apply=%region_1.2 | reduce | flops 786432 | bytes 2621442 | tf_op jit(solution)/shard_map/grad_input/reduce_sum | solution.py:46
  148.7 1.9 copy.17
  150.6 8.5 %all-to-all-start.3 = ((bf16[4,8,2,16,256]{4,3,2,1,0:T(8,128)(2,1)}), bf16[4,8,2,16,256]{4,3,2,1,0:T(8,128)(2,1)}, u32[]{:S(2)}, u32[]{:S(2)}) async-start(bf16[4,8,2,16,256]{4,3,2,1,0:T(8,128)(2,1)} %copy.17), calls=%async_computation.3 | async-start | bytes 1048576 | tf_op jit(solution)/shard_map/grad_input/all_to_all | solution.py:37
  159.1 1.4 broadcast_select_fusion.1
  160.5 4.2 %collective-permute-start.2 = (bf16[1024,512]{1,0:T(8,128)(2,1)}, bf16[1024,512]{1,0:T(8,128)(2,1)}, u32[]{:S(2)}, u32[]{:S(2)}) collective-permute-start(bf16[1024,512]{1,0:T(8,128)(2,1)} %broadcast_select_fusion.1), channel_id=1, source_target_pairs={{0,128},{128,0},{256,384},{384,256},{1,129},{129,1},{257,385},{385... | collective-permute-start | bytes 3145736 | tf_op jit(solution)/shard_map/act_columns/ppermute | solution.py:107
  164.7 1.3 collective-permute-start.3
  166.0 17.5 %collective-permute-done.2 = bf16[1024,512]{1,0:T(8,128)(2,1)} collective-permute-done((bf16[1024,512]{1,0:T(8,128)(2,1)}, bf16[1024,512]{1,0:T(8,128)(2,1)}, u32[]{:S(2)}, u32[]{:S(2)}) %collective-permute-start.2) | collective-permute-done | bytes 1048608 | tf_op jit(solution)/shard_map/act_columns/ppermute | solution.py:107
  183.5 14.4 %collective-permute-done.3 = bf16[1024,512]{1,0:T(8,128)(2,1)} collective-permute-done((bf16[1024,512]{1,0:T(8,128)(2,1)}, bf16[1024,512]{1,0:T(8,128)(2,1)}, u32[]{:S(2)}, u32[]{:S(2)}) %collective-permute-start.3) | collective-permute-done | bytes 1048608 | tf_op jit(solution)/shard_map/grad_input/ppermute | solution.py:33
  197.9 2.3 broadcast_select_fusion
  200.2 2.2 collective-permute-start.4
  202.5 1.1 reduce_sum.47
  203.6 0.7 copy.18
  204.3 8.7 %all-to-all-start.4 = ((bf16[4,128,128]{2,1,0:T(8,128)(2,1)}), bf16[4,128,128]{2,1,0:T(8,128)(2,1)S(1)}, u32[]{:S(2)}, u32[]{:S(2)}) async-start(bf16[4,128,128]{2,1,0:T(8,128)(2,1)} %bitcast.12), calls=%async_computation.4 | async-start | bytes 262144 | tf_op jit(solution)/shard_map/grad_input/all_to_all | solution.py:37
  213.0 4.1 %convolution_convert_fusion = bf16[1024,512]{1,0:T(8,128)(2,1)} fusion(f16[1024,512]{1,0:T(8,128)(2,1)} %copy-done.1, f16[1024,1024]{1,0:T(8,128)(2,1)} %copy-done.2), kind=kOutput, calls=%fused_computation.4 | convolution fusion | flops 1078984704 | bytes 4194304 | tf_op jit(solution)/shard_map/grad_weight/dot_general | solution.py:67
  217.1 2.3 convolution_multiply_fusion.1
  219.4 7.8 %all-to-all-done.4 = bf16[4,128,128]{2,1,0:T(8,128)(2,1)S(1)} async-done(((bf16[4,128,128]{2,1,0:T(8,128)(2,1)}), bf16[4,128,128]{2,1,0:T(8,128)(2,1)S(1)}, u32[]{:S(2)}, u32[]{:S(2)}) %all-to-all-start.4) | async-done | bytes 131104 | tf_op jit(solution)/shard_map/grad_input/all_to_all | solution.py:37
  227.2 0.6 reduce_sum.48
  227.9 3.3 %convolution_multiply_fusion = f32[512,512]{1,0:T(8,128)} fusion(bf16[1024,512]{1,0:T(8,128)(2,1)} %broadcast_select_fusion, bf16[1024,512]{1,0:T(8,128)(2,1)} %collective-permute-done.4, pred[]{:T(512)S(6)} %eq.21, f16[1024,512]{1,0:T(8,128)(2,1)} %copy-done.1), kind=kOutput, calls=%fused_computation.6 | convolution fusion | flops 539230208 | bytes 4194305 | tf_op jit(solution)/shard_map/grad_factor/dot_general | solution.py:67
  (10 shorter events, 0.1 us)
Async XLA Ops:
  7.2 1.3 copy-start
  9.9 41.7 %all-to-all-start = ((bf16[8,32,1024]{2,1,0:T(8,128)(2,1)}), bf16[8,32,1024]{2,1,0:T(8,128)(2,1)S(1)}, u32[]{:S(2)}, u32[]{:S(2)}) async-start(bf16[8,32,1024]{2,1,0:T(8,128)(2,1)} %broadcast_in_dim.2), calls=%async_computation | async-start | bytes 1048576 | tf_op jit(solution)/shard_map/gather_tokens/all_to_all | solution.py:37
  22.5 72.7 %all-gather.4.cloned.1.call-start = ((), (), s32[]{:S(2)}) async-start(), calls=%async_computation.5 | async-start | bytes 1179648 | tf_op jit(solution)/shard_map/grad_out_piece/all_gather | solution.py:79
  68.3 3.6 %copy-start.2 = (f16[1024,1024]{1,0:T(8,128)(2,1)}, f16[1024,1024]{1,0:T(8,128)(2,1)S(1)}, u32[]{:S(2)}) copy-start(f16[1024,1024]{1,0:T(8,128)(2,1)S(1)} %all-gather.5) | copy-start | bytes 6291460
  68.9 3.0 %copy-start.3 = (bf16[1024,512]{1,0:T(8,128)(2,1)S(1)}, bf16[1024,512]{1,0:T(8,128)(2,1)}, u32[]{:S(2)}) copy-start(bf16[1024,512]{1,0:T(8,128)(2,1)} %param.4) | copy-start | bytes 3145732
  70.0 23.8 %collective-permute-start = (bf16[1024,512]{1,0:T(8,128)(2,1)}, bf16[1024,512]{1,0:T(8,128)(2,1)}, u32[]{:S(2)}, u32[]{:S(2)}) collective-permute-start(bf16[1024,512]{1,0:T(8,128)(2,1)} %constant_dynamic-slice_fusion), channel_id=1, source_target_pairs={{0,64},{64,0},{1,65},{65,1},{2,66},{66,2},{3,67},{67,3},{4,68},{68... | collective-permute-start | bytes 3145736 | tf_op jit(solution)/shard_map/preact/ppermute | solution.py:28
  74.2 19.6 %all-to-all-start.1 = ((f16[8,128,512]{2,1,0:T(8,128)(2,1)}), f16[8,128,512]{2,1,0:T(8,128)(2,1)}, u32[]{:S(2)}, u32[]{:S(2)}) async-start(f16[8,128,512]{2,1,0:T(8,128)(2,1)} %bitcast.27), calls=%async_computation.1 | async-start | bytes 2097152 | tf_op jit(solution)/shard_map/preact/all_to_all | solution.py:37
  109.4 1.0 copy-start.1
  114.2 31.6 %all-to-all-start.2 = ((bf16[4,1024,256]{2,1,0:T(8,128)(2,1)}), bf16[4,1024,256]{2,1,0:T(8,128)(2,1)}, u32[]{:S(2)}, u32[]{:S(2)}) async-start(bf16[4,1024,256]{2,1,0:T(8,128)(2,1)} %convert_bitcast_fusion), calls=%async_computation.2 | async-start | bytes 4194304 | tf_op jit(solution)/shard_map/grad_input/all_to_all | solution.py:37
  121.1 1.7 collective-permute-start.1
  150.6 47.3 %all-to-all-start.3 = ((bf16[4,8,2,16,256]{4,3,2,1,0:T(8,128)(2,1)}), bf16[4,8,2,16,256]{4,3,2,1,0:T(8,128)(2,1)}, u32[]{:S(2)}, u32[]{:S(2)}) async-start(bf16[4,8,2,16,256]{4,3,2,1,0:T(8,128)(2,1)} %copy.17), calls=%async_computation.3 | async-start | bytes 1048576 | tf_op jit(solution)/shard_map/grad_input/all_to_all | solution.py:37
  160.5 23.0 %collective-permute-start.2 = (bf16[1024,512]{1,0:T(8,128)(2,1)}, bf16[1024,512]{1,0:T(8,128)(2,1)}, u32[]{:S(2)}, u32[]{:S(2)}) collective-permute-start(bf16[1024,512]{1,0:T(8,128)(2,1)} %broadcast_select_fusion.1), channel_id=1, source_target_pairs={{0,128},{128,0},{256,384},{384,256},{1,129},{129,1},{257,385},{385... | collective-permute-start | bytes 3145736 | tf_op jit(solution)/shard_map/act_columns/ppermute | solution.py:107
  164.7 33.2 %collective-permute-start.3 = (bf16[1024,512]{1,0:T(8,128)(2,1)}, bf16[1024,512]{1,0:T(8,128)(2,1)}, u32[]{:S(2)}, u32[]{:S(2)}) collective-permute-start(bf16[1024,512]{1,0:T(8,128)(2,1)} %broadcast_select_fusion.2), channel_id=1, source_target_pairs={{0,2},{4,6},{65,67},{69,71},{130,128},{134,132},{195,193},{199,197... | collective-permute-start | bytes 3145736 | tf_op jit(solution)/shard_map/grad_input/ppermute | solution.py:33
  200.2 27.6 %collective-permute-start.4 = (bf16[1024,512]{1,0:T(8,128)(2,1)}, bf16[1024,512]{1,0:T(8,128)(2,1)}, u32[]{:S(2)}, u32[]{:S(2)}) collective-permute-start(bf16[1024,512]{1,0:T(8,128)(2,1)} %broadcast_select_fusion), channel_id=1, source_target_pairs={{0,1},{2,3},{4,5},{6,7},{65,64},{67,66},{69,68},{71,70},{130,131},... | collective-permute-start | bytes 3145736 | tf_op jit(solution)/shard_map/grad_factor/ppermute | solution.py:33
  204.3 22.9 %all-to-all-start.4 = ((bf16[4,128,128]{2,1,0:T(8,128)(2,1)}), bf16[4,128,128]{2,1,0:T(8,128)(2,1)S(1)}, u32[]{:S(2)}, u32[]{:S(2)}) async-start(bf16[4,128,128]{2,1,0:T(8,128)(2,1)} %bitcast.12), calls=%async_computation.4 | async-start | bytes 262144 | tf_op jit(solution)/shard_map/grad_input/all_to_all | solution.py:37
Sparse Core Ops, SparseCore 0:
  26.0 66.6 all-gather.3

commit v7 on v6

--- a/solution.py
+++ b/solution.py
@@ -3,12 +3,14 @@
 import jax
 import jax.numpy as jnp
 from jax import lax
+from jax.experimental import pallas as pl
+from jax.experimental.pallas import tpu as pltpu
 from jax.sharding import Mesh, PartitionSpec as P
 
 BF16 = jnp.bfloat16
 F16 = jnp.float16
 F32 = jnp.float32
-IN = ("y", "core")
+IN = ("yh", "yl", "core")
 OUT = ("zh", "x")
 TOK = ("th", "tl")
 TOKEN_SCALE = 8192.0
@@ -67,10 +69,26 @@
     return lax.dot_general(left, right, (((0,), (0,)), ((), ())), preferred_element_type=F32)
 
 
+def sum_kernel(parts_ref, out_ref):
+    out_ref[0] = jnp.sum(parts_ref[:, :, 0].astype(F32), axis=0).astype(BF16)
+
+
+def sum_by_tl(parts):
+    return pl.pallas_call(
+        sum_kernel,
+        grid=(4,),
+        in_specs=[pl.BlockSpec((4, 16, 1, 16, 256), lambda i: (0, 0, i, 0, 0))],
+        out_specs=pl.BlockSpec((1, 16, 16, 256), lambda i: (i, 0, 0, 0)),
+        out_shape=jax.ShapeDtypeStruct((4, 16, 16, 256), BF16),
+        compiler_params=pltpu.CompilerParams(vmem_limit_bytes=16 * 2**20),
+        cost_estimate=pl.CostEstimate(flops=2**20, bytes_accessed=5 * 2**19, transcendentals=0),
+    )(parts.reshape(4, 16, 4, 16, 256))
+
+
 def on_device(tokens_in, weight, grad_out):
-    y, core, zh, x, th, tl = (lax.axis_index(a) for a in ("y", "core", "zh", "x", "th", "tl"))
+    core, zh, x, th, tl = (lax.axis_index(a) for a in ("core", "zh", "x", "th", "tl"))
     tok = th * 4 + tl
-    piece = y * 2 + core
+    piece = lax.axis_index(IN)
 
     with jax.named_scope("grad_out_piece"):
         own_grad, own = lax.optimization_barrier(
@@ -104,15 +122,14 @@
 
     with jax.named_scope("act_columns"):
         act_cols = jnp.where(core == x // 2, act_cols, act_other)
-        from_y = lax.ppermute(act_cols, "y", [(0, 1), (1, 0), (2, 3), (3, 2)])
+        act_pair = lax.all_gather(act_cols, "yl", axis=0)
 
     with jax.named_scope("grad_input"):
         by_x = weight.reshape(2, 4, 128, 512).transpose(1, 0, 2, 3).reshape(4, 256, 512)
         share = jnp.einsum("rc,kfc->krf", grad_rows, by_x, preferred_element_type=F32).astype(BF16)
         part, cross = lax.optimization_barrier((exchange(share, "x"), cross))
         mid = send_along(cross, 2, (0, 4))
-        part = total(part).astype(BF16).reshape(8, 2, 4, 16, 256).transpose(2, 0, 1, 3, 4)
-        part, from_y, mid = lax.optimization_barrier((exchange(part, "tl"), from_y, mid))
+        part, mid = lax.optimization_barrier((exchange(sum_by_tl(part), "tl"), mid))
         part = total(part).astype(BF16)
         part = part.reshape(8, 2, 16, 2, 128).transpose(3, 1, 0, 2, 4).reshape(4, 128, 128)
         grad_input = total(exchange(part, ("zh", "th"))).astype(BF16)
@@ -127,13 +144,13 @@
         grad_factor = tn_dot(grad_rows, cross) / 1024.0
 
     with jax.named_scope("act_factor"):
-        act_cols = jnp.where(y % 2 == zh, act_cols, from_y)
+        act_cols = lax.dynamic_index_in_dim(act_pair, zh, 0, keepdims=False)
         act_factor = tn_dot(cols_of(tokens, tok * 128, 128), act_cols) / 1024.0
     return (grad_input, grad_weight, act_factor, grad_factor)
 
 
 def solution(mesh):
-    fine = Mesh(mesh.devices.reshape(4, 2, 2, 4, 2, 4), ("y", "core", "zh", "x", "th", "tl"))
+    fine = Mesh(mesh.devices.reshape(2, 2, 2, 2, 4, 2, 4), IN + OUT + TOK)
     return jax.shard_map(
         on_device,
         mesh=fine,

time: 239 us -> 232 us (0.971)
  the two profiles are of different devices: /device:TPU:8 before, /device:TPU:10 now
where the time goes in v7:
time: 232 us; the launch traced here: 231 us
  waiting for transfers between devices  104 us (45%)
  starting transfers between devices  45.9 us (20%)
  blocking collectives  29.5 us (13%)
  between operations  15.7 us (7%)
  matrix products  14.1 us (6%)
  other arithmetic  13.9 us (6%)
  local copies, waits for them, and re-layouts  7.72 us (3%)
    all_to_all x5, waiting for transfers between devices, exchange(): return lax.all_to_all(value, axis, split_axis=0, concat_axis=0, tiled=True)  67.6 us
    all_to_all x5, starting transfers between devices, exchange(): return lax.all_to_all(value, axis, split_axis=0, concat_axis=0, tiled=True)  39.3 us
    ppermute x3, waiting for transfers between devices, send_along(): return lax.ppermute(value, IN + TOK, pairs)  35.7 us
    all_gather x2, blocking collectives, gather_scaled(): return lax.all_gather(scaled, axis, axis=0, tiled=True)  29.5 us
    dot_general x3, matrix products, tn_dot(): lax.dot_general(left, right, (((0,), (0,)), ((), ())), preferred_element_...  9.17 us
  transfers between devices with their start and end apart: 11, of which 5 were waited for; matrix products, arithmetic and copies ran while one was open for 11% of the time, Pallas kernels for 0%

profile of v7, /device:TPU:10, one launch (start us, length us, event | category | flops | bytes accessed | tf_op | source)
XLA Modules:
  0.0 231.2 jit_solution(6217361100575753248)
XLA Ops:
  8.0 0.0 copy-start
  8.0 0.9 constant_dynamic-slice_fusion.1
  9.0 0.3 copy-done
  9.3 0.7 constant_dynamic-slice_fusion.2
  9.9 0.9 broadcast_in_dim.2
  10.8 12.5 %all-to-all-start = ((bf16[8,32,1024]{2,1,0:T(8,128)(2,1)}), bf16[8,32,1024]{2,1,0:T(8,128)(2,1)S(1)}, u32[]{:S(2)}, u32[]{:S(2)}) async-start(bf16[8,32,1024]{2,1,0:T(8,128)(2,1)} %broadcast_in_dim.2), calls=%async_computation | async-start | bytes 1048576 | tf_op jit(solution)/shard_map/gather_tokens/all_to_all | solution.py:39
  23.3 0.0 all-gather.6.cloned.1.call-start
  23.3 0.7 all-gather.6.cloned.1.call-update
  24.1 28.4 %all-to-all-done = bf16[8,32,1024]{2,1,0:T(8,128)(2,1)S(1)} async-done(((bf16[8,32,1024]{2,1,0:T(8,128)(2,1)}), bf16[8,32,1024]{2,1,0:T(8,128)(2,1)S(1)}, u32[]{:S(2)}, u32[]{:S(2)}) %all-to-all-start) | async-done | bytes 524320 | tf_op jit(solution)/shard_map/gather_tokens/all_to_all | solution.py:39
  52.5 0.1 multiply_convert_fusion.2
  52.6 0.1 copy.9
  52.7 16.0 %all-gather.9 = f16[1024,1024]{1,0:T(8,128)(2,1)S(1)} all-gather(f16[256,1024]{1,0:T(8,128)(2,1)S(1)} %bitcast.24), channel_id=1, replica_groups=mesh['yh'=2,'yl'=2,'core'=2,'zh'=2,'x'=4,'th'=2,'tl'=4] {'x'}, dimensions={0}, use_global_device_ids=true | all-gather | bytes 2621440 | tf_op jit(solution)/shard_map/gather_tokens/all_gather | solution.py:61
  68.7 0.6 multiply_convert_fusion
  69.3 0.0 copy-start.7
  69.4 0.1 constant_dynamic-slice_fusion
  69.5 2.2 collective-permute-start
  71.7 2.2 convolution_convert_fusion.1
  73.9 5.1 %all-to-all-start.1 = ((f16[8,128,512]{2,1,0:T(8,128)(2,1)}), f16[8,128,512]{2,1,0:T(8,128)(2,1)S(1)}, u32[]{:S(2)}, u32[]{:S(2)}) async-start(f16[8,128,512]{2,1,0:T(8,128)(2,1)} %bitcast.27), calls=%async_computation.1 | async-start | bytes 2097152 | tf_op jit(solution)/shard_map/preact/all_to_all | solution.py:39
  79.0 2.3 copy.10
  81.3 12.2 %all-to-all-done.1 = f16[8,128,512]{2,1,0:T(8,128)(2,1)S(1)} async-done(((f16[8,128,512]{2,1,0:T(8,128)(2,1)}), f16[8,128,512]{2,1,0:T(8,128)(2,1)S(1)}, u32[]{:S(2)}, u32[]{:S(2)}) %all-to-all-start.1) | async-done | bytes 1048608 | tf_op jit(solution)/shard_map/preact/all_to_all | solution.py:39
  93.5 0.1 convert_reduce_fusion
  93.7 0.0 all-gather.6.cloned.1.call-done
  93.7 1.2 multiply_convert_fusion.3
  94.9 13.5 %all-gather.10 = f16[1024,512]{1,0:T(8,128)(2,1)S(1)} all-gather(f16[128,512]{1,0:T(8,128)(2,1)S(1)} %multiply_convert_fusion.3), channel_id=1, replica_groups=mesh['yh'=2,'yl'=2,'core'=2,'zh'=2,'x'=4,'th'=2,'tl'=4] {'yh','yl','core'}, dimensions={0}, use_global_device_ids=true | all-gather | bytes 1179648 | tf_op jit(solution)/shard_map/gather_grad/all_gather | solution.py:61
  108.4 1.0 copy-done.3
  109.4 2.7 %convert_bitcast_fusion = bf16[4,1024,256]{2,1,0:T(8,128)(2,1)} fusion(bf16[4,256,512]{2,1,0:T(8,128)(2,1)S(1)} %bitcast.28, f16[1024,512]{1,0:T(8,128)(2,1)S(1)} %all-gather.10), kind=kOutput, calls=%fused_computation.1 | convolution fusion | flops 1076363264 | bytes 4194304 | tf_op jit(solution)/shard_map/grad_input/rc,kfc->krf/dot_general | solution.py:129
  112.0 5.0 %all-to-all-start.2 = ((bf16[4,1024,256]{2,1,0:T(8,128)(2,1)}), bf16[4,1024,256]{2,1,0:T(8,128)(2,1)S(1)}, u32[]{:S(2)}, u32[]{:S(2)}) async-start(bf16[4,1024,256]{2,1,0:T(8,128)(2,1)} %convert_bitcast_fusion), calls=%async_computation.2 | async-start | bytes 4194304 | tf_op jit(solution)/shard_map/grad_input/all_to_all | solution.py:39
  117.0 2.4 %multiply_convert_fusion.1 = bf16[1024,512]{1,0:T(8,128)(2,1)} fusion(f16[1024,512]{1,0:T(8,128)(2,1)} %copy-done.3), kind=kLoop, calls=%fused_computation.2 | loop fusion | flops 1572864 | bytes 2097152 | tf_op jit(solution)/shard_map/gather_grad/convert_element_type | solution.py:65
  119.4 1.7 collective-permute-start.1
  121.1 2.8 %broadcast_select_fusion.2 = bf16[1024,512]{1,0:T(8,128)(2,1)} fusion(bf16[1024,512]{1,0:T(8,128)(2,1)} %collective-permute-done.1, pred[]{:T(512)S(6)} %eq.14, f16[1024,512]{1,0:T(8,128)(2,1)} %copy-done.3), kind=kLoop, calls=%fused_computation.16 | loop fusion | flops 2097152 | bytes 3145729 | tf_op jit(solution)/shard_map/factor_columns/jit(_where)/select_n | solution.py:121
  123.9 18.5 %all-to-all-done.2 = bf16[4,1024,256]{2,1,0:T(8,128)(2,1)S(1)} async-done(((bf16[4,1024,256]{2,1,0:T(8,128)(2,1)}), bf16[4,1024,256]{2,1,0:T(8,128)(2,1)S(1)}, u32[]{:S(2)}, u32[]{:S(2)}) %all-to-all-start.2) | async-done | bytes 2097184 | tf_op jit(solution)/shard_map/grad_input/all_to_all | solution.py:39
  142.4 0.5 grad_input.1
  142.9 0.8 copy-done.1
  143.7 7.9 %all-to-all-start.3 = ((bf16[4,16,16,256]{3,2,1,0:T(8,128)(2,1)}), bf16[4,16,16,256]{3,2,1,0:T(8,128)(2,1)}, u32[]{:S(2)}, u32[]{:S(2)}) async-start(bf16[4,16,16,256]{3,2,1,0:T(8,128)(2,1)} %copy-done.1), calls=%async_computation.3 | async-start | bytes 1048576 | tf_op jit(solution)/shard_map/grad_input/all_to_all | solution.py:39
  151.6 1.4 collective-permute-start.2
  153.0 2.5 %broadcast_select_fusion.1 = bf16[1024,512]{1,0:T(8,128)(2,1)} fusion(bf16[1024,512]{1,0:T(8,128)(2,1)} %collective-permute-done, pred[]{:T(512)S(6)} %eq.15, bf16[1024,1024]{1,0:T(8,128)(2,1)} %copy-done.2, s32[]{:T(128)S(6)} %select_n.60), kind=kLoop, calls=%fused_computation.15 | loop fusion | flops 524288 | bytes 3145733 | tf_op jit(solution)/shard_map/act_columns/jit(_where)/select_n | solution.py:124
  155.5 0.0 all-gather.8.cloned.1.call-update
  155.5 35.7 %collective-permute-done.2 = bf16[1024,512]{1,0:T(8,128)(2,1)} collective-permute-done((bf16[1024,512]{1,0:T(8,128)(2,1)}, bf16[1024,512]{1,0:T(8,128)(2,1)}, u32[]{:S(2)}, u32[]{:S(2)}) %collective-permute-start.2) | collective-permute-done | bytes 1048608 | tf_op jit(solution)/shard_map/grad_input/ppermute | solution.py:35
  191.3 2.3 broadcast_select_fusion
  193.6 1.3 collective-permute-start.3
  194.9 1.1 reduce_sum.34
  196.1 0.7 copy.11
  196.8 8.8 %all-to-all-start.4 = ((bf16[4,128,128]{2,1,0:T(8,128)(2,1)}), bf16[4,128,128]{2,1,0:T(8,128)(2,1)S(1)}, u32[]{:S(2)}, u32[]{:S(2)}) async-start(bf16[4,128,128]{2,1,0:T(8,128)(2,1)} %bitcast.11), calls=%async_computation.4 | async-start | bytes 262144 | tf_op jit(solution)/shard_map/grad_input/all_to_all | solution.py:39
  205.6 3.9 %convolution_convert_fusion = bf16[1024,512]{1,0:T(8,128)(2,1)} fusion(f16[1024,512]{1,0:T(8,128)(2,1)S(1)} %copy-done.4, f16[1024,1024]{1,0:T(8,128)(2,1)} %copy-done.5), kind=kOutput, calls=%fused_computation.4 | convolution fusion | flops 1078984704 | bytes 4194304 | tf_op jit(solution)/shard_map/grad_weight/dot_general | solution.py:69
  209.4 2.4 %convolution_multiply_fusion.1 = f32[128,512]{1,0:T(8,128)} fusion(bf16[2,1024,512]{2,1,0:T(8,128)(2,1)} %bitcast.29, s32[]{:T(128)S(6)} %select_n.67, bf16[1024,1024]{1,0:T(8,128)(2,1)} %copy-done.2, s32[]{:T(128)S(6)} %select_n.63), kind=kOutput, calls=%fused_computation.7 | convolution fusion | flops 134283264 | bytes 1572872 | tf_op jit(solution)/shard_map/act_factor/dot_general | solution.py:69
  211.8 8.4 %all-to-all-done.4 = bf16[4,128,128]{2,1,0:T(8,128)(2,1)S(1)} async-done(((bf16[4,128,128]{2,1,0:T(8,128)(2,1)}), bf16[4,128,128]{2,1,0:T(8,128)(2,1)S(1)}, u32[]{:S(2)}, u32[]{:S(2)}) %all-to-all-start.4) | async-done | bytes 131104 | tf_op jit(solution)/shard_map/grad_input/all_to_all | solution.py:39
  220.2 0.6 reduce_sum.35
  220.8 3.0 %convolution_multiply_fusion = f32[512,512]{1,0:T(8,128)} fusion(bf16[1024,512]{1,0:T(8,128)(2,1)} %broadcast_select_fusion, bf16[1024,512]{1,0:T(8,128)(2,1)S(1)} %collective-permute-done.3, pred[]{:T(512)S(6)} %eq.16, f16[1024,512]{1,0:T(8,128)(2,1)S(1)} %copy-done.4), kind=kOutput, calls=%fused_computation.6 | convolution fusion | flops 539230208 | bytes 4194305 | tf_op jit(solution)/shard_map/grad_factor/dot_general | solution.py:69
  (20 shorter events, 0.1 us)
Async XLA Ops:
  8.0 1.3 copy-start
  10.8 41.7 %all-to-all-start = ((bf16[8,32,1024]{2,1,0:T(8,128)(2,1)}), bf16[8,32,1024]{2,1,0:T(8,128)(2,1)S(1)}, u32[]{:S(2)}, u32[]{:S(2)}) async-start(bf16[8,32,1024]{2,1,0:T(8,128)(2,1)} %broadcast_in_dim.2), calls=%async_computation | async-start | bytes 1048576 | tf_op jit(solution)/shard_map/gather_tokens/all_to_all | solution.py:39
  23.3 70.4 %all-gather.6.cloned.1.call-start = ((), (), s32[]{:S(2)}) async-start(), calls=%async_computation.5 | async-start | bytes 1179648 | tf_op jit(solution)/shard_map/grad_out_piece/all_gather | solution.py:97
  68.7 3.0 %copy-start.5 = (f16[1024,1024]{1,0:T(8,128)(2,1)}, f16[1024,1024]{1,0:T(8,128)(2,1)S(1)}, u32[]{:S(2)}) copy-start(f16[1024,1024]{1,0:T(8,128)(2,1)S(1)} %all-gather.9) | copy-start | bytes 6291460
  69.3 4.6 %copy-start.2 = (bf16[1024,1024]{1,0:T(8,128)(2,1)}, bf16[1024,1024]{1,0:T(8,128)(2,1)S(1)}, u32[]{:S(2)}) copy-start(bf16[1024,1024]{1,0:T(8,128)(2,1)S(1)} %multiply_convert_fusion) | copy-start | bytes 6291460
  69.3 2.3 %copy-start.7 = (bf16[1024,512]{1,0:T(8,128)(2,1)S(1)}, bf16[1024,512]{1,0:T(8,128)(2,1)}, u32[]{:S(2)}) copy-start(bf16[1024,512]{1,0:T(8,128)(2,1)} %param.4) | copy-start | bytes 3145732
  69.5 24.1 %collective-permute-start = (bf16[1024,512]{1,0:T(8,128)(2,1)S(1)}, bf16[1024,512]{1,0:T(8,128)(2,1)}, u32[]{:S(2)}, u32[]{:S(2)}) collective-permute-start(bf16[1024,512]{1,0:T(8,128)(2,1)S(1)} %constant_dynamic-slice_fusion), channel_id=1, source_target_pairs={{0,64},{64,0},{1,65},{65,1},{2,66},{66,2},{3,67},{67,3},{4,68},{68... | collective-permute-start | bytes 3145736 | tf_op jit(solution)/shard_map/preact/ppermute | solution.py:30
  73.9 19.6 %all-to-all-start.1 = ((f16[8,128,512]{2,1,0:T(8,128)(2,1)}), f16[8,128,512]{2,1,0:T(8,128)(2,1)S(1)}, u32[]{:S(2)}, u32[]{:S(2)}) async-start(f16[8,128,512]{2,1,0:T(8,128)(2,1)} %bitcast.27), calls=%async_computation.1 | async-start | bytes 2097152 | tf_op jit(solution)/shard_map/preact/all_to_all | solution.py:39
  93.5 15.8 %copy-start.8 = (bf16[4,2,128,512]{3,2,1,0:T(8,128)(2,1)S(1)}, bf16[4,2,128,512]{3,2,1,0:T(8,128)(2,1)}, u32[]{:S(2)}) copy-start(bf16[4,2,128,512]{3,2,1,0:T(8,128)(2,1)} %copy.10) | copy-start | bytes 3145732
  108.4 1.0 copy-start.3
  112.0 30.3 %all-to-all-start.2 = ((bf16[4,1024,256]{2,1,0:T(8,128)(2,1)}), bf16[4,1024,256]{2,1,0:T(8,128)(2,1)S(1)}, u32[]{:S(2)}, u32[]{:S(2)}) async-start(bf16[4,1024,256]{2,1,0:T(8,128)(2,1)} %convert_bitcast_fusion), calls=%async_computation.2 | async-start | bytes 4194304 | tf_op jit(solution)/shard_map/grad_input/all_to_all | solution.py:39
  119.4 1.7 collective-permute-start.1
  142.9 0.8 copy-start.1
  143.7 47.6 %all-to-all-start.3 = ((bf16[4,16,16,256]{3,2,1,0:T(8,128)(2,1)}), bf16[4,16,16,256]{3,2,1,0:T(8,128)(2,1)}, u32[]{:S(2)}, u32[]{:S(2)}) async-start(bf16[4,16,16,256]{3,2,1,0:T(8,128)(2,1)} %copy-done.1), calls=%async_computation.3 | async-start | bytes 1048576 | tf_op jit(solution)/shard_map/grad_input/all_to_all | solution.py:39
  151.6 57.9 %all-gather.8.cloned.1.call-start = ((), (), s32[]{:S(2)}) async-start(), calls=%async_computation.6 | async-start | bytes 3145728 | tf_op jit(solution)/shard_map/act_columns/all_gather | solution.py:125
  151.6 39.7 %copy-start.6 = (bf16[1024,512]{1,0:T(8,128)(2,1)S(1)}, bf16[1024,512]{1,0:T(8,128)(2,1)}, u32[]{:S(2)}) copy-start(bf16[1024,512]{1,0:T(8,128)(2,1)} %broadcast_select_fusion.2) | copy-start | bytes 3145732
  151.6 39.7 %collective-permute-start.2 = (bf16[1024,512]{1,0:T(8,128)(2,1)}, bf16[1024,512]{1,0:T(8,128)(2,1)}, u32[]{:S(2)}, u32[]{:S(2)}) collective-permute-start(bf16[1024,512]{1,0:T(8,128)(2,1)} %broadcast_select_fusion.2), channel_id=1, source_target_pairs={{0,2},{4,6},{65,67},{69,71},{130,128},{134,132},{195,193},{199,197... | collective-permute-start | bytes 3145736 | tf_op jit(solution)/shard_map/grad_input/ppermute | solution.py:35
  155.5 50.0 %copy-start.4 = (f16[1024,512]{1,0:T(8,128)(2,1)S(1)}, f16[1024,512]{1,0:T(8,128)(2,1)}, u32[]{:S(2)}) copy-start(f16[1024,512]{1,0:T(8,128)(2,1)} %copy-done.3) | copy-start | bytes 3145732
  193.6 27.2 %collective-permute-start.3 = (bf16[1024,512]{1,0:T(8,128)(2,1)}, bf16[1024,512]{1,0:T(8,128)(2,1)S(1)}, u32[]{:S(2)}, u32[]{:S(2)}) collective-permute-start(bf16[1024,512]{1,0:T(8,128)(2,1)} %broadcast_select_fusion), channel_id=1, source_target_pairs={{0,1},{2,3},{4,5},{6,7},{65,64},{67,66},{69,68},{71,70},{130,131},... | collective-permute-start | bytes 3145736 | tf_op jit(solution)/shard_map/grad_factor/ppermute | solution.py:35
  196.8 23.4 %all-to-all-start.4 = ((bf16[4,128,128]{2,1,0:T(8,128)(2,1)}), bf16[4,128,128]{2,1,0:T(8,128)(2,1)S(1)}, u32[]{:S(2)}, u32[]{:S(2)}) async-start(bf16[4,128,128]{2,1,0:T(8,128)(2,1)} %bitcast.11), calls=%async_computation.4 | async-start | bytes 262144 | tf_op jit(solution)/shard_map/grad_input/all_to_all | solution.py:39
Sparse Core Ops, SparseCore 0:
  26.8 66.4 all-gather.5
Sparse Core Ops, SparseCore 1:
  155.6 51.3 all-gather.7

commit v8 on v7

--- a/solution.py
+++ b/solution.py
@@ -39,11 +39,6 @@
     return lax.all_to_all(value, axis, split_axis=0, concat_axis=0, tiled=True)
 
 
-def spread(value, axis):
-    size = lax.axis_size(axis)
-    return exchange(jnp.broadcast_to(value[None], (size,) + value.shape), axis)
-
-
 def total(parts):
     return jnp.sum(parts.astype(F32), axis=0)
 
@@ -54,6 +49,10 @@
 
 def cols_of(value, start, size):
     return lax.dynamic_slice_in_dim(value, start, size, 1)
+
+
+def both_th(own, other, th):
+    return jnp.where(th == 0, jnp.stack([own, other]), jnp.stack([other, own]))
 
 
 def gather_scaled(value, axis, scale):
@@ -85,31 +84,59 @@
     )(parts.reshape(4, 16, 4, 16, 256))
 
 
+def split_kernel(parts_ref, out_ref):
+    added = jnp.sum(parts_ref[:, :, 0].astype(F32), axis=0).astype(BF16)
+    out_ref[0, 0] = added[:, :, :128]
+    out_ref[1, 0] = added[:, :, 128:]
+
+
+def sum_by_zh_th(parts):
+    return pl.pallas_call(
+        split_kernel,
+        grid=(2,),
+        in_specs=[pl.BlockSpec((4, 8, 1, 16, 256), lambda i: (0, 0, i, 0, 0))],
+        out_specs=pl.BlockSpec((2, 1, 8, 16, 128), lambda i: (0, i, 0, 0, 0)),
+        out_shape=jax.ShapeDtypeStruct((2, 2, 8, 16, 128), BF16),
+        compiler_params=pltpu.CompilerParams(vmem_limit_bytes=16 * 2**20),
+        cost_estimate=pl.CostEstimate(flops=2**18, bytes_accessed=5 * 2**17, transcendentals=0),
+    )(parts.reshape(4, 8, 2, 16, 256)).reshape(4, 128, 128)
+
+
 def on_device(tokens_in, weight, grad_out):
-    core, zh, x, th, tl = (lax.axis_index(a) for a in ("core", "zh", "x", "th", "tl"))
+    core, yl, zh, x, th, tl = (lax.axis_index(a) for a in ("core", "yl", "zh", "x", "th", "tl"))
     tok = th * 4 + tl
     piece = lax.axis_index(IN)
 
-    with jax.named_scope("grad_out_piece"):
-        own_grad, own = lax.optimization_barrier(
-            (rows_of(grad_out, piece * 16, 16), rows_of(tokens_in, x * 32, 32))
-        )
-        grad_out_rows = lax.all_gather(own_grad, TOK, axis=0, tiled=True)
+    with jax.named_scope("gather_quarter"):
+        own = rows_of(tokens_in, x * 32, 32)
+        own_grad = rows_of(grad_out, piece * 16, 16)
+        keep = cols_of(own_grad, th * 2048, 2048).reshape(16, 4, 512)
+        send = cols_of(own_grad, (1 - th) * 2048, 2048)
+        send = jnp.concatenate([own, send[:, :1024], send[:, 1024:]], axis=0)
+        got = swap(send, "th")
+        got_grad = jnp.concatenate([got[32:48], got[48:]], axis=1).reshape(16, 4, 512)
+        near_grad = both_th(keep, got_grad, th).transpose(2, 1, 0, 3).reshape(4, 16, 1024)
+        near = both_th(own, got[:32], th).reshape(64, 1024)
+        near = jnp.concatenate([jnp.broadcast_to(near[None], (4, 64, 1024)), near_grad], axis=1)
+        near = exchange(near, "tl")
+        quarter = near[:, :64].reshape(4, 2, 2, 16, 1024).transpose(2, 1, 0, 3, 4)
+        grad_out_piece = near[:, 64:].reshape(4, 16, 2, 512).transpose(2, 0, 1, 3).reshape(128, 512)
 
     with jax.named_scope("gather_tokens"):
-        near = spread(own, TOK).reshape(8, 2, 16, 1024)
-        near = near.transpose(1, 0, 2, 3).reshape(256, 1024)
-        tokens = unscaled(gather_scaled(near, "x", TOKEN_SCALE), TOKEN_SCALE)
+        quarter = quarter.reshape(256, 1024)
+        tokens = unscaled(gather_scaled(quarter, "x", TOKEN_SCALE), TOKEN_SCALE)
+
+    with jax.named_scope("act_columns"):
+        act_start = x % 2 * 512
+        act_own = lax.dynamic_slice(tokens, (core * 512, act_start), (512, 512))
+        act_other = swap(lax.dynamic_slice(tokens, ((1 - core) * 512, act_start), (512, 512)), "core")
 
     with jax.named_scope("preact"):
         partial = jnp.dot(tokens, weight, preferred_element_type=F32).astype(F16)
-        act_cols = cols_of(tokens, x % 2 * 512, 512)
-        act_other = swap(act_cols, "core")
         parts, act_other = lax.optimization_barrier(
             (exchange(partial.reshape(8, 128, 512), IN), act_other)
         )
         preact = total(parts)
-        grad_out_piece = cols_of(grad_out_rows, tok * 512, 512)
         grad_piece = (grad_out_piece.astype(F32) * gelu_slope(preact)).astype(BF16)
 
     with jax.named_scope("gather_grad"):
@@ -121,31 +148,35 @@
         cross = jnp.where(away == 0, grad_rows, far)
 
     with jax.named_scope("act_columns"):
-        act_cols = jnp.where(core == x // 2, act_cols, act_other)
-        act_pair = lax.all_gather(act_cols, "yl", axis=0)
+        act_half = jnp.where(core == x // 2, act_own, act_other)
+        from_y = swap(act_half, "yl")
 
     with jax.named_scope("grad_input"):
         by_x = weight.reshape(2, 4, 128, 512).transpose(1, 0, 2, 3).reshape(4, 256, 512)
         share = jnp.einsum("rc,kfc->krf", grad_rows, by_x, preferred_element_type=F32).astype(BF16)
-        part, cross = lax.optimization_barrier((exchange(share, "x"), cross))
+        part, cross, from_y = lax.optimization_barrier((exchange(share, "x"), cross, from_y))
         mid = send_along(cross, 2, (0, 4))
-        part, mid = lax.optimization_barrier((exchange(sum_by_tl(part), "tl"), mid))
-        part = total(part).astype(BF16)
-        part = part.reshape(8, 2, 16, 2, 128).transpose(3, 1, 0, 2, 4).reshape(4, 128, 128)
-        grad_input = total(exchange(part, ("zh", "th"))).astype(BF16)
+        part, mid = lax.optimization_barrier((sum_by_tl(part), mid))
+        cross = jnp.where(away & 2 == 0, cross, mid)
+        near = send_along(cross, 1, (0, 2, 4, 6))
+        act_half = jnp.where(yl == zh, act_half, from_y)
+        act_rest = swap(act_half, "core")
+        part, near = lax.optimization_barrier((exchange(part, "tl"), near))
+        part = exchange(sum_by_zh_th(part), ("zh", "th"))
+        grad_input = total(part).astype(BF16)
 
     with jax.named_scope("grad_weight"):
         grad_weight = tn_dot(tokens, grad_rows).astype(BF16)
 
     with jax.named_scope("grad_factor"):
-        cross = jnp.where(away & 2 == 0, cross, mid)
-        near = send_along(cross, 1, (0, 2, 4, 6))
         cross = jnp.where(away & 1 == 0, cross, near)
         grad_factor = tn_dot(grad_rows, cross) / 1024.0
 
     with jax.named_scope("act_factor"):
-        act_cols = lax.dynamic_index_in_dim(act_pair, zh, 0, keepdims=False)
-        act_factor = tn_dot(cols_of(tokens, tok * 128, 128), act_cols) / 1024.0
+        act_rows = cols_of(tokens, tok * 128, 128)
+        act_factor = tn_dot(rows_of(act_rows, core * 512, 512), act_half)
+        act_factor += tn_dot(rows_of(act_rows, (1 - core) * 512, 512), act_rest)
+        act_factor /= 1024.0
     return (grad_input, grad_weight, act_factor, grad_factor)
 
 

time: 232 us -> 226 us (0.974)
  the two profiles are of different devices: /device:TPU:10 before, /device:TPU:122 now
where the time goes in v8:
time: 226 us; the launch traced here: 225 us
  starting transfers between devices  85.7 us (38%)
  blocking collectives  54.3 us (24%)
  waiting for transfers between devices  47.8 us (21%)
  matrix products  16 us (7%)
  other arithmetic  10.9 us (5%)
  local copies, waits for them, and re-layouts  6.51 us (3%)
  Pallas kernels  2.47 us (1%)
    all_to_all x4, starting transfers between devices, exchange(): return lax.all_to_all(value, axis, split_axis=0, concat_axis=0, tiled=True)  65.1 us
    all_gather x2, blocking collectives, gather_scaled(): return lax.all_gather(scaled, axis, axis=0, tiled=True)  34.3 us
    all_to_all x4, waiting for transfers between devices, exchange(): return lax.all_to_all(value, axis, split_axis=0, concat_axis=0, tiled=True)  20.6 us
    all_to_all x1, blocking collectives, exchange(): return lax.all_to_all(value, axis, split_axis=0, concat_axis=0, tiled=True)  20 us
    ppermute x4, waiting for transfers between devices, swap(): return lax.ppermute(value, axis, [(0, 1), (1, 0)])  19.7 us
    ppermute x4, starting transfers between devices, swap(): return lax.ppermute(value, axis, [(0, 1), (1, 0)])  16.1 us
    dot_general x4, matrix products, tn_dot(): lax.dot_general(left, right, (((0,), (0,)), ((), ())), preferred_element_...  11.1 us
    ppermute x3, waiting for transfers between devices, send_along(): return lax.ppermute(value, IN + TOK, pairs)  7.52 us
  transfers between devices with their start and end apart: 11, of which 7 were waited for; matrix products, arithmetic and copies ran while one was open for 10% of the time, Pallas kernels for 1%

profile of v8, /device:TPU:122, one launch (start us, length us, event | category | flops | bytes accessed | tf_op | source)
XLA Modules:
  0.0 224.5 jit_solution(10243712866100080677)
XLA Ops:
  0.7 0.9 copy-done
  1.6 1.0 fusion.17
  2.6 9.1 %collective-permute-start = (bf16[64,1024]{1,0:T(8,128)(2,1)S(1)}, bf16[64,1024]{1,0:T(8,128)(2,1)S(1)}, u32[]{:S(2)}, u32[]{:S(2)}) collective-permute-start(bf16[64,1024]{1,0:T(8,128)(2,1)S(1)} %pad_maximum_fusion.1), channel_id=1, source_target_pairs={{0,4},{4,0},{1,5},{5,1},{2,6},{6,2},{3,7},{7,3},{8,12},{12,8},{9,1... | collective-permute-start | bytes 393224 | tf_op jit(solution)/shard_map/gather_quarter/ppermute | solution.py:30
  11.7 1.0 dynamic_slice.25
  12.8 8.7 %collective-permute-done = bf16[64,1024]{1,0:T(8,128)(2,1)S(1)} collective-permute-done((bf16[64,1024]{1,0:T(8,128)(2,1)S(1)}, bf16[64,1024]{1,0:T(8,128)(2,1)S(1)}, u32[]{:S(2)}, u32[]{:S(2)}) %collective-permute-start) | collective-permute-done | bytes 131104 | tf_op jit(solution)/shard_map/gather_quarter/ppermute | solution.py:30
  21.6 0.1 copy.12
  22.0 20.0 %all_to_all.25 = bf16[4,80,1024]{2,1,0:T(8,128)(2,1)S(1)} all-to-all(bf16[4,80,1024]{2,1,0:T(8,128)(2,1)S(1)} %pad_maximum_fusion), channel_id=1, replica_groups=mesh['yh'=2,'yl'=2,'core'=2,'zh'=2,'x'=4,'th'=2,'tl'=4] {'tl'}, dimensions={0} | all-to-all | bytes 1310720 | tf_op jit(solution)/shard_map/gather_quarter/all_to_all | solution.py:39
  42.0 0.1 multiply_convert_fusion.2
  42.2 0.6 copy-done.3
  42.8 20.6 %all-gather.2 = f16[1024,1024]{1,0:T(8,128)(2,1)S(1)} all-gather(f16[256,1024]{1,0:T(8,128)(2,1)S(1)} %bitcast.35), channel_id=1, replica_groups=mesh['yh'=2,'yl'=2,'core'=2,'zh'=2,'x'=4,'th'=2,'tl'=4] {'x'}, dimensions={0}, use_global_device_ids=true | all-gather | bytes 2621440 | tf_op jit(solution)/shard_map/gather_tokens/all_gather | solution.py:60
  63.5 2.2 convolution_convert_fusion.1
  65.7 4.7 %all-to-all-start.1 = ((f16[8,128,512]{2,1,0:T(8,128)(2,1)}), f16[8,128,512]{2,1,0:T(8,128)(2,1)S(1)}, u32[]{:S(2)}, u32[]{:S(2)}) async-start(f16[8,128,512]{2,1,0:T(8,128)(2,1)} %bitcast.38), calls=%async_computation.1 | async-start | bytes 2097152 | tf_op jit(solution)/shard_map/preact/all_to_all | solution.py:39
  70.4 0.6 multiply_convert_fusion
  71.0 1.3 copy-done.2
  72.3 0.8 dynamic_slice.26
  73.2 2.0 collective-permute-start.1
  75.3 0.9 slice_convert_fusion
  76.3 0.2 reshape.75
  76.6 0.6 collective-permute-done.1
  77.2 7.1 %all-to-all-done.1 = f16[8,128,512]{2,1,0:T(8,128)(2,1)S(1)} async-done(((f16[8,128,512]{2,1,0:T(8,128)(2,1)}), f16[8,128,512]{2,1,0:T(8,128)(2,1)S(1)}, u32[]{:S(2)}, u32[]{:S(2)}) %all-to-all-start.1) | async-done | bytes 1048608 | tf_op jit(solution)/shard_map/preact/all_to_all | solution.py:39
  84.3 0.1 convert_reduce_fusion
  84.5 0.2 multiply_convert_fusion.3
  84.7 13.7 %all-gather.3 = f16[1024,512]{1,0:T(8,128)(2,1)S(1)} all-gather(f16[128,512]{1,0:T(8,128)(2,1)S(1)} %multiply_convert_fusion.3), channel_id=1, replica_groups=mesh['yh'=2,'yl'=2,'core'=2,'zh'=2,'x'=4,'th'=2,'tl'=4] {'yh','yl','core'}, dimensions={0}, use_global_device_ids=true | all-gather | bytes 1179648 | tf_op jit(solution)/shard_map/gather_grad/all_gather | solution.py:60
  98.3 2.7 %convert_bitcast_fusion = bf16[4,1024,256]{2,1,0:T(8,128)(2,1)} fusion(bf16[4,256,512]{2,1,0:T(8,128)(2,1)S(1)} %bitcast.39, f16[1024,512]{1,0:T(8,128)(2,1)S(1)} %all-gather.3), kind=kOutput, calls=%fused_computation.1 | convolution fusion | flops 1076363264 | bytes 4194304 | tf_op jit(solution)/shard_map/grad_input/rc,kfc->krf/dot_general | solution.py:156
  101.0 5.2 %all-to-all-start.2 = ((bf16[4,1024,256]{2,1,0:T(8,128)(2,1)}), bf16[4,1024,256]{2,1,0:T(8,128)(2,1)S(1)}, u32[]{:S(2)}, u32[]{:S(2)}) async-start(bf16[4,1024,256]{2,1,0:T(8,128)(2,1)} %convert_bitcast_fusion), calls=%async_computation.2 | async-start | bytes 4194304 | tf_op jit(solution)/shard_map/grad_input/all_to_all | solution.py:39
  106.2 1.2 multiply_convert_fusion.1
  107.3 1.6 collective-permute-start.2
  109.0 2.0 dynamic-slice_select_fusion
  111.0 3.0 %collective-permute-start.3 = (bf16[512,512]{1,0:T(8,128)(2,1)}, bf16[512,512]{1,0:T(8,128)(2,1)}, u32[]{:S(2)}, u32[]{:S(2)}) collective-permute-start(bf16[512,512]{1,0:T(8,128)(2,1)} %dynamic-slice_select_fusion), channel_id=1, source_target_pairs={{0,128},{128,0},{1,129},{129,1},{2,130},{130,2},{3,131},{131,3},{4... | collective-permute-start | bytes 1572872 | tf_op jit(solution)/shard_map/act_columns/ppermute | solution.py:30
  114.0 2.5 %broadcast_select_fusion.1 = bf16[1024,512]{1,0:T(8,128)(2,1)} fusion(bf16[1024,512]{1,0:T(8,128)(2,1)} %collective-permute-done.2, pred[]{:T(512)S(6)} %eq.22, f16[1024,512]{1,0:T(8,128)(2,1)S(1)} %all-gather.3), kind=kLoop, calls=%fused_computation.14 | loop fusion | flops 2097152 | bytes 3145729 | tf_op jit(solution)/shard_map/factor_columns/jit(_where)/select_n | solution.py:148
  116.5 10.4 %collective-permute-done.3 = bf16[512,512]{1,0:T(8,128)(2,1)} collective-permute-done((bf16[512,512]{1,0:T(8,128)(2,1)}, bf16[512,512]{1,0:T(8,128)(2,1)}, u32[]{:S(2)}, u32[]{:S(2)}) %collective-permute-start.3) | collective-permute-done | bytes 524320 | tf_op jit(solution)/shard_map/act_columns/ppermute | solution.py:30
  126.9 4.9 %all-to-all-done.2 = bf16[4,1024,256]{2,1,0:T(8,128)(2,1)S(1)} async-done(((bf16[4,1024,256]{2,1,0:T(8,128)(2,1)}), bf16[4,1024,256]{2,1,0:T(8,128)(2,1)S(1)}, u32[]{:S(2)}, u32[]{:S(2)}) %all-to-all-start.2) | async-done | bytes 2097184 | tf_op jit(solution)/shard_map/grad_input/all_to_all | solution.py:39
  131.8 1.6 collective-permute-start.4
  133.5 1.7 grad_input.2
  135.2 38.0 %all-to-all-start.3 = ((bf16[4,16,16,256]{3,2,1,0:T(8,128)(2,1)}), bf16[4,16,16,256]{3,2,1,0:T(8,128)(2,1)S(1)}, u32[]{:S(2)}, u32[]{:S(2)}) async-start(bf16[4,16,16,256]{3,2,1,0:T(8,128)(2,1)} %grad_input.2), calls=%async_computation.3 | async-start | bytes 1048576 | tf_op jit(solution)/shard_map/grad_input/all_to_all | solution.py:39
  173.1 1.3 broadcast_select_fusion
  174.5 1.3 collective-permute-start.5
  175.8 1.1 broadcast_select_fusion.2
  176.9 1.9 collective-permute-start.6
  178.9 3.9 %convolution_convert_fusion = bf16[1024,512]{1,0:T(8,128)(2,1)} fusion(f16[1024,512]{1,0:T(8,128)(2,1)S(1)} %all-gather.3, f16[1024,1024]{1,0:T(8,128)(2,1)} %copy-done.1), kind=kOutput, calls=%fused_computation.4 | convolution fusion | flops 1078984704 | bytes 4194304 | tf_op jit(solution)/shard_map/grad_weight/dot_general | solution.py:68
  182.7 2.2 fusion.14
  184.9 7.5 %collective-permute-done.5 = bf16[1024,512]{1,0:T(8,128)(2,1)} collective-permute-done((bf16[1024,512]{1,0:T(8,128)(2,1)S(1)}, bf16[1024,512]{1,0:T(8,128)(2,1)}, u32[]{:S(2)}, u32[]{:S(2)}) %collective-permute-start.5) | collective-permute-done | bytes 1048608 | tf_op jit(solution)/shard_map/grad_input/ppermute | solution.py:35
  192.4 0.8 grad_input.3
  193.2 17.2 %all-to-all-start.4 = ((bf16[4,128,128]{2,1,0:T(8,128)(2,1)}), bf16[4,128,128]{2,1,0:T(8,128)(2,1)S(1)}, u32[]{:S(2)}, u32[]{:S(2)}) async-start(bf16[4,128,128]{2,1,0:T(8,128)(2,1)} %bitcast.17), calls=%async_computation.4 | async-start | bytes 262144 | tf_op jit(solution)/shard_map/grad_input/all_to_all | solution.py:39
  210.4 2.1 fusion
  212.4 3.0 %convolution_multiply_fusion = f32[512,512]{1,0:T(8,128)} fusion(bf16[1024,512]{1,0:T(8,128)(2,1)S(1)} %broadcast_select_fusion, bf16[1024,512]{1,0:T(8,128)(2,1)} %collective-permute-done.5, pred[]{:T(512)S(6)} %eq.26, f16[1024,512]{1,0:T(8,128)(2,1)S(1)} %all-gather.3), kind=kOutput, calls=%fused_computation.6 | convolution fusion | flops 539230208 | bytes 4194305 | tf_op jit(solution)/shard_map/grad_factor/dot_general | solution.py:68
  215.4 8.5 %all-to-all-done.4 = bf16[4,128,128]{2,1,0:T(8,128)(2,1)S(1)} async-done(((bf16[4,128,128]{2,1,0:T(8,128)(2,1)}), bf16[4,128,128]{2,1,0:T(8,128)(2,1)S(1)}, u32[]{:S(2)}, u32[]{:S(2)}) %all-to-all-start.4) | async-done | bytes 131104 | tf_op jit(solution)/shard_map/grad_input/all_to_all | solution.py:39
  223.9 0.6 reduce_sum.22
  (31 shorter events, 0.7 us)
Async XLA Ops:
  0.6 1.0 copy-start
  2.6 18.9 %collective-permute-start = (bf16[64,1024]{1,0:T(8,128)(2,1)S(1)}, bf16[64,1024]{1,0:T(8,128)(2,1)S(1)}, u32[]{:S(2)}, u32[]{:S(2)}) collective-permute-start(bf16[64,1024]{1,0:T(8,128)(2,1)S(1)} %pad_maximum_fusion.1), channel_id=1, source_target_pairs={{0,4},{4,0},{1,5},{5,1},{2,6},{6,2},{3,7},{7,3},{8,12},{12,8},{9,1... | collective-permute-start | bytes 393224 | tf_op jit(solution)/shard_map/gather_quarter/ppermute | solution.py:30
  42.0 0.8 copy-start.3
  42.1 21.3 %copy-start.4 = (bf16[1024,512]{1,0:T(8,128)(2,1)S(1)}, bf16[1024,512]{1,0:T(8,128)(2,1)}, u32[]{:S(2)}) copy-start(bf16[1024,512]{1,0:T(8,128)(2,1)} %param.4) | copy-start | bytes 3145732
  63.5 7.0 %copy-start.1 = (f16[1024,1024]{1,0:T(8,128)(2,1)}, f16[1024,1024]{1,0:T(8,128)(2,1)S(1)}, u32[]{:S(2)}) copy-start(f16[1024,1024]{1,0:T(8,128)(2,1)S(1)} %all-gather.2) | copy-start | bytes 6291460
  65.7 18.6 %all-to-all-start.1 = ((f16[8,128,512]{2,1,0:T(8,128)(2,1)}), f16[8,128,512]{2,1,0:T(8,128)(2,1)S(1)}, u32[]{:S(2)}, u32[]{:S(2)}) async-start(f16[8,128,512]{2,1,0:T(8,128)(2,1)} %bitcast.38), calls=%async_computation.1 | async-start | bytes 2097152 | tf_op jit(solution)/shard_map/preact/all_to_all | solution.py:39
  70.4 4.8 %copy-start.5 = (bf16[1024,512]{1,0:T(8,128)(2,1)S(1)}, bf16[1024,512]{1,0:T(8,128)(2,1)}, u32[]{:S(2)}) copy-start(bf16[1024,512]{1,0:T(8,128)(2,1)} %param.4) | copy-start | bytes 3145732
  71.0 1.3 copy-start.2
  73.2 4.0 %collective-permute-start.1 = (bf16[512,512]{1,0:T(8,128)(2,1)}, bf16[512,512]{1,0:T(8,128)(2,1)S(1)}, u32[]{:S(2)}, u32[]{:S(2)}) collective-permute-start(bf16[512,512]{1,0:T(8,128)(2,1)} %dynamic_slice.26), channel_id=1, source_target_pairs={{0,64},{64,0},{1,65},{65,1},{2,66},{66,2},{3,67},{67,3},{4,68},{68... | collective-permute-start | bytes 1572872 | tf_op jit(solution)/shard_map/act_columns/ppermute | solution.py:30
  77.2 23.8 %copy-start.6 = (bf16[512,512]{1,0:T(8,128)(2,1)}, bf16[512,512]{1,0:T(8,128)(2,1)S(1)}, u32[]{:S(2)}) copy-start(bf16[512,512]{1,0:T(8,128)(2,1)S(1)} %collective-permute-done.1) | copy-start | bytes 1572868
  101.0 30.9 %all-to-all-start.2 = ((bf16[4,1024,256]{2,1,0:T(8,128)(2,1)}), bf16[4,1024,256]{2,1,0:T(8,128)(2,1)S(1)}, u32[]{:S(2)}, u32[]{:S(2)}) async-start(bf16[4,1024,256]{2,1,0:T(8,128)(2,1)} %convert_bitcast_fusion), calls=%async_computation.2 | async-start | bytes 4194304 | tf_op jit(solution)/shard_map/grad_input/all_to_all | solution.py:39
  107.3 6.6 %collective-permute-start.2 = (bf16[1024,512]{1,0:T(8,128)(2,1)}, bf16[1024,512]{1,0:T(8,128)(2,1)}, u32[]{:S(2)}, u32[]{:S(2)}) collective-permute-start(bf16[1024,512]{1,0:T(8,128)(2,1)} %multiply_convert_fusion.1), channel_id=1, source_target_pairs={{0,4},{65,69},{130,134},{195,199},{260,256},{325,321},{390,386},{4... | collective-permute-start | bytes 3145736 | tf_op jit(solution)/shard_map/factor_columns/ppermute | solution.py:35
  111.0 15.9 %collective-permute-start.3 = (bf16[512,512]{1,0:T(8,128)(2,1)}, bf16[512,512]{1,0:T(8,128)(2,1)}, u32[]{:S(2)}, u32[]{:S(2)}) collective-permute-start(bf16[512,512]{1,0:T(8,128)(2,1)} %dynamic-slice_select_fusion), channel_id=1, source_target_pairs={{0,128},{128,0},{1,129},{129,1},{2,130},{130,2},{3,131},{131,3},{4... | collective-permute-start | bytes 1572872 | tf_op jit(solution)/shard_map/act_columns/ppermute | solution.py:30
  131.8 3.3 %collective-permute-start.4 = (bf16[1024,512]{1,0:T(8,128)(2,1)}, bf16[1024,512]{1,0:T(8,128)(2,1)}, u32[]{:S(2)}, u32[]{:S(2)}) collective-permute-start(bf16[1024,512]{1,0:T(8,128)(2,1)} %broadcast_select_fusion.1), channel_id=1, source_target_pairs={{0,2},{4,6},{65,67},{69,71},{130,128},{134,132},{195,193},{199,197... | collective-permute-start | bytes 3145736 | tf_op jit(solution)/shard_map/grad_input/ppermute | solution.py:35
  135.2 57.2 %all-to-all-start.3 = ((bf16[4,16,16,256]{3,2,1,0:T(8,128)(2,1)}), bf16[4,16,16,256]{3,2,1,0:T(8,128)(2,1)S(1)}, u32[]{:S(2)}, u32[]{:S(2)}) async-start(bf16[4,16,16,256]{3,2,1,0:T(8,128)(2,1)} %grad_input.2), calls=%async_computation.3 | async-start | bytes 1048576 | tf_op jit(solution)/shard_map/grad_input/all_to_all | solution.py:39
  174.5 17.9 %collective-permute-start.5 = (bf16[1024,512]{1,0:T(8,128)(2,1)S(1)}, bf16[1024,512]{1,0:T(8,128)(2,1)}, u32[]{:S(2)}, u32[]{:S(2)}) collective-permute-start(bf16[1024,512]{1,0:T(8,128)(2,1)S(1)} %broadcast_select_fusion), channel_id=1, source_target_pairs={{0,1},{2,3},{4,5},{6,7},{65,64},{67,66},{69,68},{71,70},{130,131},... | collective-permute-start | bytes 3145736 | tf_op jit(solution)/shard_map/grad_input/ppermute | solution.py:35
  176.9 5.8 %collective-permute-start.6 = (bf16[512,512]{1,0:T(8,128)(2,1)S(1)}, bf16[512,512]{1,0:T(8,128)(2,1)}, u32[]{:S(2)}, u32[]{:S(2)}) collective-permute-start(bf16[512,512]{1,0:T(8,128)(2,1)S(1)} %broadcast_select_fusion.2), channel_id=1, source_target_pairs={{0,64},{64,0},{1,65},{65,1},{2,66},{66,2},{3,67},{67,3},{4,68},{68... | collective-permute-start | bytes 1572872 | tf_op jit(solution)/shard_map/grad_input/ppermute | solution.py:30
  193.2 30.7 %all-to-all-start.4 = ((bf16[4,128,128]{2,1,0:T(8,128)(2,1)}), bf16[4,128,128]{2,1,0:T(8,128)(2,1)S(1)}, u32[]{:S(2)}, u32[]{:S(2)}) async-start(bf16[4,128,128]{2,1,0:T(8,128)(2,1)} %bitcast.17), calls=%async_computation.4 | async-start | bytes 262144 | tf_op jit(solution)/shard_map/grad_input/all_to_all | solution.py:39

commit v9 on v8

--- a/solution.py
+++ b/solution.py
@@ -156,12 +156,7 @@
         share = jnp.einsum("rc,kfc->krf", grad_rows, by_x, preferred_element_type=F32).astype(BF16)
         part, cross, from_y = lax.optimization_barrier((exchange(share, "x"), cross, from_y))
         mid = send_along(cross, 2, (0, 4))
-        part, mid = lax.optimization_barrier((sum_by_tl(part), mid))
-        cross = jnp.where(away & 2 == 0, cross, mid)
-        near = send_along(cross, 1, (0, 2, 4, 6))
-        act_half = jnp.where(yl == zh, act_half, from_y)
-        act_rest = swap(act_half, "core")
-        part, near = lax.optimization_barrier((exchange(part, "tl"), near))
+        part, mid = lax.optimization_barrier((exchange(sum_by_tl(part), "tl"), mid))
         part = exchange(sum_by_zh_th(part), ("zh", "th"))
         grad_input = total(part).astype(BF16)
 
@@ -169,10 +164,14 @@
         grad_weight = tn_dot(tokens, grad_rows).astype(BF16)
 
     with jax.named_scope("grad_factor"):
+        cross = jnp.where(away & 2 == 0, cross, mid)
+        near = send_along(cross, 1, (0, 2, 4, 6))
         cross = jnp.where(away & 1 == 0, cross, near)
         grad_factor = tn_dot(grad_rows, cross) / 1024.0
 
     with jax.named_scope("act_factor"):
+        act_half = jnp.where(yl == zh, act_half, from_y)
+        act_rest = swap(act_half, "core")
         act_rows = cols_of(tokens, tok * 128, 128)
         act_factor = tn_dot(rows_of(act_rows, core * 512, 512), act_half)
         act_factor += tn_dot(rows_of(act_rows, (1 - core) * 512, 512), act_rest)

time: 226 us -> 221 us (0.978)
  the two profiles are of different devices: /device:TPU:122 before, /device:TPU:8 now
where the time goes in v9:
time: 221 us; the launch traced here: 220 us
  waiting for transfers between devices  74.3 us (34%)
  blocking collectives  55.8 us (25%)
  starting transfers between devices  54.3 us (25%)
  matrix products  13.9 us (6%)
  other arithmetic  10.9 us (5%)
  local copies, waits for them, and re-layouts  7.47 us (3%)
  Pallas kernels  2.44 us (1%)
    ppermute x3, waiting for transfers between devices, send_along(): return lax.ppermute(value, IN + TOK, pairs)  37.1 us
    all_gather x2, blocking collectives, gather_scaled(): return lax.all_gather(scaled, axis, axis=0, tiled=True)  34.8 us
    ppermute x4, starting transfers between devices, swap(): return lax.ppermute(value, axis, [(0, 1), (1, 0)])  24.9 us
    all_to_all x4, starting transfers between devices, exchange(): return lax.all_to_all(value, axis, split_axis=0, concat_axis=0, tiled=True)  24.1 us
    all_to_all x1, blocking collectives, exchange(): return lax.all_to_all(value, axis, split_axis=0, concat_axis=0, tiled=True)  21.1 us
    all_to_all x4, waiting for transfers between devices, exchange(): return lax.all_to_all(value, axis, split_axis=0, concat_axis=0, tiled=True)  20.7 us
    ppermute x4, waiting for transfers between devices, swap(): return lax.ppermute(value, axis, [(0, 1), (1, 0)])  16.4 us
    dot_general x4, matrix products, tn_dot(): lax.dot_general(left, right, (((0,), (0,)), ((), ())), preferred_element_...  9.08 us
  transfers between devices with their start and end apart: 11, of which 7 were waited for; matrix products, arithmetic and copies ran while one was open for 8% of the time, Pallas kernels for 0%

profile of v9, /device:TPU:8, one launch (start us, length us, event | category | flops | bytes accessed | tf_op | source)
XLA Modules:
  0.0 220.0 jit_solution(5221846878562658776)
XLA Ops:
  0.7 0.9 copy-done
  1.6 1.0 fusion.17
  2.6 9.1 %collective-permute-start = (bf16[64,1024]{1,0:T(8,128)(2,1)S(1)}, bf16[64,1024]{1,0:T(8,128)(2,1)S(1)}, u32[]{:S(2)}, u32[]{:S(2)}) collective-permute-start(bf16[64,1024]{1,0:T(8,128)(2,1)S(1)} %pad_maximum_fusion.1), channel_id=1, source_target_pairs={{0,4},{4,0},{1,5},{5,1},{2,6},{6,2},{3,7},{7,3},{8,12},{12,8},{9,1... | collective-permute-start | bytes 393224 | tf_op jit(solution)/shard_map/gather_quarter/ppermute | solution.py:30
  11.7 1.0 dynamic_slice.25
  12.8 10.8 %collective-permute-done = bf16[64,1024]{1,0:T(8,128)(2,1)S(1)} collective-permute-done((bf16[64,1024]{1,0:T(8,128)(2,1)S(1)}, bf16[64,1024]{1,0:T(8,128)(2,1)S(1)}, u32[]{:S(2)}, u32[]{:S(2)}) %collective-permute-start) | collective-permute-done | bytes 131104 | tf_op jit(solution)/shard_map/gather_quarter/ppermute | solution.py:30
  23.8 0.1 copy.12
  24.1 21.1 %all_to_all.25 = bf16[4,80,1024]{2,1,0:T(8,128)(2,1)S(1)} all-to-all(bf16[4,80,1024]{2,1,0:T(8,128)(2,1)S(1)} %pad_maximum_fusion), channel_id=1, replica_groups=mesh['yh'=2,'yl'=2,'core'=2,'zh'=2,'x'=4,'th'=2,'tl'=4] {'tl'}, dimensions={0} | all-to-all | bytes 1310720 | tf_op jit(solution)/shard_map/gather_quarter/all_to_all | solution.py:39
  45.4 0.6 copy-done.3
  46.0 21.7 %all-gather.2 = f16[1024,1024]{1,0:T(8,128)(2,1)S(1)} all-gather(f16[256,1024]{1,0:T(8,128)(2,1)S(1)} %bitcast.35), channel_id=1, replica_groups=mesh['yh'=2,'yl'=2,'core'=2,'zh'=2,'x'=4,'th'=2,'tl'=4] {'x'}, dimensions={0}, use_global_device_ids=true | all-gather | bytes 2621440 | tf_op jit(solution)/shard_map/gather_tokens/all_gather | solution.py:60
  67.8 2.2 %convolution_convert_fusion.1 = f16[1024,512]{1,0:T(8,128)(2,1)} fusion(bf16[1024,512]{1,0:T(8,128)(2,1)S(1)} %copy-done.4, f16[1024,1024]{1,0:T(8,128)(2,1)S(1)} %all-gather.2), kind=kOutput, calls=%fused_computation.5 | convolution fusion | flops 1077411840 | bytes 4194304 | tf_op jit(solution)/shard_map/preact/dot_general | solution.py:135
  70.0 4.9 %all-to-all-start.1 = ((f16[8,128,512]{2,1,0:T(8,128)(2,1)}), f16[8,128,512]{2,1,0:T(8,128)(2,1)S(1)}, u32[]{:S(2)}, u32[]{:S(2)}) async-start(f16[8,128,512]{2,1,0:T(8,128)(2,1)} %bitcast.38), calls=%async_computation.1 | async-start | bytes 2097152 | tf_op jit(solution)/shard_map/preact/all_to_all | solution.py:39
  74.9 0.6 multiply_convert_fusion
  75.5 1.3 copy-done.2
  76.8 0.8 dynamic_slice.26
  77.6 2.0 collective-permute-start.1
  79.8 0.9 slice_convert_fusion
  80.7 0.2 reshape.75
  81.0 0.6 collective-permute-done.1
  81.6 7.8 %all-to-all-done.1 = f16[8,128,512]{2,1,0:T(8,128)(2,1)S(1)} async-done(((f16[8,128,512]{2,1,0:T(8,128)(2,1)}), f16[8,128,512]{2,1,0:T(8,128)(2,1)S(1)}, u32[]{:S(2)}, u32[]{:S(2)}) %all-to-all-start.1) | async-done | bytes 1048608 | tf_op jit(solution)/shard_map/preact/all_to_all | solution.py:39
  89.4 0.1 convert_reduce_fusion
  89.5 0.2 multiply_convert_fusion.3
  89.7 13.1 %all-gather.3 = f16[1024,512]{1,0:T(8,128)(2,1)S(1)} all-gather(f16[128,512]{1,0:T(8,128)(2,1)S(1)} %multiply_convert_fusion.3), channel_id=1, replica_groups=mesh['yh'=2,'yl'=2,'core'=2,'zh'=2,'x'=4,'th'=2,'tl'=4] {'yh','yl','core'}, dimensions={0}, use_global_device_ids=true | all-gather | bytes 1179648 | tf_op jit(solution)/shard_map/gather_grad/all_gather | solution.py:60
  102.8 2.6 %convert_bitcast_fusion = bf16[4,1024,256]{2,1,0:T(8,128)(2,1)} fusion(bf16[4,256,512]{2,1,0:T(8,128)(2,1)S(1)} %bitcast.39, f16[1024,512]{1,0:T(8,128)(2,1)S(1)} %all-gather.3), kind=kOutput, calls=%fused_computation.1 | convolution fusion | flops 1076363264 | bytes 4194304 | tf_op jit(solution)/shard_map/grad_input/rc,kfc->krf/dot_general | solution.py:156
  105.4 3.6 %all-to-all-start.2 = ((bf16[4,1024,256]{2,1,0:T(8,128)(2,1)}), bf16[4,1024,256]{2,1,0:T(8,128)(2,1)S(1)}, u32[]{:S(2)}, u32[]{:S(2)}) async-start(bf16[4,1024,256]{2,1,0:T(8,128)(2,1)} %convert_bitcast_fusion), calls=%async_computation.2 | async-start | bytes 4194304 | tf_op jit(solution)/shard_map/grad_input/all_to_all | solution.py:39
  109.1 1.2 multiply_convert_fusion.1
  110.2 1.6 collective-permute-start.2
  111.9 2.0 dynamic-slice_select_fusion
  113.8 11.8 %collective-permute-start.3 = (bf16[512,512]{1,0:T(8,128)(2,1)}, bf16[512,512]{1,0:T(8,128)(2,1)}, u32[]{:S(2)}, u32[]{:S(2)}) collective-permute-start(bf16[512,512]{1,0:T(8,128)(2,1)} %dynamic-slice_select_fusion), channel_id=1, source_target_pairs={{0,128},{128,0},{1,129},{129,1},{2,130},{130,2},{3,131},{131,3},{4... | collective-permute-start | bytes 1572872 | tf_op jit(solution)/shard_map/act_columns/ppermute | solution.py:30
  125.7 2.5 %broadcast_select_fusion.1 = bf16[1024,512]{1,0:T(8,128)(2,1)} fusion(bf16[1024,512]{1,0:T(8,128)(2,1)} %collective-permute-done.2, pred[]{:T(512)S(6)} %eq.22, f16[1024,512]{1,0:T(8,128)(2,1)S(1)} %all-gather.3), kind=kLoop, calls=%fused_computation.14 | loop fusion | flops 2097152 | bytes 3145729 | tf_op jit(solution)/shard_map/factor_columns/jit(_where)/select_n | solution.py:148
  128.2 4.9 %collective-permute-done.3 = bf16[512,512]{1,0:T(8,128)(2,1)} collective-permute-done((bf16[512,512]{1,0:T(8,128)(2,1)}, bf16[512,512]{1,0:T(8,128)(2,1)}, u32[]{:S(2)}, u32[]{:S(2)}) %collective-permute-start.3) | collective-permute-done | bytes 524320 | tf_op jit(solution)/shard_map/act_columns/ppermute | solution.py:30
  133.2 3.0 %all-to-all-done.2 = bf16[4,1024,256]{2,1,0:T(8,128)(2,1)S(1)} async-done(((bf16[4,1024,256]{2,1,0:T(8,128)(2,1)}), bf16[4,1024,256]{2,1,0:T(8,128)(2,1)S(1)}, u32[]{:S(2)}, u32[]{:S(2)}) %all-to-all-start.2) | async-done | bytes 2097184 | tf_op jit(solution)/shard_map/grad_input/all_to_all | solution.py:39
  136.1 1.7 grad_input.2
  137.8 3.5 %all-to-all-start.3 = ((bf16[4,16,16,256]{3,2,1,0:T(8,128)(2,1)}), bf16[4,16,16,256]{3,2,1,0:T(8,128)(2,1)S(1)}, u32[]{:S(2)}, u32[]{:S(2)}) async-start(bf16[4,16,16,256]{3,2,1,0:T(8,128)(2,1)} %grad_input.2), calls=%async_computation.3 | async-start | bytes 1048576 | tf_op jit(solution)/shard_map/grad_input/all_to_all | solution.py:39
  141.3 1.3 collective-permute-start.4
  142.6 37.1 %collective-permute-done.4 = bf16[1024,512]{1,0:T(8,128)(2,1)S(1)} collective-permute-done((bf16[1024,512]{1,0:T(8,128)(2,1)}, bf16[1024,512]{1,0:T(8,128)(2,1)S(1)}, u32[]{:S(2)}, u32[]{:S(2)}) %collective-permute-start.4) | collective-permute-done | bytes 1048608 | tf_op jit(solution)/shard_map/grad_input/ppermute | solution.py:35
  179.7 1.0 copy-done.6
  180.7 1.3 broadcast_select_fusion
  182.0 2.3 %collective-permute-start.6 = (bf16[1024,512]{1,0:T(8,128)(2,1)S(1)}, bf16[1024,512]{1,0:T(8,128)(2,1)}, u32[]{:S(2)}, u32[]{:S(2)}) collective-permute-start(bf16[1024,512]{1,0:T(8,128)(2,1)S(1)} %broadcast_select_fusion), channel_id=1, source_target_pairs={{0,1},{2,3},{4,5},{6,7},{65,64},{67,66},{69,68},{71,70},{130,131},... | collective-permute-start | bytes 3145736 | tf_op jit(solution)/shard_map/grad_factor/ppermute | solution.py:35
  184.3 1.1 broadcast_select_fusion.2
  185.4 1.9 collective-permute-start.5
  187.4 3.9 %convolution_convert_fusion = bf16[1024,512]{1,0:T(8,128)(2,1)} fusion(f16[1024,512]{1,0:T(8,128)(2,1)S(1)} %all-gather.3, f16[1024,1024]{1,0:T(8,128)(2,1)} %copy-done.1), kind=kOutput, calls=%fused_computation.4 | convolution fusion | flops 1078984704 | bytes 4194304 | tf_op jit(solution)/shard_map/grad_weight/dot_general | solution.py:68
  191.2 0.8 grad_input.3
  192.0 12.2 %all-to-all-start.4 = ((bf16[4,128,128]{2,1,0:T(8,128)(2,1)}), bf16[4,128,128]{2,1,0:T(8,128)(2,1)S(1)}, u32[]{:S(2)}, u32[]{:S(2)}) async-start(bf16[4,128,128]{2,1,0:T(8,128)(2,1)} %bitcast.17), calls=%async_computation.4 | async-start | bytes 262144 | tf_op jit(solution)/shard_map/grad_input/all_to_all | solution.py:39
  204.2 1.5 fusion.14
  205.6 2.0 fusion
  207.6 10.0 %all-to-all-done.4 = bf16[4,128,128]{2,1,0:T(8,128)(2,1)S(1)} async-done(((bf16[4,128,128]{2,1,0:T(8,128)(2,1)}), bf16[4,128,128]{2,1,0:T(8,128)(2,1)S(1)}, u32[]{:S(2)}, u32[]{:S(2)}) %all-to-all-start.4) | async-done | bytes 131104 | tf_op jit(solution)/shard_map/grad_input/all_to_all | solution.py:39
  217.6 0.6 reduce_sum.22
  218.3 1.7 convolution_multiply_fusion
  (33 shorter events, 0.8 us)
Async XLA Ops:
  0.6 1.0 copy-start
  2.6 21.0 %collective-permute-start = (bf16[64,1024]{1,0:T(8,128)(2,1)S(1)}, bf16[64,1024]{1,0:T(8,128)(2,1)S(1)}, u32[]{:S(2)}, u32[]{:S(2)}) collective-permute-start(bf16[64,1024]{1,0:T(8,128)(2,1)S(1)} %pad_maximum_fusion.1), channel_id=1, source_target_pairs={{0,4},{4,0},{1,5},{5,1},{2,6},{6,2},{3,7},{7,3},{8,12},{12,8},{9,1... | collective-permute-start | bytes 393224 | tf_op jit(solution)/shard_map/gather_quarter/ppermute | solution.py:30
  45.2 0.8 copy-start.3
  45.3 22.4 %copy-start.4 = (bf16[1024,512]{1,0:T(8,128)(2,1)S(1)}, bf16[1024,512]{1,0:T(8,128)(2,1)}, u32[]{:S(2)}) copy-start(bf16[1024,512]{1,0:T(8,128)(2,1)} %param.4) | copy-start | bytes 3145732
  67.7 7.1 %copy-start.1 = (f16[1024,1024]{1,0:T(8,128)(2,1)}, f16[1024,1024]{1,0:T(8,128)(2,1)S(1)}, u32[]{:S(2)}) copy-start(f16[1024,1024]{1,0:T(8,128)(2,1)S(1)} %all-gather.2) | copy-start | bytes 6291460
  70.0 19.4 %all-to-all-start.1 = ((f16[8,128,512]{2,1,0:T(8,128)(2,1)}), f16[8,128,512]{2,1,0:T(8,128)(2,1)S(1)}, u32[]{:S(2)}, u32[]{:S(2)}) async-start(f16[8,128,512]{2,1,0:T(8,128)(2,1)} %bitcast.38), calls=%async_computation.1 | async-start | bytes 2097152 | tf_op jit(solution)/shard_map/preact/all_to_all | solution.py:39
  74.9 4.8 %copy-start.5 = (bf16[1024,512]{1,0:T(8,128)(2,1)S(1)}, bf16[1024,512]{1,0:T(8,128)(2,1)}, u32[]{:S(2)}) copy-start(bf16[1024,512]{1,0:T(8,128)(2,1)} %param.4) | copy-start | bytes 3145732
  75.5 1.3 copy-start.2
  77.6 4.0 %collective-permute-start.1 = (bf16[512,512]{1,0:T(8,128)(2,1)}, bf16[512,512]{1,0:T(8,128)(2,1)S(1)}, u32[]{:S(2)}, u32[]{:S(2)}) collective-permute-start(bf16[512,512]{1,0:T(8,128)(2,1)} %dynamic_slice.26), channel_id=1, source_target_pairs={{0,64},{64,0},{1,65},{65,1},{2,66},{66,2},{3,67},{67,3},{4,68},{68... | collective-permute-start | bytes 1572872 | tf_op jit(solution)/shard_map/act_columns/ppermute | solution.py:30
  81.6 23.8 %copy-start.7 = (bf16[512,512]{1,0:T(8,128)(2,1)}, bf16[512,512]{1,0:T(8,128)(2,1)S(1)}, u32[]{:S(2)}) copy-start(bf16[512,512]{1,0:T(8,128)(2,1)S(1)} %collective-permute-done.1) | copy-start | bytes 1572868
  105.4 30.7 %all-to-all-start.2 = ((bf16[4,1024,256]{2,1,0:T(8,128)(2,1)}), bf16[4,1024,256]{2,1,0:T(8,128)(2,1)S(1)}, u32[]{:S(2)}, u32[]{:S(2)}) async-start(bf16[4,1024,256]{2,1,0:T(8,128)(2,1)} %convert_bitcast_fusion), calls=%async_computation.2 | async-start | bytes 4194304 | tf_op jit(solution)/shard_map/grad_input/all_to_all | solution.py:39
  110.2 15.5 %collective-permute-start.2 = (bf16[1024,512]{1,0:T(8,128)(2,1)}, bf16[1024,512]{1,0:T(8,128)(2,1)}, u32[]{:S(2)}, u32[]{:S(2)}) collective-permute-start(bf16[1024,512]{1,0:T(8,128)(2,1)} %multiply_convert_fusion.1), channel_id=1, source_target_pairs={{0,4},{65,69},{130,134},{195,199},{260,256},{325,321},{390,386},{4... | collective-permute-start | bytes 3145736 | tf_op jit(solution)/shard_map/factor_columns/ppermute | solution.py:35
  113.8 19.3 %collective-permute-start.3 = (bf16[512,512]{1,0:T(8,128)(2,1)}, bf16[512,512]{1,0:T(8,128)(2,1)}, u32[]{:S(2)}, u32[]{:S(2)}) collective-permute-start(bf16[512,512]{1,0:T(8,128)(2,1)} %dynamic-slice_select_fusion), channel_id=1, source_target_pairs={{0,128},{128,0},{1,129},{129,1},{2,130},{130,2},{3,131},{131,3},{4... | collective-permute-start | bytes 1572872 | tf_op jit(solution)/shard_map/act_columns/ppermute | solution.py:30
  137.8 42.9 %all-to-all-start.3 = ((bf16[4,16,16,256]{3,2,1,0:T(8,128)(2,1)}), bf16[4,16,16,256]{3,2,1,0:T(8,128)(2,1)S(1)}, u32[]{:S(2)}, u32[]{:S(2)}) async-start(bf16[4,16,16,256]{3,2,1,0:T(8,128)(2,1)} %grad_input.2), calls=%async_computation.3 | async-start | bytes 1048576 | tf_op jit(solution)/shard_map/grad_input/all_to_all | solution.py:39
  141.3 38.4 %collective-permute-start.4 = (bf16[1024,512]{1,0:T(8,128)(2,1)}, bf16[1024,512]{1,0:T(8,128)(2,1)S(1)}, u32[]{:S(2)}, u32[]{:S(2)}) collective-permute-start(bf16[1024,512]{1,0:T(8,128)(2,1)} %broadcast_select_fusion.1), channel_id=1, source_target_pairs={{0,2},{4,6},{65,67},{69,71},{130,128},{134,132},{195,193},{199,197... | collective-permute-start | bytes 3145736 | tf_op jit(solution)/shard_map/grad_input/ppermute | solution.py:35
  179.7 1.0 copy-start.6
  182.0 36.2 %collective-permute-start.6 = (bf16[1024,512]{1,0:T(8,128)(2,1)S(1)}, bf16[1024,512]{1,0:T(8,128)(2,1)}, u32[]{:S(2)}, u32[]{:S(2)}) collective-permute-start(bf16[1024,512]{1,0:T(8,128)(2,1)S(1)} %broadcast_select_fusion), channel_id=1, source_target_pairs={{0,1},{2,3},{4,5},{6,7},{65,64},{67,66},{69,68},{71,70},{130,131},... | collective-permute-start | bytes 3145736 | tf_op jit(solution)/shard_map/grad_factor/ppermute | solution.py:35
  185.4 18.8 %collective-permute-start.5 = (bf16[512,512]{1,0:T(8,128)(2,1)S(1)}, bf16[512,512]{1,0:T(8,128)(2,1)}, u32[]{:S(2)}, u32[]{:S(2)}) collective-permute-start(bf16[512,512]{1,0:T(8,128)(2,1)S(1)} %broadcast_select_fusion.2), channel_id=1, source_target_pairs={{0,64},{64,0},{1,65},{65,1},{2,66},{66,2},{3,67},{67,3},{4,68},{68... | collective-permute-start | bytes 1572872 | tf_op jit(solution)/shard_map/act_factor/ppermute | solution.py:30
  192.0 25.6 %all-to-all-start.4 = ((bf16[4,128,128]{2,1,0:T(8,128)(2,1)}), bf16[4,128,128]{2,1,0:T(8,128)(2,1)S(1)}, u32[]{:S(2)}, u32[]{:S(2)}) async-start(bf16[4,128,128]{2,1,0:T(8,128)(2,1)} %bitcast.17), calls=%async_computation.4 | async-start | bytes 262144 | tf_op jit(solution)/shard_map/grad_input/all_to_all | solution.py:39

commit v10 on v9

--- a/solution.py
+++ b/solution.py
@@ -156,12 +156,13 @@
         share = jnp.einsum("rc,kfc->krf", grad_rows, by_x, preferred_element_type=F32).astype(BF16)
         part, cross, from_y = lax.optimization_barrier((exchange(share, "x"), cross, from_y))
         mid = send_along(cross, 2, (0, 4))
-        part, mid = lax.optimization_barrier((exchange(sum_by_tl(part), "tl"), mid))
+        act_half = jnp.where(yl == zh, act_half, from_y)
+        grad_weight = tn_dot(tokens, grad_rows).astype(BF16)
+        part, mid, act_rest, grad_weight = lax.optimization_barrier(
+            (exchange(sum_by_tl(part), "tl"), mid, swap(act_half, "core"), grad_weight)
+        )
         part = exchange(sum_by_zh_th(part), ("zh", "th"))
         grad_input = total(part).astype(BF16)
-
-    with jax.named_scope("grad_weight"):
-        grad_weight = tn_dot(tokens, grad_rows).astype(BF16)
 
     with jax.named_scope("grad_factor"):
         cross = jnp.where(away & 2 == 0, cross, mid)
@@ -170,8 +171,6 @@
         grad_factor = tn_dot(grad_rows, cross) / 1024.0
 
     with jax.named_scope("act_factor"):
-        act_half = jnp.where(yl == zh, act_half, from_y)
-        act_rest = swap(act_half, "core")
         act_rows = cols_of(tokens, tok * 128, 128)
         act_factor = tn_dot(rows_of(act_rows, core * 512, 512), act_half)
         act_factor += tn_dot(rows_of(act_rows, (1 - core) * 512, 512), act_rest)

time: 221 us -> 217 us (0.982)
  waiting for transfers between devices: 74.3 us -> 62.5 us
  starting transfers between devices: 54.3 us -> 60.5 us
    ppermute x3, waiting for transfers between devices: 37.1 us -> 24.7 us  [send_along(): return lax.ppermute(value, IN + TOK, pairs)]
    ppermute x4, starting transfers between devices: 24.9 us -> 31.2 us  [swap(): return lax.ppermute(value, axis, [(0, 1), (1, 0)])]
  transfers between devices with their start and end apart: 11 -> 11, of which waited for: 7 -> 7; matrix products, arithmetic and copies ran while one was open for 8% -> 9% of each run, Pallas kernels for 0% -> 0%
where the time goes in v10:
time: 217 us; the launch traced here: 216 us
  waiting for transfers between devices  62.5 us (29%)
  starting transfers between devices  60.5 us (28%)
  blocking collectives  55.8 us (26%)
  matrix products  15.2 us (7%)
  other arithmetic  11.8 us (5%)
  local copies, waits for them, and re-layouts  6.51 us (3%)
  Pallas kernels  2.45 us (1%)
    all_gather x2, blocking collectives, gather_scaled(): return lax.all_gather(scaled, axis, axis=0, tiled=True)  34.8 us
    ppermute x4, starting transfers between devices, swap(): return lax.ppermute(value, axis, [(0, 1), (1, 0)])  31.2 us
    all_to_all x4, starting transfers between devices, exchange(): return lax.all_to_all(value, axis, split_axis=0, concat_axis=0, tiled=True)  25 us
    ppermute x3, waiting for transfers between devices, send_along(): return lax.ppermute(value, IN + TOK, pairs)  24.7 us
    all_to_all x4, waiting for transfers between devices, exchange(): return lax.all_to_all(value, axis, split_axis=0, concat_axis=0, tiled=True)  21.4 us
    all_to_all x1, blocking collectives, exchange(): return lax.all_to_all(value, axis, split_axis=0, concat_axis=0, tiled=True)  21.1 us
    ppermute x4, waiting for transfers between devices, swap(): return lax.ppermute(value, axis, [(0, 1), (1, 0)])  16.4 us
    dot_general x4, matrix products, tn_dot(): lax.dot_general(left, right, (((0,), (0,)), ((), ())), preferred_element_...  10.4 us
  transfers between devices with their start and end apart: 11, of which 7 were waited for; matrix products, arithmetic and copies ran while one was open for 9% of the time, Pallas kernels for 0%

profile of v10, /device:TPU:8, one launch (start us, length us, event | category | flops | bytes accessed | tf_op | source)
XLA Modules:
  0.0 215.8 jit_solution(6032446054666403433)
XLA Ops:
  0.7 0.9 copy-done
  1.6 1.0 fusion.17
  2.6 9.1 %collective-permute-start = (bf16[64,1024]{1,0:T(8,128)(2,1)S(1)}, bf16[64,1024]{1,0:T(8,128)(2,1)S(1)}, u32[]{:S(2)}, u32[]{:S(2)}) collective-permute-start(bf16[64,1024]{1,0:T(8,128)(2,1)S(1)} %pad_maximum_fusion.1), channel_id=1, source_target_pairs={{0,4},{4,0},{1,5},{5,1},{2,6},{6,2},{3,7},{7,3},{8,12},{12,8},{9,1... | collective-permute-start | bytes 393224 | tf_op jit(solution)/shard_map/gather_quarter/ppermute | solution.py:30
  11.7 1.0 dynamic_slice.25
  12.8 10.8 %collective-permute-done = bf16[64,1024]{1,0:T(8,128)(2,1)S(1)} collective-permute-done((bf16[64,1024]{1,0:T(8,128)(2,1)S(1)}, bf16[64,1024]{1,0:T(8,128)(2,1)S(1)}, u32[]{:S(2)}, u32[]{:S(2)}) %collective-permute-start) | collective-permute-done | bytes 131104 | tf_op jit(solution)/shard_map/gather_quarter/ppermute | solution.py:30
  23.8 0.1 copy.12
  24.1 21.1 %all_to_all.25 = bf16[4,80,1024]{2,1,0:T(8,128)(2,1)S(1)} all-to-all(bf16[4,80,1024]{2,1,0:T(8,128)(2,1)S(1)} %pad_maximum_fusion), channel_id=1, replica_groups=mesh['yh'=2,'yl'=2,'core'=2,'zh'=2,'x'=4,'th'=2,'tl'=4] {'tl'}, dimensions={0} | all-to-all | bytes 1310720 | tf_op jit(solution)/shard_map/gather_quarter/all_to_all | solution.py:39
  45.2 0.1 multiply_convert_fusion.2
  45.4 0.6 copy-done.4
  46.0 21.7 %all-gather.2 = f16[1024,1024]{1,0:T(8,128)(2,1)S(1)} all-gather(f16[256,1024]{1,0:T(8,128)(2,1)S(1)} %bitcast.35), channel_id=1, replica_groups=mesh['yh'=2,'yl'=2,'core'=2,'zh'=2,'x'=4,'th'=2,'tl'=4] {'x'}, dimensions={0}, use_global_device_ids=true | all-gather | bytes 2621440 | tf_op jit(solution)/shard_map/gather_tokens/all_gather | solution.py:60
  67.8 2.2 %convolution_convert_fusion.1 = f16[1024,512]{1,0:T(8,128)(2,1)} fusion(bf16[1024,512]{1,0:T(8,128)(2,1)S(1)} %copy-done.5, f16[1024,1024]{1,0:T(8,128)(2,1)S(1)} %all-gather.2), kind=kOutput, calls=%fused_computation.5 | convolution fusion | flops 1077411840 | bytes 4194304 | tf_op jit(solution)/shard_map/preact/dot_general | solution.py:135
  70.0 4.9 %all-to-all-start.1 = ((f16[8,128,512]{2,1,0:T(8,128)(2,1)}), f16[8,128,512]{2,1,0:T(8,128)(2,1)S(1)}, u32[]{:S(2)}, u32[]{:S(2)}) async-start(f16[8,128,512]{2,1,0:T(8,128)(2,1)} %bitcast.38), calls=%async_computation.1 | async-start | bytes 2097152 | tf_op jit(solution)/shard_map/preact/all_to_all | solution.py:39
  74.9 0.6 multiply_convert_fusion
  75.5 1.3 copy-done.2
  76.8 0.8 dynamic_slice.26
  77.6 2.0 collective-permute-start.1
  79.8 0.9 slice_convert_fusion
  80.7 0.2 reshape.75
  81.0 0.6 collective-permute-done.1
  81.6 7.8 %all-to-all-done.1 = f16[8,128,512]{2,1,0:T(8,128)(2,1)S(1)} async-done(((f16[8,128,512]{2,1,0:T(8,128)(2,1)}), f16[8,128,512]{2,1,0:T(8,128)(2,1)S(1)}, u32[]{:S(2)}, u32[]{:S(2)}) %all-to-all-start.1) | async-done | bytes 1048608 | tf_op jit(solution)/shard_map/preact/all_to_all | solution.py:39
  89.4 0.1 convert_reduce_fusion
  89.5 0.2 multiply_convert_fusion.3
  89.7 13.1 %all-gather.3 = f16[1024,512]{1,0:T(8,128)(2,1)S(1)} all-gather(f16[128,512]{1,0:T(8,128)(2,1)S(1)} %multiply_convert_fusion.3), channel_id=1, replica_groups=mesh['yh'=2,'yl'=2,'core'=2,'zh'=2,'x'=4,'th'=2,'tl'=4] {'yh','yl','core'}, dimensions={0}, use_global_device_ids=true | all-gather | bytes 1179648 | tf_op jit(solution)/shard_map/gather_grad/all_gather | solution.py:60
  102.8 2.6 %convert_bitcast_fusion = bf16[4,1024,256]{2,1,0:T(8,128)(2,1)} fusion(bf16[4,256,512]{2,1,0:T(8,128)(2,1)S(1)} %bitcast.39, f16[1024,512]{1,0:T(8,128)(2,1)S(1)} %all-gather.3), kind=kOutput, calls=%fused_computation.1 | convolution fusion | flops 1076363264 | bytes 4194304 | tf_op jit(solution)/shard_map/grad_input/rc,kfc->krf/dot_general | solution.py:156
  105.4 3.6 %all-to-all-start.2 = ((bf16[4,1024,256]{2,1,0:T(8,128)(2,1)}), bf16[4,1024,256]{2,1,0:T(8,128)(2,1)S(1)}, u32[]{:S(2)}, u32[]{:S(2)}) async-start(bf16[4,1024,256]{2,1,0:T(8,128)(2,1)} %convert_bitcast_fusion), calls=%async_computation.2 | async-start | bytes 4194304 | tf_op jit(solution)/shard_map/grad_input/all_to_all | solution.py:39
  109.1 1.2 multiply_convert_fusion.1
  110.2 1.6 collective-permute-start.2
  111.9 2.0 dynamic-slice_select_fusion
  113.8 11.8 %collective-permute-start.3 = (bf16[512,512]{1,0:T(8,128)(2,1)}, bf16[512,512]{1,0:T(8,128)(2,1)}, u32[]{:S(2)}, u32[]{:S(2)}) collective-permute-start(bf16[512,512]{1,0:T(8,128)(2,1)} %dynamic-slice_select_fusion), channel_id=1, source_target_pairs={{0,128},{128,0},{1,129},{129,1},{2,130},{130,2},{3,131},{131,3},{4... | collective-permute-start | bytes 1572872 | tf_op jit(solution)/shard_map/act_columns/ppermute | solution.py:30
  125.7 2.5 %broadcast_select_fusion.1 = bf16[1024,512]{1,0:T(8,128)(2,1)} fusion(bf16[1024,512]{1,0:T(8,128)(2,1)} %collective-permute-done.2, pred[]{:T(512)S(6)} %eq.22, f16[1024,512]{1,0:T(8,128)(2,1)S(1)} %all-gather.3), kind=kLoop, calls=%fused_computation.14 | loop fusion | flops 2097152 | bytes 3145729 | tf_op jit(solution)/shard_map/factor_columns/jit(_where)/select_n | solution.py:148
  128.2 4.9 %collective-permute-done.3 = bf16[512,512]{1,0:T(8,128)(2,1)} collective-permute-done((bf16[512,512]{1,0:T(8,128)(2,1)}, bf16[512,512]{1,0:T(8,128)(2,1)}, u32[]{:S(2)}, u32[]{:S(2)}) %collective-permute-start.3) | collective-permute-done | bytes 524320 | tf_op jit(solution)/shard_map/act_columns/ppermute | solution.py:30
  133.2 3.0 %all-to-all-done.2 = bf16[4,1024,256]{2,1,0:T(8,128)(2,1)S(1)} async-done(((bf16[4,1024,256]{2,1,0:T(8,128)(2,1)}), bf16[4,1024,256]{2,1,0:T(8,128)(2,1)S(1)}, u32[]{:S(2)}, u32[]{:S(2)}) %all-to-all-start.2) | async-done | bytes 2097184 | tf_op jit(solution)/shard_map/grad_input/all_to_all | solution.py:39
  136.1 1.7 grad_input.2
  137.8 3.5 %all-to-all-start.3 = ((bf16[4,16,16,256]{3,2,1,0:T(8,128)(2,1)}), bf16[4,16,16,256]{3,2,1,0:T(8,128)(2,1)S(1)}, u32[]{:S(2)}, u32[]{:S(2)}) async-start(bf16[4,16,16,256]{3,2,1,0:T(8,128)(2,1)} %grad_input.2), calls=%async_computation.3 | async-start | bytes 1048576 | tf_op jit(solution)/shard_map/grad_input/all_to_all | solution.py:39
  141.3 1.3 collective-permute-start.4
  142.6 1.1 broadcast_select_fusion.2
  143.7 8.2 %collective-permute-start.5 = (bf16[512,512]{1,0:T(8,128)(2,1)S(1)}, bf16[512,512]{1,0:T(8,128)(2,1)}, u32[]{:S(2)}, u32[]{:S(2)}) collective-permute-start(bf16[512,512]{1,0:T(8,128)(2,1)S(1)} %broadcast_select_fusion.2), channel_id=1, source_target_pairs={{0,64},{64,0},{1,65},{65,1},{2,66},{66,2},{3,67},{67,3},{4,68},{68... | collective-permute-start | bytes 1572872 | tf_op jit(solution)/shard_map/grad_input/ppermute | solution.py:30
  151.9 3.9 %convolution_convert_fusion = bf16[1024,512]{1,0:T(8,128)(2,1)} fusion(f16[1024,512]{1,0:T(8,128)(2,1)S(1)} %all-gather.3, f16[1024,1024]{1,0:T(8,128)(2,1)} %copy-done.1), kind=kOutput, calls=%fused_computation.4 | convolution fusion | flops 1078984704 | bytes 4194304 | tf_op jit(solution)/shard_map/grad_input/dot_general | solution.py:68
  155.9 24.7 %collective-permute-done.4 = bf16[1024,512]{1,0:T(8,128)(2,1)} collective-permute-done((bf16[1024,512]{1,0:T(8,128)(2,1)}, bf16[1024,512]{1,0:T(8,128)(2,1)}, u32[]{:S(2)}, u32[]{:S(2)}) %collective-permute-start.4) | collective-permute-done | bytes 1048608 | tf_op jit(solution)/shard_map/grad_input/ppermute | solution.py:35
  180.6 2.3 %broadcast_select_fusion = bf16[1024,512]{1,0:T(8,128)(2,1)} fusion(bf16[1024,512]{1,0:T(8,128)(2,1)S(1)} %copy-done.3, bf16[1024,512]{1,0:T(8,128)(2,1)} %collective-permute-done.4, pred[]{:T(512)S(6)} %eq.26), kind=kLoop, calls=%fused_computation.12 | loop fusion | flops 524288 | bytes 3145729 | tf_op jit(solution)/shard_map/grad_factor/jit(_where)/select_n | solution.py:168
  182.9 1.3 collective-permute-start.6
  184.3 0.8 grad_input.3
  185.1 13.0 %all-to-all-start.4 = ((bf16[4,128,128]{2,1,0:T(8,128)(2,1)}), bf16[4,128,128]{2,1,0:T(8,128)(2,1)S(1)}, u32[]{:S(2)}, u32[]{:S(2)}) async-start(bf16[4,128,128]{2,1,0:T(8,128)(2,1)} %bitcast.17), calls=%async_computation.4 | async-start | bytes 262144 | tf_op jit(solution)/shard_map/grad_input/all_to_all | solution.py:39
  198.1 1.5 fusion.14
  199.5 2.0 fusion
  201.5 10.7 %all-to-all-done.4 = bf16[4,128,128]{2,1,0:T(8,128)(2,1)S(1)} async-done(((bf16[4,128,128]{2,1,0:T(8,128)(2,1)}), bf16[4,128,128]{2,1,0:T(8,128)(2,1)S(1)}, u32[]{:S(2)}, u32[]{:S(2)}) %all-to-all-start.4) | async-done | bytes 131104 | tf_op jit(solution)/shard_map/grad_input/all_to_all | solution.py:39
  212.2 0.6 reduce_sum.22
  212.8 3.0 %convolution_multiply_fusion = f32[512,512]{1,0:T(8,128)} fusion(bf16[1024,512]{1,0:T(8,128)(2,1)} %broadcast_select_fusion, bf16[1024,512]{1,0:T(8,128)(2,1)S(1)} %collective-permute-done.6, pred[]{:T(512)S(6)} %eq.25, f16[1024,512]{1,0:T(8,128)(2,1)S(1)} %all-gather.3), kind=kOutput, calls=%fused_computation.6 | convolution fusion | flops 539230208 | bytes 4194305 | tf_op jit(solution)/shard_map/grad_factor/dot_general | solution.py:68
  (33 shorter events, 0.7 us)
Async XLA Ops:
  0.6 1.0 copy-start
  2.6 21.0 %collective-permute-start = (bf16[64,1024]{1,0:T(8,128)(2,1)S(1)}, bf16[64,1024]{1,0:T(8,128)(2,1)S(1)}, u32[]{:S(2)}, u32[]{:S(2)}) collective-permute-start(bf16[64,1024]{1,0:T(8,128)(2,1)S(1)} %pad_maximum_fusion.1), channel_id=1, source_target_pairs={{0,4},{4,0},{1,5},{5,1},{2,6},{6,2},{3,7},{7,3},{8,12},{12,8},{9,1... | collective-permute-start | bytes 393224 | tf_op jit(solution)/shard_map/gather_quarter/ppermute | solution.py:30
  45.2 0.8 copy-start.4
  45.3 22.4 %copy-start.5 = (bf16[1024,512]{1,0:T(8,128)(2,1)S(1)}, bf16[1024,512]{1,0:T(8,128)(2,1)}, u32[]{:S(2)}) copy-start(bf16[1024,512]{1,0:T(8,128)(2,1)} %param.4) | copy-start | bytes 3145732
  67.7 7.1 %copy-start.1 = (f16[1024,1024]{1,0:T(8,128)(2,1)}, f16[1024,1024]{1,0:T(8,128)(2,1)S(1)}, u32[]{:S(2)}) copy-start(f16[1024,1024]{1,0:T(8,128)(2,1)S(1)} %all-gather.2) | copy-start | bytes 6291460
  70.0 19.4 %all-to-all-start.1 = ((f16[8,128,512]{2,1,0:T(8,128)(2,1)}), f16[8,128,512]{2,1,0:T(8,128)(2,1)S(1)}, u32[]{:S(2)}, u32[]{:S(2)}) async-start(f16[8,128,512]{2,1,0:T(8,128)(2,1)} %bitcast.38), calls=%async_computation.1 | async-start | bytes 2097152 | tf_op jit(solution)/shard_map/preact/all_to_all | solution.py:39
  74.9 4.8 %copy-start.6 = (bf16[1024,512]{1,0:T(8,128)(2,1)S(1)}, bf16[1024,512]{1,0:T(8,128)(2,1)}, u32[]{:S(2)}) copy-start(bf16[1024,512]{1,0:T(8,128)(2,1)} %param.4) | copy-start | bytes 3145732
  75.5 1.3 copy-start.2
  77.6 4.0 %collective-permute-start.1 = (bf16[512,512]{1,0:T(8,128)(2,1)}, bf16[512,512]{1,0:T(8,128)(2,1)S(1)}, u32[]{:S(2)}, u32[]{:S(2)}) collective-permute-start(bf16[512,512]{1,0:T(8,128)(2,1)} %dynamic_slice.26), channel_id=1, source_target_pairs={{0,64},{64,0},{1,65},{65,1},{2,66},{66,2},{3,67},{67,3},{4,68},{68... | collective-permute-start | bytes 1572872 | tf_op jit(solution)/shard_map/act_columns/ppermute | solution.py:30
  81.6 23.8 %copy-start.7 = (bf16[512,512]{1,0:T(8,128)(2,1)}, bf16[512,512]{1,0:T(8,128)(2,1)S(1)}, u32[]{:S(2)}) copy-start(bf16[512,512]{1,0:T(8,128)(2,1)S(1)} %collective-permute-done.1) | copy-start | bytes 1572868
  105.4 30.7 %all-to-all-start.2 = ((bf16[4,1024,256]{2,1,0:T(8,128)(2,1)}), bf16[4,1024,256]{2,1,0:T(8,128)(2,1)S(1)}, u32[]{:S(2)}, u32[]{:S(2)}) async-start(bf16[4,1024,256]{2,1,0:T(8,128)(2,1)} %convert_bitcast_fusion), calls=%async_computation.2 | async-start | bytes 4194304 | tf_op jit(solution)/shard_map/grad_input/all_to_all | solution.py:39
  110.2 15.5 %collective-permute-start.2 = (bf16[1024,512]{1,0:T(8,128)(2,1)}, bf16[1024,512]{1,0:T(8,128)(2,1)}, u32[]{:S(2)}, u32[]{:S(2)}) collective-permute-start(bf16[1024,512]{1,0:T(8,128)(2,1)} %multiply_convert_fusion.1), channel_id=1, source_target_pairs={{0,4},{65,69},{130,134},{195,199},{260,256},{325,321},{390,386},{4... | collective-permute-start | bytes 3145736 | tf_op jit(solution)/shard_map/factor_columns/ppermute | solution.py:35
  113.8 19.3 %collective-permute-start.3 = (bf16[512,512]{1,0:T(8,128)(2,1)}, bf16[512,512]{1,0:T(8,128)(2,1)}, u32[]{:S(2)}, u32[]{:S(2)}) collective-permute-start(bf16[512,512]{1,0:T(8,128)(2,1)} %dynamic-slice_select_fusion), channel_id=1, source_target_pairs={{0,128},{128,0},{1,129},{129,1},{2,130},{130,2},{3,131},{131,3},{4... | collective-permute-start | bytes 1572872 | tf_op jit(solution)/shard_map/act_columns/ppermute | solution.py:30
  137.8 42.8 %all-to-all-start.3 = ((bf16[4,16,16,256]{3,2,1,0:T(8,128)(2,1)}), bf16[4,16,16,256]{3,2,1,0:T(8,128)(2,1)S(1)}, u32[]{:S(2)}, u32[]{:S(2)}) async-start(bf16[4,16,16,256]{3,2,1,0:T(8,128)(2,1)} %grad_input.2), calls=%async_computation.3 | async-start | bytes 1048576 | tf_op jit(solution)/shard_map/grad_input/all_to_all | solution.py:39
  141.3 39.3 %collective-permute-start.4 = (bf16[1024,512]{1,0:T(8,128)(2,1)}, bf16[1024,512]{1,0:T(8,128)(2,1)}, u32[]{:S(2)}, u32[]{:S(2)}) collective-permute-start(bf16[1024,512]{1,0:T(8,128)(2,1)} %broadcast_select_fusion.1), channel_id=1, source_target_pairs={{0,2},{4,6},{65,67},{69,71},{130,128},{134,132},{195,193},{199,197... | collective-permute-start | bytes 3145736 | tf_op jit(solution)/shard_map/grad_input/ppermute | solution.py:35
  143.7 12.2 %collective-permute-start.5 = (bf16[512,512]{1,0:T(8,128)(2,1)S(1)}, bf16[512,512]{1,0:T(8,128)(2,1)}, u32[]{:S(2)}, u32[]{:S(2)}) collective-permute-start(bf16[512,512]{1,0:T(8,128)(2,1)S(1)} %broadcast_select_fusion.2), channel_id=1, source_target_pairs={{0,64},{64,0},{1,65},{65,1},{2,66},{66,2},{3,67},{67,3},{4,68},{68... | collective-permute-start | bytes 1572872 | tf_op jit(solution)/shard_map/grad_input/ppermute | solution.py:30
  151.9 28.7 %copy-start.3 = (bf16[1024,512]{1,0:T(8,128)(2,1)S(1)}, bf16[1024,512]{1,0:T(8,128)(2,1)}, u32[]{:S(2)}) copy-start(bf16[1024,512]{1,0:T(8,128)(2,1)} %broadcast_select_fusion.1) | copy-start | bytes 3145732
  182.9 30.0 %collective-permute-start.6 = (bf16[1024,512]{1,0:T(8,128)(2,1)}, bf16[1024,512]{1,0:T(8,128)(2,1)S(1)}, u32[]{:S(2)}, u32[]{:S(2)}) collective-permute-start(bf16[1024,512]{1,0:T(8,128)(2,1)} %broadcast_select_fusion), channel_id=1, source_target_pairs={{0,1},{2,3},{4,5},{6,7},{65,64},{67,66},{69,68},{71,70},{130,131},... | collective-permute-start | bytes 3145736 | tf_op jit(solution)/shard_map/grad_factor/ppermute | solution.py:35
  185.1 27.2 %all-to-all-start.4 = ((bf16[4,128,128]{2,1,0:T(8,128)(2,1)}), bf16[4,128,128]{2,1,0:T(8,128)(2,1)S(1)}, u32[]{:S(2)}, u32[]{:S(2)}) async-start(bf16[4,128,128]{2,1,0:T(8,128)(2,1)} %bitcast.17), calls=%async_computation.4 | async-start | bytes 262144 | tf_op jit(solution)/shard_map/grad_input/all_to_all | solution.py:39

commit v11 on v10

--- a/solution.py
+++ b/solution.py
@@ -30,8 +30,13 @@
     return lax.ppermute(value, axis, [(0, 1), (1, 0)])
 
 
-def send_along(value, bit, holders):
-    pairs = [(i * 8 + (i ^ h), i * 8 + (i ^ h ^ bit)) for i in range(8) for h in holders]
+def send_along(value, bits, before):
+    pairs = []
+    for i in range(8):
+        holders = [0]
+        for done in before:
+            holders += [h ^ done[i % 2] for h in holders]
+        pairs += [(i * 8 + (i ^ h), i * 8 + (i ^ h ^ bits[i % 2])) for h in holders]
     return lax.ppermute(value, IN + TOK, pairs)
 
 
@@ -144,7 +149,7 @@
 
     with jax.named_scope("factor_columns"):
         away = tok ^ piece
-        far = send_along(grad_rows, 4, (0,))
+        far = send_along(grad_rows, (4, 4), ())
         cross = jnp.where(away == 0, grad_rows, far)
 
     with jax.named_scope("act_columns"):
@@ -155,7 +160,7 @@
         by_x = weight.reshape(2, 4, 128, 512).transpose(1, 0, 2, 3).reshape(4, 256, 512)
         share = jnp.einsum("rc,kfc->krf", grad_rows, by_x, preferred_element_type=F32).astype(BF16)
         part, cross, from_y = lax.optimization_barrier((exchange(share, "x"), cross, from_y))
-        mid = send_along(cross, 2, (0, 4))
+        mid = send_along(cross, (2, 1), ((4, 4),))
         act_half = jnp.where(yl == zh, act_half, from_y)
         grad_weight = tn_dot(tokens, grad_rows).astype(BF16)
         part, mid, act_rest, grad_weight = lax.optimization_barrier(
@@ -165,9 +170,9 @@
         grad_input = total(part).astype(BF16)
 
     with jax.named_scope("grad_factor"):
-        cross = jnp.where(away & 2 == 0, cross, mid)
-        near = send_along(cross, 1, (0, 2, 4, 6))
-        cross = jnp.where(away & 1 == 0, cross, near)
+        cross = jnp.where(away & (2 - core) == 0, cross, mid)
+        near = send_along(cross, (1, 2), ((4, 4), (2, 1)))
+        cross = jnp.where(away & (1 + core) == 0, cross, near)
         grad_factor = tn_dot(grad_rows, cross) / 1024.0
 
     with jax.named_scope("act_factor"):

time: 217 us -> 224 us (1.032)
  the two profiles are of different devices: /device:TPU:8 before, /device:TPU:28 now
where the time goes in v11:
time: 224 us; the launch traced here: 223 us
  waiting for transfers between devices  74.8 us (33%)
  starting transfers between devices  56.5 us (25%)
  blocking collectives  54.9 us (25%)
  matrix products  15.2 us (7%)
  other arithmetic  12 us (5%)
  local copies, waits for them, and re-layouts  6.51 us (3%)
  Pallas kernels  2.45 us (1%)
    all_to_all x4, starting transfers between devices, exchange(): return lax.all_to_all(value, axis, split_axis=0, concat_axis=0, tiled=True)  36.4 us
    all_gather x2, blocking collectives, gather_scaled(): return lax.all_gather(scaled, axis, axis=0, tiled=True)  33.8 us
    ppermute x3, waiting for transfers between devices, send_along(): return lax.ppermute(value, IN + TOK, pairs)  32.2 us
    ppermute x4, waiting for transfers between devices, swap(): return lax.ppermute(value, axis, [(0, 1), (1, 0)])  22.1 us
    all_to_all x1, blocking collectives, exchange(): return lax.all_to_all(value, axis, split_axis=0, concat_axis=0, tiled=True)  21.1 us
    all_to_all x4, waiting for transfers between devices, exchange(): return lax.all_to_all(value, axis, split_axis=0, concat_axis=0, tiled=True)  20.5 us
    ppermute x4, starting transfers between devices, swap(): return lax.ppermute(value, axis, [(0, 1), (1, 0)])  15.8 us
    dot_general x4, matrix products, tn_dot(): lax.dot_general(left, right, (((0,), (0,)), ((), ())), preferred_element_...  10.4 us
  transfers between devices with their start and end apart: 11, of which 7 were waited for; matrix products, arithmetic and copies ran while one was open for 8% of the time, Pallas kernels for 0%

profile of v11, /device:TPU:28, one launch (start us, length us, event | category | flops | bytes accessed | tf_op | source)
XLA Modules:
  0.0 223.3 jit_solution(9060355887877410446)
XLA Ops:
  0.7 0.9 copy-done
  1.6 1.0 fusion.17
  2.6 9.1 %collective-permute-start = (bf16[64,1024]{1,0:T(8,128)(2,1)S(1)}, bf16[64,1024]{1,0:T(8,128)(2,1)S(1)}, u32[]{:S(2)}, u32[]{:S(2)}) collective-permute-start(bf16[64,1024]{1,0:T(8,128)(2,1)S(1)} %pad_maximum_fusion.1), channel_id=1, source_target_pairs={{0,4},{4,0},{1,5},{5,1},{2,6},{6,2},{3,7},{7,3},{8,12},{12,8},{9,1... | collective-permute-start | bytes 393224 | tf_op jit(solution)/shard_map/gather_quarter/ppermute | solution.py:30
  11.7 1.0 dynamic_slice.25
  12.8 10.8 %collective-permute-done = bf16[64,1024]{1,0:T(8,128)(2,1)S(1)} collective-permute-done((bf16[64,1024]{1,0:T(8,128)(2,1)S(1)}, bf16[64,1024]{1,0:T(8,128)(2,1)S(1)}, u32[]{:S(2)}, u32[]{:S(2)}) %collective-permute-start) | collective-permute-done | bytes 131104 | tf_op jit(solution)/shard_map/gather_quarter/ppermute | solution.py:30
  23.7 0.1 copy.12
  24.1 21.1 %all_to_all.25 = bf16[4,80,1024]{2,1,0:T(8,128)(2,1)S(1)} all-to-all(bf16[4,80,1024]{2,1,0:T(8,128)(2,1)S(1)} %pad_maximum_fusion), channel_id=1, replica_groups=mesh['yh'=2,'yl'=2,'core'=2,'zh'=2,'x'=4,'th'=2,'tl'=4] {'tl'}, dimensions={0} | all-to-all | bytes 1310720 | tf_op jit(solution)/shard_map/gather_quarter/all_to_all | solution.py:44
  45.2 0.1 multiply_convert_fusion.2
  45.4 0.6 copy-done.4
  46.0 20.1 %all-gather.2 = f16[1024,1024]{1,0:T(8,128)(2,1)S(1)} all-gather(f16[256,1024]{1,0:T(8,128)(2,1)S(1)} %bitcast.35), channel_id=1, replica_groups=mesh['yh'=2,'yl'=2,'core'=2,'zh'=2,'x'=4,'th'=2,'tl'=4] {'x'}, dimensions={0}, use_global_device_ids=true | all-gather | bytes 2621440 | tf_op jit(solution)/shard_map/gather_tokens/all_gather | solution.py:65
  66.1 2.2 convolution_convert_fusion.1
  68.4 4.7 %all-to-all-start.1 = ((f16[8,128,512]{2,1,0:T(8,128)(2,1)}), f16[8,128,512]{2,1,0:T(8,128)(2,1)S(1)}, u32[]{:S(2)}, u32[]{:S(2)}) async-start(f16[8,128,512]{2,1,0:T(8,128)(2,1)} %bitcast.38), calls=%async_computation.1 | async-start | bytes 2097152 | tf_op jit(solution)/shard_map/preact/all_to_all | solution.py:44
  73.1 0.6 multiply_convert_fusion
  73.7 1.3 copy-done.2
  75.0 0.8 dynamic_slice.26
  75.8 2.0 collective-permute-start.1
  78.0 0.9 slice_convert_fusion
  79.0 0.2 reshape.75
  79.2 0.6 collective-permute-done.1
  79.9 7.1 %all-to-all-done.1 = f16[8,128,512]{2,1,0:T(8,128)(2,1)S(1)} async-done(((f16[8,128,512]{2,1,0:T(8,128)(2,1)}), f16[8,128,512]{2,1,0:T(8,128)(2,1)S(1)}, u32[]{:S(2)}, u32[]{:S(2)}) %all-to-all-start.1) | async-done | bytes 1048608 | tf_op jit(solution)/shard_map/preact/all_to_all | solution.py:44
  87.0 0.1 convert_reduce_fusion
  87.1 0.2 multiply_convert_fusion.3
  87.3 13.7 %all-gather.3 = f16[1024,512]{1,0:T(8,128)(2,1)S(1)} all-gather(f16[128,512]{1,0:T(8,128)(2,1)S(1)} %multiply_convert_fusion.3), channel_id=1, replica_groups=mesh['yh'=2,'yl'=2,'core'=2,'zh'=2,'x'=4,'th'=2,'tl'=4] {'yh','yl','core'}, dimensions={0}, use_global_device_ids=true | all-gather | bytes 1179648 | tf_op jit(solution)/shard_map/gather_grad/all_gather | solution.py:65
  101.0 2.6 %convert_bitcast_fusion = bf16[4,1024,256]{2,1,0:T(8,128)(2,1)} fusion(bf16[4,256,512]{2,1,0:T(8,128)(2,1)S(1)} %bitcast.39, f16[1024,512]{1,0:T(8,128)(2,1)S(1)} %all-gather.3), kind=kOutput, calls=%fused_computation.1 | convolution fusion | flops 1076363264 | bytes 4194304 | tf_op jit(solution)/shard_map/grad_input/rc,kfc->krf/dot_general | solution.py:161
  103.7 5.6 %all-to-all-start.2 = ((bf16[4,1024,256]{2,1,0:T(8,128)(2,1)}), bf16[4,1024,256]{2,1,0:T(8,128)(2,1)S(1)}, u32[]{:S(2)}, u32[]{:S(2)}) async-start(bf16[4,1024,256]{2,1,0:T(8,128)(2,1)} %convert_bitcast_fusion), calls=%async_computation.2 | async-start | bytes 4194304 | tf_op jit(solution)/shard_map/grad_input/all_to_all | solution.py:44
  109.3 1.2 multiply_convert_fusion.1
  110.5 1.6 collective-permute-start.2
  112.1 2.1 dynamic-slice_select_fusion
  114.2 2.7 %collective-permute-start.3 = (bf16[512,512]{1,0:T(8,128)(2,1)}, bf16[512,512]{1,0:T(8,128)(2,1)}, u32[]{:S(2)}, u32[]{:S(2)}) collective-permute-start(bf16[512,512]{1,0:T(8,128)(2,1)} %dynamic-slice_select_fusion), channel_id=1, source_target_pairs={{0,128},{128,0},{1,129},{129,1},{2,130},{130,2},{3,131},{131,3},{4... | collective-permute-start | bytes 1572872 | tf_op jit(solution)/shard_map/act_columns/ppermute | solution.py:30
  117.0 2.5 %broadcast_select_fusion.1 = bf16[1024,512]{1,0:T(8,128)(2,1)} fusion(bf16[1024,512]{1,0:T(8,128)(2,1)} %collective-permute-done.2, pred[]{:T(512)S(6)} %eq.22, f16[1024,512]{1,0:T(8,128)(2,1)S(1)} %all-gather.3), kind=kLoop, calls=%fused_computation.14 | loop fusion | flops 2097152 | bytes 3145729 | tf_op jit(solution)/shard_map/factor_columns/jit(_where)/select_n | solution.py:153
  119.5 10.7 %collective-permute-done.3 = bf16[512,512]{1,0:T(8,128)(2,1)} collective-permute-done((bf16[512,512]{1,0:T(8,128)(2,1)}, bf16[512,512]{1,0:T(8,128)(2,1)}, u32[]{:S(2)}, u32[]{:S(2)}) %collective-permute-start.3) | collective-permute-done | bytes 524320 | tf_op jit(solution)/shard_map/act_columns/ppermute | solution.py:30
  130.2 3.3 %all-to-all-done.2 = bf16[4,1024,256]{2,1,0:T(8,128)(2,1)S(1)} async-done(((bf16[4,1024,256]{2,1,0:T(8,128)(2,1)}), bf16[4,1024,256]{2,1,0:T(8,128)(2,1)S(1)}, u32[]{:S(2)}, u32[]{:S(2)}) %all-to-all-start.2) | async-done | bytes 2097184 | tf_op jit(solution)/shard_map/grad_input/all_to_all | solution.py:44
  133.5 1.7 grad_input.2
  135.1 13.2 %all-to-all-start.3 = ((bf16[4,16,16,256]{3,2,1,0:T(8,128)(2,1)}), bf16[4,16,16,256]{3,2,1,0:T(8,128)(2,1)S(1)}, u32[]{:S(2)}, u32[]{:S(2)}) async-start(bf16[4,16,16,256]{3,2,1,0:T(8,128)(2,1)} %grad_input.2), calls=%async_computation.3 | async-start | bytes 1048576 | tf_op jit(solution)/shard_map/grad_input/all_to_all | solution.py:44
  148.3 1.3 collective-permute-start.4
  149.6 1.1 broadcast_select_fusion.2
  150.7 1.9 collective-permute-start.5
  152.6 3.9 %convolution_convert_fusion = bf16[1024,512]{1,0:T(8,128)(2,1)} fusion(f16[1024,512]{1,0:T(8,128)(2,1)S(1)} %all-gather.3, f16[1024,1024]{1,0:T(8,128)(2,1)} %copy-done.1), kind=kOutput, calls=%fused_computation.4 | convolution fusion | flops 1078984704 | bytes 4194304 | tf_op jit(solution)/shard_map/grad_input/dot_general | solution.py:73
  156.6 32.2 %collective-permute-done.4 = bf16[1024,512]{1,0:T(8,128)(2,1)} collective-permute-done((bf16[1024,512]{1,0:T(8,128)(2,1)}, bf16[1024,512]{1,0:T(8,128)(2,1)}, u32[]{:S(2)}, u32[]{:S(2)}) %collective-permute-start.4) | collective-permute-done | bytes 1048608 | tf_op jit(solution)/shard_map/grad_input/ppermute | solution.py:40
  188.8 2.3 %broadcast_select_fusion = bf16[1024,512]{1,0:T(8,128)(2,1)} fusion(bf16[1024,512]{1,0:T(8,128)(2,1)S(1)} %copy-done.3, bf16[1024,512]{1,0:T(8,128)(2,1)} %collective-permute-done.4, pred[]{:T(512)S(6)} %eq.26), kind=kLoop, calls=%fused_computation.12 | loop fusion | flops 524288 | bytes 3145729 | tf_op jit(solution)/shard_map/grad_factor/jit(_where)/select_n | solution.py:173
  191.1 1.3 collective-permute-start.6
  192.5 0.8 grad_input.3
  193.3 12.9 %all-to-all-start.4 = ((bf16[4,128,128]{2,1,0:T(8,128)(2,1)}), bf16[4,128,128]{2,1,0:T(8,128)(2,1)S(1)}, u32[]{:S(2)}, u32[]{:S(2)}) async-start(bf16[4,128,128]{2,1,0:T(8,128)(2,1)} %bitcast.17), calls=%async_computation.4 | async-start | bytes 262144 | tf_op jit(solution)/shard_map/grad_input/all_to_all | solution.py:44
  206.2 1.5 fusion.14
  207.7 2.0 fusion
  209.7 10.1 %all-to-all-done.4 = bf16[4,128,128]{2,1,0:T(8,128)(2,1)S(1)} async-done(((bf16[4,128,128]{2,1,0:T(8,128)(2,1)}), bf16[4,128,128]{2,1,0:T(8,128)(2,1)S(1)}, u32[]{:S(2)}, u32[]{:S(2)}) %all-to-all-start.4) | async-done | bytes 131104 | tf_op jit(solution)/shard_map/grad_input/all_to_all | solution.py:44
  219.7 0.6 reduce_sum.22
  220.4 3.0 %convolution_multiply_fusion = f32[512,512]{1,0:T(8,128)} fusion(bf16[1024,512]{1,0:T(8,128)(2,1)} %broadcast_select_fusion, bf16[1024,512]{1,0:T(8,128)(2,1)S(1)} %collective-permute-done.6, pred[]{:T(512)S(6)} %eq.25, f16[1024,512]{1,0:T(8,128)(2,1)S(1)} %all-gather.3), kind=kOutput, calls=%fused_computation.6 | convolution fusion | flops 539230208 | bytes 4194305 | tf_op jit(solution)/shard_map/grad_factor/dot_general | solution.py:73
  (33 shorter events, 0.7 us)
Async XLA Ops:
  0.6 1.0 copy-start
  2.6 21.0 %collective-permute-start = (bf16[64,1024]{1,0:T(8,128)(2,1)S(1)}, bf16[64,1024]{1,0:T(8,128)(2,1)S(1)}, u32[]{:S(2)}, u32[]{:S(2)}) collective-permute-start(bf16[64,1024]{1,0:T(8,128)(2,1)S(1)} %pad_maximum_fusion.1), channel_id=1, source_target_pairs={{0,4},{4,0},{1,5},{5,1},{2,6},{6,2},{3,7},{7,3},{8,12},{12,8},{9,1... | collective-permute-start | bytes 393224 | tf_op jit(solution)/shard_map/gather_quarter/ppermute | solution.py:30
  45.2 0.8 copy-start.4
  45.3 20.9 %copy-start.5 = (bf16[1024,512]{1,0:T(8,128)(2,1)S(1)}, bf16[1024,512]{1,0:T(8,128)(2,1)}, u32[]{:S(2)}) copy-start(bf16[1024,512]{1,0:T(8,128)(2,1)} %param.4) | copy-start | bytes 3145732
  66.1 7.0 %copy-start.1 = (f16[1024,1024]{1,0:T(8,128)(2,1)}, f16[1024,1024]{1,0:T(8,128)(2,1)S(1)}, u32[]{:S(2)}) copy-start(f16[1024,1024]{1,0:T(8,128)(2,1)S(1)} %all-gather.2) | copy-start | bytes 6291460
  68.4 18.6 %all-to-all-start.1 = ((f16[8,128,512]{2,1,0:T(8,128)(2,1)}), f16[8,128,512]{2,1,0:T(8,128)(2,1)S(1)}, u32[]{:S(2)}, u32[]{:S(2)}) async-start(f16[8,128,512]{2,1,0:T(8,128)(2,1)} %bitcast.38), calls=%async_computation.1 | async-start | bytes 2097152 | tf_op jit(solution)/shard_map/preact/all_to_all | solution.py:44
  73.1 4.8 %copy-start.6 = (bf16[1024,512]{1,0:T(8,128)(2,1)S(1)}, bf16[1024,512]{1,0:T(8,128)(2,1)}, u32[]{:S(2)}) copy-start(bf16[1024,512]{1,0:T(8,128)(2,1)} %param.4) | copy-start | bytes 3145732
  73.7 1.3 copy-start.2
  75.8 4.0 %collective-permute-start.1 = (bf16[512,512]{1,0:T(8,128)(2,1)}, bf16[512,512]{1,0:T(8,128)(2,1)S(1)}, u32[]{:S(2)}, u32[]{:S(2)}) collective-permute-start(bf16[512,512]{1,0:T(8,128)(2,1)} %dynamic_slice.26), channel_id=1, source_target_pairs={{0,64},{64,0},{1,65},{65,1},{2,66},{66,2},{3,67},{67,3},{4,68},{68... | collective-permute-start | bytes 1572872 | tf_op jit(solution)/shard_map/act_columns/ppermute | solution.py:30
  79.9 23.8 %copy-start.7 = (bf16[512,512]{1,0:T(8,128)(2,1)}, bf16[512,512]{1,0:T(8,128)(2,1)S(1)}, u32[]{:S(2)}) copy-start(bf16[512,512]{1,0:T(8,128)(2,1)S(1)} %collective-permute-done.1) | copy-start | bytes 1572868
  103.7 29.8 %all-to-all-start.2 = ((bf16[4,1024,256]{2,1,0:T(8,128)(2,1)}), bf16[4,1024,256]{2,1,0:T(8,128)(2,1)S(1)}, u32[]{:S(2)}, u32[]{:S(2)}) async-start(bf16[4,1024,256]{2,1,0:T(8,128)(2,1)} %convert_bitcast_fusion), calls=%async_computation.2 | async-start | bytes 4194304 | tf_op jit(solution)/shard_map/grad_input/all_to_all | solution.py:44
  110.5 6.5 %collective-permute-start.2 = (bf16[1024,512]{1,0:T(8,128)(2,1)}, bf16[1024,512]{1,0:T(8,128)(2,1)}, u32[]{:S(2)}, u32[]{:S(2)}) collective-permute-start(bf16[1024,512]{1,0:T(8,128)(2,1)} %multiply_convert_fusion.1), channel_id=1, source_target_pairs={{0,4},{65,69},{130,134},{195,199},{260,256},{325,321},{390,386},{4... | collective-permute-start | bytes 3145736 | tf_op jit(solution)/shard_map/factor_columns/ppermute | solution.py:40
  114.2 15.9 %collective-permute-start.3 = (bf16[512,512]{1,0:T(8,128)(2,1)}, bf16[512,512]{1,0:T(8,128)(2,1)}, u32[]{:S(2)}, u32[]{:S(2)}) collective-permute-start(bf16[512,512]{1,0:T(8,128)(2,1)} %dynamic-slice_select_fusion), channel_id=1, source_target_pairs={{0,128},{128,0},{1,129},{129,1},{2,130},{130,2},{3,131},{131,3},{4... | collective-permute-start | bytes 1572872 | tf_op jit(solution)/shard_map/act_columns/ppermute | solution.py:30
  135.1 53.7 %all-to-all-start.3 = ((bf16[4,16,16,256]{3,2,1,0:T(8,128)(2,1)}), bf16[4,16,16,256]{3,2,1,0:T(8,128)(2,1)S(1)}, u32[]{:S(2)}, u32[]{:S(2)}) async-start(bf16[4,16,16,256]{3,2,1,0:T(8,128)(2,1)} %grad_input.2), calls=%async_computation.3 | async-start | bytes 1048576 | tf_op jit(solution)/shard_map/grad_input/all_to_all | solution.py:44
  148.3 40.5 %collective-permute-start.4 = (bf16[1024,512]{1,0:T(8,128)(2,1)}, bf16[1024,512]{1,0:T(8,128)(2,1)}, u32[]{:S(2)}, u32[]{:S(2)}) collective-permute-start(bf16[1024,512]{1,0:T(8,128)(2,1)} %broadcast_select_fusion.1), channel_id=1, source_target_pairs={{0,2},{4,6},{65,64},{69,68},{130,128},{134,132},{195,194},{199,198... | collective-permute-start | bytes 3145736 | tf_op jit(solution)/shard_map/grad_input/ppermute | solution.py:40
  150.7 5.9 %collective-permute-start.5 = (bf16[512,512]{1,0:T(8,128)(2,1)S(1)}, bf16[512,512]{1,0:T(8,128)(2,1)}, u32[]{:S(2)}, u32[]{:S(2)}) collective-permute-start(bf16[512,512]{1,0:T(8,128)(2,1)S(1)} %broadcast_select_fusion.2), channel_id=1, source_target_pairs={{0,64},{64,0},{1,65},{65,1},{2,66},{66,2},{3,67},{67,3},{4,68},{68... | collective-permute-start | bytes 1572872 | tf_op jit(solution)/shard_map/grad_input/ppermute | solution.py:30
  152.6 36.2 %copy-start.3 = (bf16[1024,512]{1,0:T(8,128)(2,1)S(1)}, bf16[1024,512]{1,0:T(8,128)(2,1)}, u32[]{:S(2)}) copy-start(bf16[1024,512]{1,0:T(8,128)(2,1)} %broadcast_select_fusion.1) | copy-start | bytes 3145732
  191.1 29.2 %collective-permute-start.6 = (bf16[1024,512]{1,0:T(8,128)(2,1)}, bf16[1024,512]{1,0:T(8,128)(2,1)S(1)}, u32[]{:S(2)}, u32[]{:S(2)}) collective-permute-start(bf16[1024,512]{1,0:T(8,128)(2,1)} %broadcast_select_fusion), channel_id=1, source_target_pairs={{0,1},{4,5},{2,3},{6,7},{65,67},{69,71},{64,66},{68,70},{130,131},... | collective-permute-start | bytes 3145736 | tf_op jit(solution)/shard_map/grad_factor/ppermute | solution.py:40
  193.3 26.4 %all-to-all-start.4 = ((bf16[4,128,128]{2,1,0:T(8,128)(2,1)}), bf16[4,128,128]{2,1,0:T(8,128)(2,1)S(1)}, u32[]{:S(2)}, u32[]{:S(2)}) async-start(bf16[4,128,128]{2,1,0:T(8,128)(2,1)} %bitcast.17), calls=%async_computation.4 | async-start | bytes 262144 | tf_op jit(solution)/shard_map/grad_input/all_to_all | solution.py:44

commit v12 on v10

--- a/solution.py
+++ b/solution.py
@@ -146,6 +146,7 @@
         away = tok ^ piece
         far = send_along(grad_rows, 4, (0,))
         cross = jnp.where(away == 0, grad_rows, far)
+        mid = send_along(cross, 2, (0, 4))
 
     with jax.named_scope("act_columns"):
         act_half = jnp.where(core == x // 2, act_own, act_other)
@@ -154,14 +155,13 @@
     with jax.named_scope("grad_input"):
         by_x = weight.reshape(2, 4, 128, 512).transpose(1, 0, 2, 3).reshape(4, 256, 512)
         share = jnp.einsum("rc,kfc->krf", grad_rows, by_x, preferred_element_type=F32).astype(BF16)
-        part, cross, from_y = lax.optimization_barrier((exchange(share, "x"), cross, from_y))
-        mid = send_along(cross, 2, (0, 4))
+        part, from_y = lax.optimization_barrier((exchange(share, "x"), from_y))
         act_half = jnp.where(yl == zh, act_half, from_y)
         grad_weight = tn_dot(tokens, grad_rows).astype(BF16)
-        part, mid, act_rest, grad_weight = lax.optimization_barrier(
-            (exchange(sum_by_tl(part), "tl"), mid, swap(act_half, "core"), grad_weight)
+        part, cross, act_rest, grad_weight = lax.optimization_barrier(
+            (exchange(sum_by_tl(part), "tl"), cross, swap(act_half, "core"), grad_weight)
         )
-        part = exchange(sum_by_zh_th(part), ("zh", "th"))
+        part, mid = lax.optimization_barrier((exchange(sum_by_zh_th(part), ("zh", "th")), mid))
         grad_input = total(part).astype(BF16)
 
     with jax.named_scope("grad_factor"):

time: 217 us -> 217 us (level)
  the two profiles are of different devices: /device:TPU:8 before, /device:TPU:64 now
where the time goes in v12:
time: 217 us; the launch traced here: 216 us
  waiting for transfers between devices  67.7 us (31%)
  blocking collectives  58 us (27%)
  starting transfers between devices  57.1 us (26%)
  matrix products  13.4 us (6%)
  other arithmetic  9.2 us (4%)
  local copies, waits for them, and re-layouts  6.54 us (3%)
  Pallas kernels  2.44 us (1%)
    all_to_all x4, waiting for transfers between devices, exchange(): return lax.all_to_all(value, axis, split_axis=0, concat_axis=0, tiled=True)  45.1 us
    all_gather x2, blocking collectives, gather_scaled(): return lax.all_gather(scaled, axis, axis=0, tiled=True)  35.6 us
    all_to_all x4, starting transfers between devices, exchange(): return lax.all_to_all(value, axis, split_axis=0, concat_axis=0, tiled=True)  26.5 us
    ppermute x4, starting transfers between devices, swap(): return lax.ppermute(value, axis, [(0, 1), (1, 0)])  22.7 us
    all_to_all x1, blocking collectives, exchange(): return lax.all_to_all(value, axis, split_axis=0, concat_axis=0, tiled=True)  22.4 us
    ppermute x4, waiting for transfers between devices, swap(): return lax.ppermute(value, axis, [(0, 1), (1, 0)])  14 us
    ppermute x3, waiting for transfers between devices, send_along(): return lax.ppermute(value, IN + TOK, pairs)  8.57 us
    dot_general x4, matrix products, tn_dot(): lax.dot_general(left, right, (((0,), (0,)), ((), ())), preferred_element_...  8.55 us
  transfers between devices with their start and end apart: 11, of which 8 were waited for; matrix products, arithmetic and copies ran while one was open for 7% of the time, Pallas kernels for 1%

profile of v12, /device:TPU:64, one launch (start us, length us, event | category | flops | bytes accessed | tf_op | source)
XLA Modules:
  0.0 215.5 jit_solution(14571187998745693081)
XLA Ops:
  0.7 0.9 copy-done
  1.6 1.0 fusion.17
  2.6 9.1 %collective-permute-start = (bf16[64,1024]{1,0:T(8,128)(2,1)S(1)}, bf16[64,1024]{1,0:T(8,128)(2,1)S(1)}, u32[]{:S(2)}, u32[]{:S(2)}) collective-permute-start(bf16[64,1024]{1,0:T(8,128)(2,1)S(1)} %pad_maximum_fusion.1), channel_id=1, source_target_pairs={{0,4},{4,0},{1,5},{5,1},{2,6},{6,2},{3,7},{7,3},{8,12},{12,8},{9,1... | collective-permute-start | bytes 393224 | tf_op jit(solution)/shard_map/gather_quarter/ppermute | solution.py:30
  11.7 1.0 dynamic_slice.25
  12.8 6.4 %collective-permute-done = bf16[64,1024]{1,0:T(8,128)(2,1)S(1)} collective-permute-done((bf16[64,1024]{1,0:T(8,128)(2,1)S(1)}, bf16[64,1024]{1,0:T(8,128)(2,1)S(1)}, u32[]{:S(2)}, u32[]{:S(2)}) %collective-permute-start) | collective-permute-done | bytes 131104 | tf_op jit(solution)/shard_map/gather_quarter/ppermute | solution.py:30
  19.3 0.1 copy.12
  19.7 22.4 %all_to_all.25 = bf16[4,80,1024]{2,1,0:T(8,128)(2,1)S(1)} all-to-all(bf16[4,80,1024]{2,1,0:T(8,128)(2,1)S(1)} %pad_maximum_fusion), channel_id=1, replica_groups=mesh['yh'=2,'yl'=2,'core'=2,'zh'=2,'x'=4,'th'=2,'tl'=4] {'tl'}, dimensions={0} | all-to-all | bytes 1310720 | tf_op jit(solution)/shard_map/gather_quarter/all_to_all | solution.py:39
  42.2 0.1 multiply_convert_fusion.2
  42.4 0.6 copy-done.4
  43.0 21.7 %all-gather.2 = f16[1024,1024]{1,0:T(8,128)(2,1)S(1)} all-gather(f16[256,1024]{1,0:T(8,128)(2,1)S(1)} %bitcast.35), channel_id=1, replica_groups=mesh['yh'=2,'yl'=2,'core'=2,'zh'=2,'x'=4,'th'=2,'tl'=4] {'x'}, dimensions={0}, use_global_device_ids=true | all-gather | bytes 2621440 | tf_op jit(solution)/shard_map/gather_tokens/all_gather | solution.py:60
  64.7 2.2 %convolution_convert_fusion.1 = f16[1024,512]{1,0:T(8,128)(2,1)} fusion(bf16[1024,512]{1,0:T(8,128)(2,1)S(1)} %copy-done.9, f16[1024,1024]{1,0:T(8,128)(2,1)S(1)} %all-gather.2), kind=kOutput, calls=%fused_computation.5 | convolution fusion | flops 1077411840 | bytes 4194304 | tf_op jit(solution)/shard_map/preact/dot_general | solution.py:135
  66.9 4.5 %all-to-all-start.1 = ((f16[8,128,512]{2,1,0:T(8,128)(2,1)}), f16[8,128,512]{2,1,0:T(8,128)(2,1)S(1)}, u32[]{:S(2)}, u32[]{:S(2)}) async-start(f16[8,128,512]{2,1,0:T(8,128)(2,1)} %bitcast.38), calls=%async_computation.1 | async-start | bytes 2097152 | tf_op jit(solution)/shard_map/preact/all_to_all | solution.py:39
  71.4 0.6 multiply_convert_fusion
  72.0 1.3 copy-done.3
  73.3 0.8 dynamic_slice.26
  74.2 2.4 %collective-permute-start.1 = (bf16[512,512]{1,0:T(8,128)(2,1)}, bf16[512,512]{1,0:T(8,128)(2,1)S(1)}, u32[]{:S(2)}, u32[]{:S(2)}) collective-permute-start(bf16[512,512]{1,0:T(8,128)(2,1)} %dynamic_slice.26), channel_id=1, source_target_pairs={{0,64},{64,0},{1,65},{65,1},{2,66},{66,2},{3,67},{67,3},{4,68},{68... | collective-permute-start | bytes 1572872 | tf_op jit(solution)/shard_map/act_columns/ppermute | solution.py:30
  76.7 0.9 slice_convert_fusion
  77.6 0.2 reshape.75
  77.9 0.4 collective-permute-done.1
  78.3 9.1 %all-to-all-done.1 = f16[8,128,512]{2,1,0:T(8,128)(2,1)S(1)} async-done(((f16[8,128,512]{2,1,0:T(8,128)(2,1)}), f16[8,128,512]{2,1,0:T(8,128)(2,1)S(1)}, u32[]{:S(2)}, u32[]{:S(2)}) %all-to-all-start.1) | async-done | bytes 1048608 | tf_op jit(solution)/shard_map/preact/all_to_all | solution.py:39
  87.4 0.1 convert_reduce_fusion
  87.5 0.2 multiply_convert_fusion.3
  87.7 13.9 %all-gather.3 = f16[1024,512]{1,0:T(8,128)(2,1)S(1)} all-gather(f16[128,512]{1,0:T(8,128)(2,1)S(1)} %multiply_convert_fusion.3), channel_id=1, replica_groups=mesh['yh'=2,'yl'=2,'core'=2,'zh'=2,'x'=4,'th'=2,'tl'=4] {'yh','yl','core'}, dimensions={0}, use_global_device_ids=true | all-gather | bytes 1179648 | tf_op jit(solution)/shard_map/gather_grad/all_gather | solution.py:60
  101.6 2.6 %convert_bitcast_fusion = bf16[4,1024,256]{2,1,0:T(8,128)(2,1)} fusion(bf16[4,256,512]{2,1,0:T(8,128)(2,1)S(1)} %bitcast.39, f16[1024,512]{1,0:T(8,128)(2,1)S(1)} %all-gather.3), kind=kOutput, calls=%fused_computation.1 | convolution fusion | flops 1076363264 | bytes 4194304 | tf_op jit(solution)/shard_map/grad_input/rc,kfc->krf/dot_general | solution.py:157
  104.2 3.6 %all-to-all-start.2 = ((bf16[4,1024,256]{2,1,0:T(8,128)(2,1)}), bf16[4,1024,256]{2,1,0:T(8,128)(2,1)S(1)}, u32[]{:S(2)}, u32[]{:S(2)}) async-start(bf16[4,1024,256]{2,1,0:T(8,128)(2,1)} %convert_bitcast_fusion), calls=%async_computation.2 | async-start | bytes 4194304 | tf_op jit(solution)/shard_map/grad_input/all_to_all | solution.py:39
  107.9 1.2 multiply_convert_fusion.1
  109.1 1.6 collective-permute-start.3
  110.7 1.2 dynamic-slice_select_fusion
  111.9 9.2 %collective-permute-start.2 = (bf16[512,512]{1,0:T(8,128)(2,1)S(1)}, bf16[512,512]{1,0:T(8,128)(2,1)}, u32[]{:S(2)}, u32[]{:S(2)}) collective-permute-start(bf16[512,512]{1,0:T(8,128)(2,1)S(1)} %dynamic-slice_select_fusion), channel_id=1, source_target_pairs={{0,128},{128,0},{1,129},{129,1},{2,130},{130,2},{3,131},{131,3},{4... | collective-permute-start | bytes 1572872 | tf_op jit(solution)/shard_map/act_columns/ppermute | solution.py:30
  121.1 7.2 %collective-permute-done.2 = bf16[512,512]{1,0:T(8,128)(2,1)} collective-permute-done((bf16[512,512]{1,0:T(8,128)(2,1)S(1)}, bf16[512,512]{1,0:T(8,128)(2,1)}, u32[]{:S(2)}, u32[]{:S(2)}) %collective-permute-start.2) | collective-permute-done | bytes 524320 | tf_op jit(solution)/shard_map/act_columns/ppermute | solution.py:30
  128.4 6.6 %all-to-all-done.2 = bf16[4,1024,256]{2,1,0:T(8,128)(2,1)S(1)} async-done(((bf16[4,1024,256]{2,1,0:T(8,128)(2,1)}), bf16[4,1024,256]{2,1,0:T(8,128)(2,1)S(1)}, u32[]{:S(2)}, u32[]{:S(2)}) %all-to-all-start.2) | async-done | bytes 2097184 | tf_op jit(solution)/shard_map/grad_input/all_to_all | solution.py:39
  134.9 1.7 grad_input.2
  136.6 6.3 %all-to-all-start.3 = ((bf16[4,16,16,256]{3,2,1,0:T(8,128)(2,1)}), bf16[4,16,16,256]{3,2,1,0:T(8,128)(2,1)S(1)}, u32[]{:S(2)}, u32[]{:S(2)}) async-start(bf16[4,16,16,256]{3,2,1,0:T(8,128)(2,1)} %grad_input.2), calls=%async_computation.3 | async-start | bytes 1048576 | tf_op jit(solution)/shard_map/grad_input/all_to_all | solution.py:39
  142.9 1.7 broadcast_select_fusion.1
  144.6 1.3 collective-permute-start.5
  146.0 1.9 collective-permute-start.4
  147.9 2.3 %convolution_convert_fusion = bf16[1024,512]{1,0:T(8,128)(2,1)} fusion(f16[1024,512]{1,0:T(8,128)(2,1)S(1)} %all-gather.3, f16[1024,1024]{1,0:T(8,128)(2,1)S(1)} %copy-done.2), kind=kOutput, calls=%fused_computation.4 | convolution fusion | flops 1078984704 | bytes 4194304 | tf_op jit(solution)/shard_map/grad_input/dot_general | solution.py:68
  150.2 14.7 %all-to-all-done.3 = bf16[4,16,16,256]{3,2,1,0:T(8,128)(2,1)S(1)} async-done(((bf16[4,16,16,256]{3,2,1,0:T(8,128)(2,1)}), bf16[4,16,16,256]{3,2,1,0:T(8,128)(2,1)S(1)}, u32[]{:S(2)}, u32[]{:S(2)}) %all-to-all-start.3) | async-done | bytes 524320 | tf_op jit(solution)/shard_map/grad_input/all_to_all | solution.py:39
  164.9 0.8 grad_input.3
  165.7 12.2 %all-to-all-start.4 = ((bf16[4,128,128]{2,1,0:T(8,128)(2,1)}), bf16[4,128,128]{2,1,0:T(8,128)(2,1)S(1)}, u32[]{:S(2)}, u32[]{:S(2)}) async-start(bf16[4,128,128]{2,1,0:T(8,128)(2,1)} %bitcast.17), calls=%async_computation.4 | async-start | bytes 262144 | tf_op jit(solution)/shard_map/grad_input/all_to_all | solution.py:39
  177.8 14.8 %all-to-all-done.4 = bf16[4,128,128]{2,1,0:T(8,128)(2,1)S(1)} async-done(((bf16[4,128,128]{2,1,0:T(8,128)(2,1)}), bf16[4,128,128]{2,1,0:T(8,128)(2,1)S(1)}, u32[]{:S(2)}, u32[]{:S(2)}) %all-to-all-start.4) | async-done | bytes 131104 | tf_op jit(solution)/shard_map/grad_input/all_to_all | solution.py:39
  192.6 2.3 %broadcast_select_fusion = bf16[1024,512]{1,0:T(8,128)(2,1)} fusion(bf16[1024,512]{1,0:T(8,128)(2,1)S(1)} %broadcast_select_fusion.1, bf16[1024,512]{1,0:T(8,128)(2,1)} %collective-permute-done.5, pred[]{:T(512)S(6)} %eq.26), kind=kLoop, calls=%fused_computation.12 | loop fusion | flops 524288 | bytes 3145729 | tf_op jit(solution)/shard_map/grad_factor/jit(_where)/select_n | solution.py:168
  195.0 5.1 %collective-permute-start.6 = (bf16[1024,512]{1,0:T(8,128)(2,1)}, bf16[1024,512]{1,0:T(8,128)(2,1)S(1)}, u32[]{:S(2)}, u32[]{:S(2)}) collective-permute-start(bf16[1024,512]{1,0:T(8,128)(2,1)} %broadcast_select_fusion), channel_id=1, source_target_pairs={{0,1},{2,3},{4,5},{6,7},{65,64},{67,66},{69,68},{71,70},{130,131},... | collective-permute-start | bytes 3145736 | tf_op jit(solution)/shard_map/grad_factor/ppermute | solution.py:35
  200.0 1.3 fusion.14
  201.4 2.0 fusion
  203.4 0.6 reduce_sum.22
  204.0 8.6 %collective-permute-done.6 = bf16[1024,512]{1,0:T(8,128)(2,1)S(1)} collective-permute-done((bf16[1024,512]{1,0:T(8,128)(2,1)}, bf16[1024,512]{1,0:T(8,128)(2,1)S(1)}, u32[]{:S(2)}, u32[]{:S(2)}) %collective-permute-start.6) | collective-permute-done | bytes 1048608 | tf_op jit(solution)/shard_map/grad_factor/ppermute | solution.py:35
  212.6 3.0 %convolution_multiply_fusion = f32[512,512]{1,0:T(8,128)} fusion(bf16[1024,512]{1,0:T(8,128)(2,1)} %broadcast_select_fusion, bf16[1024,512]{1,0:T(8,128)(2,1)S(1)} %collective-permute-done.6, pred[]{:T(512)S(6)} %eq.25, f16[1024,512]{1,0:T(8,128)(2,1)S(1)} %all-gather.3), kind=kOutput, calls=%fused_computation.6 | convolution fusion | flops 539230208 | bytes 4194305 | tf_op jit(solution)/shard_map/grad_factor/dot_general | solution.py:68
  (43 shorter events, 0.8 us)
Async XLA Ops:
  0.6 1.0 copy-start
  2.6 16.6 %collective-permute-start = (bf16[64,1024]{1,0:T(8,128)(2,1)S(1)}, bf16[64,1024]{1,0:T(8,128)(2,1)S(1)}, u32[]{:S(2)}, u32[]{:S(2)}) collective-permute-start(bf16[64,1024]{1,0:T(8,128)(2,1)S(1)} %pad_maximum_fusion.1), channel_id=1, source_target_pairs={{0,4},{4,0},{1,5},{5,1},{2,6},{6,2},{3,7},{7,3},{8,12},{12,8},{9,1... | collective-permute-start | bytes 393224 | tf_op jit(solution)/shard_map/gather_quarter/ppermute | solution.py:30
  42.1 0.8 copy-start.4
  42.3 22.4 %copy-start.9 = (bf16[1024,512]{1,0:T(8,128)(2,1)S(1)}, bf16[1024,512]{1,0:T(8,128)(2,1)}, u32[]{:S(2)}) copy-start(bf16[1024,512]{1,0:T(8,128)(2,1)} %param.4) | copy-start | bytes 3145732
  64.7 6.7 %copy-start.1 = (f16[1024,1024]{1,0:T(8,128)(2,1)}, f16[1024,1024]{1,0:T(8,128)(2,1)S(1)}, u32[]{:S(2)}) copy-start(f16[1024,1024]{1,0:T(8,128)(2,1)S(1)} %all-gather.2) | copy-start | bytes 6291460
  66.9 20.4 %all-to-all-start.1 = ((f16[8,128,512]{2,1,0:T(8,128)(2,1)}), f16[8,128,512]{2,1,0:T(8,128)(2,1)S(1)}, u32[]{:S(2)}, u32[]{:S(2)}) async-start(f16[8,128,512]{2,1,0:T(8,128)(2,1)} %bitcast.38), calls=%async_computation.1 | async-start | bytes 2097152 | tf_op jit(solution)/shard_map/preact/all_to_all | solution.py:39
  71.4 5.2 %copy-start.10 = (bf16[1024,512]{1,0:T(8,128)(2,1)S(1)}, bf16[1024,512]{1,0:T(8,128)(2,1)}, u32[]{:S(2)}) copy-start(bf16[1024,512]{1,0:T(8,128)(2,1)} %param.4) | copy-start | bytes 3145732
  72.0 1.3 copy-start.3
  74.2 4.1 %collective-permute-start.1 = (bf16[512,512]{1,0:T(8,128)(2,1)}, bf16[512,512]{1,0:T(8,128)(2,1)S(1)}, u32[]{:S(2)}, u32[]{:S(2)}) collective-permute-start(bf16[512,512]{1,0:T(8,128)(2,1)} %dynamic_slice.26), channel_id=1, source_target_pairs={{0,64},{64,0},{1,65},{65,1},{2,66},{66,2},{3,67},{67,3},{4,68},{68... | collective-permute-start | bytes 1572872 | tf_op jit(solution)/shard_map/act_columns/ppermute | solution.py:30
  78.3 26.0 %copy-start.11 = (bf16[512,512]{1,0:T(8,128)(2,1)}, bf16[512,512]{1,0:T(8,128)(2,1)S(1)}, u32[]{:S(2)}) copy-start(bf16[512,512]{1,0:T(8,128)(2,1)S(1)} %collective-permute-done.1) | copy-start | bytes 1572868
  104.2 30.7 %all-to-all-start.2 = ((bf16[4,1024,256]{2,1,0:T(8,128)(2,1)}), bf16[4,1024,256]{2,1,0:T(8,128)(2,1)S(1)}, u32[]{:S(2)}, u32[]{:S(2)}) async-start(bf16[4,1024,256]{2,1,0:T(8,128)(2,1)} %convert_bitcast_fusion), calls=%async_computation.2 | async-start | bytes 4194304 | tf_op jit(solution)/shard_map/grad_input/all_to_all | solution.py:39
  107.9 2.8 %copy-start.12 = (bf16[512,512]{1,0:T(8,128)(2,1)S(1)}, bf16[512,512]{1,0:T(8,128)(2,1)}, u32[]{:S(2)}) copy-start(bf16[512,512]{1,0:T(8,128)(2,1)} %copy-done.11) | copy-start | bytes 1572868
  109.1 33.8 %collective-permute-start.3 = (bf16[1024,512]{1,0:T(8,128)(2,1)}, bf16[1024,512]{1,0:T(8,128)(2,1)}, u32[]{:S(2)}, u32[]{:S(2)}) collective-permute-start(bf16[1024,512]{1,0:T(8,128)(2,1)} %multiply_convert_fusion.1), channel_id=1, source_target_pairs={{0,4},{65,69},{130,134},{195,199},{260,256},{325,321},{390,386},{4... | collective-permute-start | bytes 3145736 | tf_op jit(solution)/shard_map/factor_columns/ppermute | solution.py:35
  111.9 9.3 %copy-start.5 = (bf16[512,512]{1,0:T(8,128)(2,1)}, bf16[512,512]{1,0:T(8,128)(2,1)S(1)}, u32[]{:S(2)}) copy-start(bf16[512,512]{1,0:T(8,128)(2,1)S(1)} %dynamic-slice_select_fusion) | copy-start | bytes 1572868
  111.9 16.5 %collective-permute-start.2 = (bf16[512,512]{1,0:T(8,128)(2,1)S(1)}, bf16[512,512]{1,0:T(8,128)(2,1)}, u32[]{:S(2)}, u32[]{:S(2)}) collective-permute-start(bf16[512,512]{1,0:T(8,128)(2,1)S(1)} %dynamic-slice_select_fusion), channel_id=1, source_target_pairs={{0,128},{128,0},{1,129},{129,1},{2,130},{130,2},{3,131},{131,3},{4... | collective-permute-start | bytes 1572872 | tf_op jit(solution)/shard_map/act_columns/ppermute | solution.py:30
  136.6 9.3 %copy-start.6 = (bf16[512,512]{1,0:T(8,128)(2,1)S(1)}, bf16[512,512]{1,0:T(8,128)(2,1)}, u32[]{:S(2)}) copy-start(bf16[512,512]{1,0:T(8,128)(2,1)} %copy-done.5) | copy-start | bytes 1572868
  136.6 28.3 %all-to-all-start.3 = ((bf16[4,16,16,256]{3,2,1,0:T(8,128)(2,1)}), bf16[4,16,16,256]{3,2,1,0:T(8,128)(2,1)S(1)}, u32[]{:S(2)}, u32[]{:S(2)}) async-start(bf16[4,16,16,256]{3,2,1,0:T(8,128)(2,1)} %grad_input.2), calls=%async_computation.3 | async-start | bytes 1048576 | tf_op jit(solution)/shard_map/grad_input/all_to_all | solution.py:39
  142.9 5.0 %copy-start.2 = (f16[1024,1024]{1,0:T(8,128)(2,1)S(1)}, f16[1024,1024]{1,0:T(8,128)(2,1)}, u32[]{:S(2)}) copy-start(f16[1024,1024]{1,0:T(8,128)(2,1)} %copy-done.1) | copy-start | bytes 6291460
  144.6 33.2 %collective-permute-start.5 = (bf16[1024,512]{1,0:T(8,128)(2,1)S(1)}, bf16[1024,512]{1,0:T(8,128)(2,1)}, u32[]{:S(2)}, u32[]{:S(2)}) collective-permute-start(bf16[1024,512]{1,0:T(8,128)(2,1)S(1)} %broadcast_select_fusion.1), channel_id=1, source_target_pairs={{0,2},{4,6},{65,67},{69,71},{130,128},{134,132},{195,193},{199,197... | collective-permute-start | bytes 3145736 | tf_op jit(solution)/shard_map/factor_columns/ppermute | solution.py:35
  145.9 4.2 %copy-start.7 = (bf16[512,512]{1,0:T(8,128)(2,1)}, bf16[512,512]{1,0:T(8,128)(2,1)S(1)}, u32[]{:S(2)}) copy-start(bf16[512,512]{1,0:T(8,128)(2,1)S(1)} %broadcast_select_fusion.2) | copy-start | bytes 1572868
  146.0 4.2 %collective-permute-start.4 = (bf16[512,512]{1,0:T(8,128)(2,1)S(1)}, bf16[512,512]{1,0:T(8,128)(2,1)S(1)}, u32[]{:S(2)}, u32[]{:S(2)}) collective-permute-start(bf16[512,512]{1,0:T(8,128)(2,1)S(1)} %broadcast_select_fusion.2), channel_id=1, source_target_pairs={{0,64},{64,0},{1,65},{65,1},{2,66},{66,2},{3,67},{67,3},{4,68},{68... | collective-permute-start | bytes 1572872 | tf_op jit(solution)/shard_map/grad_input/ppermute | solution.py:30
  165.7 27.0 %all-to-all-start.4 = ((bf16[4,128,128]{2,1,0:T(8,128)(2,1)}), bf16[4,128,128]{2,1,0:T(8,128)(2,1)S(1)}, u32[]{:S(2)}, u32[]{:S(2)}) async-start(bf16[4,128,128]{2,1,0:T(8,128)(2,1)} %bitcast.17), calls=%async_computation.4 | async-start | bytes 262144 | tf_op jit(solution)/shard_map/grad_input/all_to_all | solution.py:39
  177.8 23.5 %copy-start.8 = (bf16[512,512]{1,0:T(8,128)(2,1)S(1)}, bf16[512,512]{1,0:T(8,128)(2,1)}, u32[]{:S(2)}) copy-start(bf16[512,512]{1,0:T(8,128)(2,1)} %copy-done.7) | copy-start | bytes 1572868
  195.0 17.6 %collective-permute-start.6 = (bf16[1024,512]{1,0:T(8,128)(2,1)}, bf16[1024,512]{1,0:T(8,128)(2,1)S(1)}, u32[]{:S(2)}, u32[]{:S(2)}) collective-permute-start(bf16[1024,512]{1,0:T(8,128)(2,1)} %broadcast_select_fusion), channel_id=1, source_target_pairs={{0,1},{2,3},{4,5},{6,7},{65,64},{67,66},{69,68},{71,70},{130,131},... | collective-permute-start | bytes 3145736 | tf_op jit(solution)/shard_map/grad_factor/ppermute | solution.py:35
